TPU v7x, 128 devices: a whole 4x4x4 slice. The times are simulated.
128 devices in a mesh: dp: 32 (over x, y, core), cent: 4 (over z).
Axes of the slice: x: 4, y: 4, z: 4, core: 2. Of those that a mesh axis runs over, the one named last changes fastest.
Arguments:
- embeddings: bfloat16 [131072, 768], P(('dp', 'cent')), may hold values from -40 to 40
- init_centroids: bfloat16 [2048, 768], P('cent'), may hold values from -40 to 40
- assign: int32 [131072], P(('dp', 'cent')), may hold values from 0 to 2047, as said below
- owner_map: int32 [2048], replicated, may hold values from 0 to 127, as said below
Outputs:
- centroids: float32 [2048, 768], P('cent')
- similarity: bfloat16 [128, 2048, 2048], P(('dp', 'cent'))
Inputs may be any that keep to these rules, and one draw needn't show every extreme that they name: `assign`: the rows of one device send at most 16 rows to one owner (owner_map of the row's cluster); in every draw some owner receives exactly 16 rows from every device. `owner_map`: every owner owns the same number of clusters.
All inputs are finite; a program needn't handle non-finite values.
Results may differ from a plain program's by a relative error of at most 0.018.
Values may be sent and summed in bfloat16 or wider, within the bound.
No kernel may reach another device: no remote copies, remote signals or barrier semaphores. Data moves between devices by JAX's collectives and lax.ppermute only.
A program may use at most 64 MiB of HBM per device.

v0:
```python
import math

import jax
import jax.numpy as jnp
from jax import lax
from jax.sharding import PartitionSpec as P

ROUNDS = 2


epsilon = 1e-06
logit_divisor = 0.02


def normalize_rows(matrix):
    wide = matrix.astype(jnp.float32)
    return (wide / jnp.sqrt(jnp.sum(wide * wide, axis=-1, keepdims=True) + epsilon)).astype(
        jnp.bfloat16
    )


def contract_final_axis(left, right):
    return lax.dot_general(
        left, right, (((1,), (1,)), ((), ())), preferred_element_type=jnp.float32
    )


def contract_first(left, right):
    return lax.dot_general(
        left, right, (((0,), (0,)), ((), ())), preferred_element_type=jnp.float32
    )


def shards(embeddings, init_centroids, assign, owner_map):
    devices = lax.axis_size(("dp", "cent"))
    cent_count = lax.axis_size("cent")
    dp_count = lax.axis_size("dp")
    unit_rows = normalize_rows(embeddings)
    centroid_block = normalize_rows(init_centroids)
    local_rows = unit_rows.shape[0]
    feature_width = unit_rows.shape[1]
    block_size = centroid_block.shape[0]
    share_rows = block_size // dp_count
    for round_index in range(ROUNDS):
        gathered = lax.all_gather(centroid_block, "cent", axis=0, tiled=True)
        reordered = gathered.reshape(cent_count, dp_count, share_rows, feature_width)
        reordered = reordered.transpose(1, 0, 2, 3).reshape(-1, feature_width)
        cosine_tile = contract_final_axis(unit_rows, reordered)
        softmax_membership = jnp.exp(cosine_tile / logit_divisor)
        weights = (softmax_membership / jnp.sum(softmax_membership, axis=1, keepdims=True)).astype(
            jnp.bfloat16
        )
        own_share = lax.psum_scatter(
            contract_first(weights, unit_rows), ("dp", "cent"), scatter_dimension=0, tiled=True
        )
        unit_share = normalize_rows(own_share)
        centroid_block = lax.all_gather(unit_share, "dp", axis=0, tiled=True)
    centroids = centroid_block.astype(jnp.float32) * math.sqrt(feature_width)
    cluster_count = owner_map.shape[0]
    capacity = 2 * local_rows // devices
    matches = assign[:, None] == jnp.arange(cluster_count, dtype=jnp.int32)[None, :]
    owner_of = jnp.sum(jnp.where(matches, owner_map[None, :], 0), axis=1)
    owner_hits = (owner_of[:, None] == jnp.arange(devices, dtype=jnp.int32)[None, :]).astype(
        jnp.int32
    )
    slot_index = jnp.sum(jnp.cumsum(owner_hits, axis=0) * owner_hits, axis=1) - 1
    position = owner_of * capacity + slot_index
    send_rows = (
        jnp.zeros((devices * capacity, feature_width), jnp.bfloat16).at[position].set(unit_rows)
    )
    send_labels = jnp.full((devices * capacity,), -1, jnp.int32).at[position].set(assign)
    arrived_vectors, got_labels = (
        lax.all_to_all(
            send_rows.reshape(devices, capacity, feature_width),
            ("dp", "cent"),
            split_axis=0,
            concat_axis=0,
            tiled=True,
        ),
        lax.all_to_all(
            send_labels.reshape(devices, capacity),
            ("dp", "cent"),
            split_axis=0,
            concat_axis=0,
            tiled=True,
        ),
    )
    received = arrived_vectors.reshape(-1, feature_width)
    labels_of = got_labels.reshape(-1)
    inner = contract_final_axis(received, received) * math.sqrt(feature_width)
    main_diagonal = jnp.eye(received.shape[0], dtype=bool)
    same_cluster = (
        (labels_of[:, None] == labels_of[None, :])
        & (labels_of[:, None] >= 0)
        & jnp.logical_not(main_diagonal)
    )
    similarity = jnp.where(same_cluster, inner, 0.0).astype(jnp.bfloat16)[None]
    return (centroids, similarity)


def solution(mesh):
    return jax.shard_map(
        shards,
        mesh=mesh,
        in_specs=(P(("dp", "cent"), None), P("cent", None), P(("dp", "cent")), P()),
        out_specs=(P("cent", None), P(("dp", "cent"), None, None)),
        check_vma=False,
    )
```

profile of v0, /device:TPU:1, one launch (start us, length us, event | category | flops | bytes accessed | tf_op | source)
XLA Modules:
  0.0 603.4 jit_solution(10950013787704615307)
XLA Ops:
  7.2 1.5 fusion.9
  8.7 2.2 fusion.10
  11.4 42.7 %all-gather.3.cloned.1.call-done = bf16[2048,768]{1,0:T(8,128)(2,1)} async-done(((bf16[512,768]{1,0:T(8,128)(2,1)}), bf16[2048,768]{1,0:T(8,128)(2,1)}) %all-gather.3.cloned.1.call-update) | async-done | bytes 3145744 | tf_op jit(solution)/shard_map/all_gather | solution.py:45
  54.1 2.2 copy.18
  56.4 3.7 fusion.3
  60.0 7.0 %fusion.5 = f32[2048,768]{1,0:T(8,128)} fusion(f32[1024,2048]{1,0:T(8,128)S(1)} %get-tuple-element.3, f32[1024]{0:T(1024)S(1)} %get-tuple-element.2, bf16[1024,768]{1,0:T(8,128)(2,1)S(1)} %copy-done, f32[1024]{0:T(1024)S(1)} %add_sqrt_fusion), kind=kOutput, calls=%fused_computation.15 | convolution fusion | flops 3229876224 | bytes 16261120 | tf_op jit(solution)/shard_map/dot_general | solution.py:29
  67.1 211.0 %reduce-scatter.3.cloned.1.call-done = f32[16,768]{1,0:T(8,128)} async-done(((f32[2048,768]{1,0:T(8,128)}), f32[16,768]{1,0:T(8,128)}) %reduce-scatter.3.cloned.1.call-update) | async-done | bytes 49168 | tf_op jit(solution)/shard_map/reduce_scatter | solution.py:53
  278.1 0.9 multiply_reduce_fusion.1
  279.9 27.3 %all_gather.13 = bf16[512,768]{1,0:T(8,128)(2,1)} all-gather(bf16[16,768]{1,0:T(8,128)(2,1)S(1)} %divide_convert_fusion.5), channel_id=1, replica_groups=mesh['dp'=32,'cent'=4] {'dp'}, dimensions={0}, use_global_device_ids=true | all-gather | bytes 811008 | tf_op jit(solution)/shard_map/all_gather | solution.py:57
  307.5 37.4 %all-gather.5.cloned.1.call-done = bf16[2048,768]{1,0:T(8,128)(2,1)} async-done(((bf16[512,768]{1,0:T(8,128)(2,1)}), bf16[2048,768]{1,0:T(8,128)(2,1)}) %all-gather.5.cloned.1.call-update) | async-done | bytes 3145744 | tf_op jit(solution)/shard_map/all_gather | solution.py:45
  344.9 2.2 copy.19
  347.1 3.7 fusion.4
  350.8 6.9 %fusion.6 = f32[2048,768]{1,0:T(8,128)} fusion(f32[1024,2048]{1,0:T(8,128)S(1)} %get-tuple-element.5, f32[1024]{0:T(1024)S(1)} %get-tuple-element.4, bf16[1024,768]{1,0:T(8,128)(2,1)S(1)} %copy-done, f32[1024]{0:T(1024)S(1)} %add_sqrt_fusion), kind=kOutput, calls=%fused_computation.16 | convolution fusion | flops 3229876224 | bytes 16261120 | tf_op jit(solution)/shard_map/dot_general | solution.py:29
  358.4 1.3 select_reduce_fusion
  360.6 4.3 scatter_custom_fusion
  365.6 8.3 %all-to-all-start = ((s32[128,1,16]{2,1,0:T(1,128)}), s32[128,1,16]{2,1,0:T(1,128)S(1)}, u32[]{:S(2)}, u32[]{:S(2)}) async-start(s32[128,1,16]{2,1,0:T(1,128)} %bitcast.12), calls=%async_computation.2 | async-start | bytes 131072 | tf_op jit(solution)/shard_map/all_to_all | solution.py:80
  374.0 7.7 %scatter_custom_fusion.1 = bf16[2048,768]{1,0:T(8,128)(2,1)} fusion(s32[1024]{0:T(1024)S(1)} %bitcast.36, bf16[]{:T(256)} %constant.7.clone.1, bf16[1024,768]{1,0:T(8,128)(2,1)S(1)} %copy-done, f32[1024]{0:T(1024)S(1)} %add_sqrt_fusion), kind=kCustom, calls=%fused_computation.25 | custom fusion | flops 2359296 | bytes 4722690 | tf_op jit(solution)/shard_map/scatter | solution.py:69
  381.7 1.9 all-to-all-done
  383.6 7.9 %all-to-all-start.1 = ((bf16[128,16,768]{2,1,0:T(8,128)(2,1)}), bf16[128,16,768]{2,1,0:T(8,128)(2,1)S(1)}, u32[]{:S(2)}, u32[]{:S(2)}) async-start(bf16[128,16,768]{2,1,0:T(8,128)(2,1)} %bitcast.13), calls=%async_computation.3 | async-start | bytes 6291456 | tf_op jit(solution)/shard_map/all_to_all | solution.py:73
  392.9 40.6 %all-to-all-done.1 = bf16[128,16,768]{2,1,0:T(8,128)(2,1)S(1)} async-done(((bf16[128,16,768]{2,1,0:T(8,128)(2,1)}), bf16[128,16,768]{2,1,0:T(8,128)(2,1)S(1)}, u32[]{:S(2)}, u32[]{:S(2)}) %all-to-all-start.1) | async-done | bytes 3145760 | tf_op jit(solution)/shard_map/all_to_all | solution.py:73
  433.5 12.2 %fusion.2 = bf16[1,2048,2048]{2,1,0:T(8,128)(2,1)} fusion(s32[2048]{0:T(1024)S(1)} %eq.64, pred[2048]{0:T(1024)(128)(4,1)S(1)} %broadcast_compare_fusion, bf16[2048,768]{1,0:T(8,128)(2,1)S(1)} %bitcast.28), kind=kOutput, calls=%fused_computation.6 | convolution fusion | flops 6476005376 | bytes 11544576 | tf_op jit(solution)/shard_map/dot_general | solution.py:23
  445.7 122.9 %reduce-scatter.5.cloned.1.call-done = f32[16,768]{1,0:T(8,128)} async-done(((f32[2048,768]{1,0:T(8,128)}), f32[16,768]{1,0:T(8,128)}) %reduce-scatter.5.cloned.1.call-update) | async-done | bytes 49168 | tf_op jit(solution)/shard_map/reduce_scatter | solution.py:53
  570.5 25.1 %all_gather.15 = bf16[512,768]{1,0:T(8,128)(2,1)S(1)} all-gather(bf16[16,768]{1,0:T(8,128)(2,1)S(1)} %divide_convert_fusion.4), channel_id=1, replica_groups=mesh['dp'=32,'cent'=4] {'dp'}, dimensions={0}, use_global_device_ids=true | all-gather | bytes 811008 | tf_op jit(solution)/shard_map/all_gather | solution.py:57
  595.6 1.3 convert_multiply_fusion.2
  (37 shorter events, 7.2 us)
Async XLA Ops:
  7.2 3.9 copy-start
  7.2 46.9 %all-gather.3.cloned.1.call-start = ((), (), s32[]{:S(2)}) async-start(), calls=%async_computation.4 | async-start | bytes 3932160 | tf_op jit(solution)/shard_map/all_gather | solution.py:45
  11.0 267.1 %reduce-scatter.3.cloned.1.call-start = ((), (), s32[]{:S(2)}) async-start(), calls=%async_computation.5 | async-start | bytes 6340608 | tf_op jit(solution)/shard_map/reduce_scatter | solution.py:53
  67.0 277.8 %all-gather.5.cloned.1.call-start = ((), (), s32[]{:S(2)}) async-start(), calls=%async_computation.6 | async-start | bytes 3932160 | tf_op jit(solution)/shard_map/all_gather | solution.py:45
  307.2 261.4 %reduce-scatter.5.cloned.1.call-start = ((), (), s32[]{:S(2)}) async-start(), calls=%async_computation.7 | async-start | bytes 6340608 | tf_op jit(solution)/shard_map/reduce_scatter | solution.py:53
  357.7 0.7 copy-start.1
  357.7 0.7 copy-start.2
  365.6 17.9 %all-to-all-start = ((s32[128,1,16]{2,1,0:T(1,128)}), s32[128,1,16]{2,1,0:T(1,128)S(1)}, u32[]{:S(2)}, u32[]{:S(2)}) async-start(s32[128,1,16]{2,1,0:T(1,128)} %bitcast.12), calls=%async_computation.2 | async-start | bytes 131072 | tf_op jit(solution)/shard_map/all_to_all | solution.py:80
  383.6 50.0 %all-to-all-start.1 = ((bf16[128,16,768]{2,1,0:T(8,128)(2,1)}), bf16[128,16,768]{2,1,0:T(8,128)(2,1)S(1)}, u32[]{:S(2)}, u32[]{:S(2)}) async-start(bf16[128,16,768]{2,1,0:T(8,128)(2,1)} %bitcast.13), calls=%async_computation.3 | async-start | bytes 6291456 | tf_op jit(solution)/shard_map/all_to_all | solution.py:73
Sparse Core Ops, SparseCore 0:
  11.1 42.9 all-gather.2
  67.1 210.9 reduce-scatter.2
  307.4 37.4 all-gather.4
  357.9 210.7 reduce-scatter.4
where the time goes:
time: 604 us; the launch traced here: 603 us
  waiting for transfers between devices  457 us (76%)
  blocking collectives  52.4 us (9%)
  matrix products  33.5 us (6%)
  other arithmetic  19.5 us (3%)
  starting transfers between devices  16.5 us (3%)
  between operations  13.9 us (2%)
  local copies, waits for them, and re-layouts  11 us (2%)
    reduce_scatter x2, waiting for transfers between devices, shards(): lax.psum_scatter(contract_first(weights, unit_rows), ('dp', 'cent'), scat...  334 us
    all_gather x2, waiting for transfers between devices, shards(): gathered = lax.all_gather(centroid_block, 'cent', axis=0, tiled=True)  80.1 us
    all_gather x2, blocking collectives, shards(): centroid_block = lax.all_gather(unit_share, 'dp', axis=0, tiled=True)  52.4 us
    all_to_all x1, waiting for transfers between devices, shards(): lax.all_to_all(send_rows.reshape(devices, capacity, feature_width), ('dp'...  40.6 us
    dot_general x3, matrix products, contract_final_axis(): lax.dot_general(left, right, (((1,), (1,)), ((), ())), preferred_element_...  19.6 us
    dot_general x2, matrix products, contract_first(): lax.dot_general(left, right, (((0,), (0,)), ((), ())), preferred_element_...  13.9 us
  transfers between devices with their start and end apart: 6, of which 6 were waited for; matrix products, arithmetic and copies ran while one was open for 5% of the time, Pallas kernels for 0%

commit v1 on v0

v1 whole, which is shorter than its diff:
```python
import math

import jax
import jax.numpy as jnp
from jax import lax
from jax.sharding import PartitionSpec as P

ROUNDS = 2
AXES = ("dp", "cent")

epsilon = 1e-06
logit_divisor = 0.02


def normalize_rows(matrix):
    wide = matrix.astype(jnp.float32)
    return (wide / jnp.sqrt(jnp.sum(wide * wide, axis=-1, keepdims=True) + epsilon)).astype(
        jnp.bfloat16
    )


def contract_final_axis(left, right):
    return lax.dot_general(
        left, right, (((1,), (1,)), ((), ())), preferred_element_type=jnp.float32
    )


def device_number(plane, core, depth, cent_count):
    return (plane * 2 + core) * cent_count + depth


def plan(dp_count, cent_count):
    planes = dp_count // 2
    spots = [
        (p, c, z) for p in range(planes) for c in range(2) for z in range(cent_count)
    ]

    def moved(core_step, depth_step):
        return [
            (
                device_number(p, c, z, cent_count),
                device_number(p, (c + core_step) % 2, (z + depth_step) % cent_count, cent_count),
            )
            for p, c, z in spots
        ]

    plane_groups = [
        [device_number(p, c, z, cent_count) for p in range(planes)]
        for c in range(2)
        for z in range(cent_count)
    ]
    return moved, plane_groups


def shards(embeddings, init_centroids, assign, owner_map):
    devices = lax.axis_size(AXES)
    cent_count = lax.axis_size("cent")
    dp_count = lax.axis_size("dp")
    planes = dp_count // 2
    moved, plane_groups = plan(dp_count, cent_count)
    core = lax.axis_index("dp") % 2

    def send(value, core_step, depth_step):
        return lax.ppermute(value, AXES, moved(core_step, depth_step))

    unit_rows = normalize_rows(embeddings)
    local_rows, feature_width = unit_rows.shape
    block_size = init_centroids.shape[0]
    half = block_size // 2
    share = half // planes
    centroid_half = normalize_rows(lax.dynamic_slice_in_dim(init_centroids, core * half, half, 0))

    cut = local_rows // 2
    first, second = unit_rows[:cut], unit_rows[cut:]
    below_first, above_second = send(first, 0, 1), send(second, 0, -1)
    below_second, above_first = send(second, 0, 1), send(first, 0, -1)
    far_first, far_second = send(below_first, 0, 1), send(above_second, 0, -1)
    pieces = [first, second, above_first, above_second, far_first, far_second, below_first, below_second]
    own = jnp.concatenate(pieces)
    other = jnp.concatenate([send(piece, 1, 0) for piece in pieces])
    rows = jnp.concatenate([own, other])
    group_rows = own.shape[0]

    def total_over_group(partial):
        mine, theirs = partial[:group_rows], partial[group_rows:]
        swapped = send(partial, 1, 0)
        chip = jnp.stack([mine + swapped[group_rows:], theirs + swapped[:group_rows]])
        result = chip
        for step in range(1, cent_count):
            result = result + jnp.roll(send(chip, 0, -step), step * local_rows, axis=1)
        return result.reshape(-1)

    for round_index in range(ROUNDS):
        scores = contract_final_axis(centroid_half, rows)
        membership = jnp.exp(scores / logit_divisor)
        total = total_over_group(jnp.sum(membership, axis=0))
        weights = (membership / total[None, :]).astype(jnp.bfloat16)
        partial = jnp.dot(weights, rows, preferred_element_type=jnp.float32).astype(jnp.bfloat16)
        arrived = lax.all_to_all(
            partial.reshape(planes, share, feature_width),
            AXES,
            0,
            0,
            axis_index_groups=plane_groups,
            tiled=True,
        )
        unit_share = normalize_rows(jnp.sum(arrived.astype(jnp.float32), axis=0))
        spread = lax.optimization_barrier(
            jnp.broadcast_to(unit_share[None], (planes, share, feature_width))
        )
        centroid_half = lax.all_to_all(
            spread, AXES, 0, 0, axis_index_groups=plane_groups, tiled=True
        ).reshape(half, feature_width)
    sibling_half = send(centroid_half, 1, 0)
    centroids = jnp.where(
        core == 0,
        jnp.concatenate([centroid_half, sibling_half]),
        jnp.concatenate([sibling_half, centroid_half]),
    ).astype(jnp.float32) * math.sqrt(feature_width)

    cluster_count = owner_map.shape[0]
    capacity = 2 * local_rows // devices
    matches = assign[:, None] == jnp.arange(cluster_count, dtype=jnp.int32)[None, :]
    owner_of = jnp.sum(jnp.where(matches, owner_map[None, :], 0), axis=1)
    owner_hits = owner_of[:, None] == jnp.arange(devices, dtype=jnp.int32)[None, :]
    earlier = (
        jnp.arange(local_rows)[:, None] > jnp.arange(local_rows)[None, :]
    ).astype(jnp.bfloat16)
    counts = jnp.dot(
        earlier, owner_hits.astype(jnp.bfloat16), preferred_element_type=jnp.float32
    )
    slot_index = jnp.sum(jnp.where(owner_hits, counts, 0.0), axis=1).astype(jnp.int32)
    position = owner_of * capacity + slot_index
    taken = position[None, :] == jnp.arange(devices * capacity, dtype=jnp.int32)[:, None]
    send_rows = jnp.dot(
        taken.astype(jnp.bfloat16), unit_rows, preferred_element_type=jnp.float32
    ).astype(jnp.bfloat16)
    send_labels = jnp.sum(jnp.where(taken, assign[None, :] + 1, 0), axis=1) - 1
    received = lax.all_to_all(
        send_rows.reshape(devices, capacity, feature_width), AXES, 0, 0, tiled=True
    ).reshape(-1, feature_width)
    labels_of = lax.all_to_all(
        send_labels.reshape(devices, capacity), AXES, 0, 0, tiled=True
    ).reshape(-1)
    inner = contract_final_axis(received, received) * math.sqrt(feature_width)
    main_diagonal = jnp.eye(received.shape[0], dtype=bool)
    same_cluster = (
        (labels_of[:, None] == labels_of[None, :])
        & (labels_of[:, None] >= 0)
        & jnp.logical_not(main_diagonal)
    )
    similarity = jnp.where(same_cluster, inner, 0.0).astype(jnp.bfloat16)[None]
    return (centroids, similarity)


def solution(mesh):
    return jax.shard_map(
        shards,
        mesh=mesh,
        in_specs=(P(AXES, None), P("cent", None), P(AXES), P()),
        out_specs=(P("cent", None), P(AXES, None, None)),
        check_vma=False,
    )
```

time: 604 us -> 284 us (0.47)
  waiting for transfers between devices: 457 us -> 104 us
  starting transfers between devices: 16.5 us -> 57.9 us
  matrix products: 33.5 us -> 72 us
  blocking collectives: 52.4 us -> 14.5 us
  between operations: 13.9 us -> 0.84 us
  local copies, waits for them, and re-layouts: 11 us -> 23.2 us
  other arithmetic: 19.5 us -> 11 us
    reduce_scatter x2 -> x0, waiting for transfers between devices: 334 us -> none  [shards(): lax.psum_scatter(contract_first(weights, unit_rows), ('dp', 'cent'), scat...]
    all_gather x2 -> x0, waiting for transfers between devices: 80.1 us -> none  [shards(): gathered = lax.all_gather(centroid_block, 'cent', axis=0, tiled=True)]
    all_gather x2 -> x0, blocking collectives: 52.4 us -> none  [shards(): centroid_block = lax.all_gather(unit_share, 'dp', axis=0, tiled=True)]
    ppermute x0 -> x23, waiting for transfers between devices: none -> 38.8 us  [send(): return lax.ppermute(value, AXES, moved(core_step, depth_step))]
    ppermute x0 -> x23, starting transfers between devices: none -> 33.2 us  [send(): return lax.ppermute(value, AXES, moved(core_step, depth_step))]
    dot_general x3, matrix products: 19.6 us -> 44.8 us  [contract_final_axis(): lax.dot_general(left, right, (((1,), (1,)), ((), ())), preferred_element_...]
    all_to_all x2 -> x5, waiting for transfers between devices: 42.5 us -> 64.9 us  [the longest x1 39.1 us: shards(): lax.all_to_all(send_rows.reshape(devices, capacity, feature_width), AXES,...]
    unnamed x6 -> x21, local copies, waits for them, and re-layouts: 0.68 us -> 18.1 us
  transfers between devices with their start and end apart: 6 -> 28, of which waited for: 6 -> 15; matrix products, arithmetic and copies ran while one was open for 5% -> 16% of each run, Pallas kernels for 0% -> 0%
where the time goes in v1:
time: 284 us; the launch traced here: 283 us
  waiting for transfers between devices  104 us (37%)
  matrix products  72 us (25%)
  starting transfers between devices  57.9 us (20%)
  local copies, waits for them, and re-layouts  23.2 us (8%)
  blocking collectives  14.5 us (5%)
  other arithmetic  11 us (4%)
    dot_general x3, matrix products, contract_final_axis(): lax.dot_general(left, right, (((1,), (1,)), ((), ())), preferred_element_...  44.8 us
    all_to_all x1, waiting for transfers between devices, shards(): lax.all_to_all(send_rows.reshape(devices, capacity, feature_width), AXES,...  39.1 us
    ppermute x23, waiting for transfers between devices, send(): return lax.ppermute(value, AXES, moved(core_step, depth_step))  38.8 us
    ppermute x23, starting transfers between devices, send(): return lax.ppermute(value, AXES, moved(core_step, depth_step))  33.2 us
    dot_general x2, matrix products, shards(): jnp.dot(weights, rows, preferred_element_type=jnp.float32)  21.5 us
    unnamed x21, local copies, waits for them, and re-layouts  18.1 us
    all_to_all x1, blocking collectives, shards(): lax.all_to_all(partial.reshape(planes, share, feature_width), AXES, 0, 0,...  14.5 us
    all_to_all x2, waiting for transfers between devices, shards(): lax.all_to_all(spread, AXES, 0, 0, axis_index_groups=plane_groups, tiled=...  11 us
  transfers between devices with their start and end apart: 28, of which 15 were waited for; matrix products, arithmetic and copies ran while one was open for 16% of the time, Pallas kernels for 0%

profile of v1, /device:TPU:1, one launch (start us, length us, event | category | flops | bytes accessed | tf_op | source)
XLA Modules:
  0.0 283.2 jit_solution(6858628927209085047)
XLA Ops:
  12.6 16.0 %collective-permute-done.2 = bf16[512,768]{1,0:T(8,128)(2,1)S(1)} collective-permute-done((bf16[512,768]{1,0:T(8,128)(2,1)}, bf16[512,768]{1,0:T(8,128)(2,1)S(1)}, u32[]{:S(2)}, u32[]{:S(2)}) %collective-permute-start.2) | collective-permute-done | bytes 786464 | tf_op jit(solution)/shard_map/ppermute | solution.py:64
  35.2 9.4 %collective-permute-done = bf16[512,768]{1,0:T(8,128)(2,1)} collective-permute-done((bf16[512,768]{1,0:T(8,128)(2,1)}, bf16[512,768]{1,0:T(8,128)(2,1)}, u32[]{:S(2)}, u32[]{:S(2)}) %collective-permute-start) | collective-permute-done | bytes 786464 | tf_op jit(solution)/shard_map/ppermute | solution.py:64
  44.7 2.9 %collective-permute-start.7 = (bf16[512,768]{1,0:T(8,128)(2,1)}, bf16[512,768]{1,0:T(8,128)(2,1)S(1)}, u32[]{:S(2)}, u32[]{:S(2)}) collective-permute-start(bf16[512,768]{1,0:T(8,128)(2,1)} %get-tuple-element.4), channel_id=1, source_target_pairs={{0,4},{1,5},{2,6},{3,7},{4,0},{5,1},{6,2},{7,3},{8,12},{9,13},{10,... | collective-permute-start | bytes 2359304 | tf_op jit(solution)/shard_map/ppermute | solution.py:64
  55.8 5.7 %collective-permute-done.4 = bf16[512,768]{1,0:T(8,128)(2,1)} collective-permute-done((bf16[512,768]{1,0:T(8,128)(2,1)}, bf16[512,768]{1,0:T(8,128)(2,1)}, u32[]{:S(2)}, u32[]{:S(2)}) %collective-permute-start.4) | collective-permute-done | bytes 786464 | tf_op jit(solution)/shard_map/ppermute | solution.py:64
  78.0 15.0 %fusion.34 = (f32[8192]{0:T(1024)S(1)}, f32[256,8192]{1,0:T(8,128)}) fusion(bf16[8192,768]{1,0:T(8,128)(2,1)} %constant_dynamic-update-slice_fusion, f32[256]{0:T(256)S(1)} %add_sqrt_fusion.1, bf16[512,768]{1,0:T(8,128)(2,1)S(1)} %copy-done, s32[]{:T(128)S(6)} %select_n.36), kind=kOutput, calls=%fused_computation.87 | convolution fusion | flops 3226001408 | bytes 21398532 | tf_op jit(solution)/shard_map/dot_general | solution.py:23
  101.0 10.4 %fusion.15 = bf16[256,768]{1,0:T(8,128)(2,1)S(1)} fusion(bf16[8192,768]{1,0:T(8,128)(2,1)} %constant_dynamic-update-slice_fusion, f32[256,8192]{1,0:T(8,128)} %get-tuple-element.15, f32[8192]{0:T(1024)S(1)} %bitcast.41), kind=kOutput, calls=%fused_computation.29 | convolution fusion | flops 3225616384 | bytes 21397504 | tf_op jit(solution)/shard_map/dot_general | solution.py:98
  111.4 14.5 %all_to_all.31 = bf16[16,16,768]{2,1,0:T(8,128)(2,1)S(1)} all-to-all(bf16[16,16,768]{2,1,0:T(8,128)(2,1)S(1)} %bitcast.31), channel_id=1, replica_groups={{0,8,16,24,32,40,48,56,64,72,80,88,96,104,112,120},{1,9,17,25,33,41,49,..., dimensions={0} | all-to-all | bytes 786432 | tf_op jit(solution)/shard_map/all_to_all | solution.py:99
  127.0 3.7 %all-to-all-start.1 = ((bf16[16,16,768]{2,1,0:T(8,128)(2,1)}), bf16[16,16,768]{2,1,0:T(8,128)(2,1)S(1)}, u32[]{:S(2)}, u32[]{:S(2)}) async-start(bf16[16,16,768]{2,1,0:T(8,128)(2,1)} %broadcast_in_dim.33), calls=%async_computation.1 | async-start | bytes 786432 | tf_op jit(solution)/shard_map/all_to_all | solution.py:111
  132.0 6.8 %all-to-all-done.1 = bf16[16,16,768]{2,1,0:T(8,128)(2,1)S(1)} async-done(((bf16[16,16,768]{2,1,0:T(8,128)(2,1)}), bf16[16,16,768]{2,1,0:T(8,128)(2,1)S(1)}, u32[]{:S(2)}, u32[]{:S(2)}) %all-to-all-start.1) | async-done | bytes 393248 | tf_op jit(solution)/shard_map/all_to_all | solution.py:111
  138.8 15.0 %fusion.35 = (f32[8192]{0:T(1024)S(1)}, f32[256,8192]{1,0:T(8,128)}) fusion(bf16[256,768]{1,0:T(8,128)(2,1)S(1)} %bitcast.30, bf16[8192,768]{1,0:T(8,128)(2,1)} %constant_dynamic-update-slice_fusion), kind=kOutput, calls=%fused_computation.88 | convolution fusion | flops 3225411584 | bytes 21397504 | tf_op jit(solution)/shard_map/dot_general | solution.py:23
  153.8 4.1 %collective-permute-start.18 = (f32[8192]{0:T(1024)S(1)}, f32[8192]{0:T(1024)S(1)}, u32[]{:S(2)}, u32[]{:S(2)}) collective-permute-start(f32[8192]{0:T(1024)S(1)} %get-tuple-element.16), channel_id=1, source_target_pairs={{0,4},{1,5},{2,6},{3,7},{4,0},{5,1},{6,2},{7,3},{8,12},{9,13},{10,... | collective-permute-start | bytes 98312 | tf_op jit(solution)/shard_map/ppermute | solution.py:64
  158.8 2.9 %collective-permute-start.19 = (f32[2,4096]{1,0:T(2,128)S(1)}, f32[2,4096]{1,0:T(2,128)S(1)}, u32[]{:S(2)}, u32[]{:S(2)}) collective-permute-start(f32[2,4096]{1,0:T(2,128)S(1)} %pad_maximum_fusion.1), channel_id=1, source_target_pairs={{0,3},{1,0},{2,1},{3,2},{4,7},{5,4},{6,5},{7,6},{8,11},{9,8},{10,9... | collective-permute-start | bytes 98312 | tf_op jit(solution)/shard_map/ppermute | solution.py:64
  162.8 3.0 %collective-permute-done.21 = f32[2,4096]{1,0:T(2,128)S(1)} collective-permute-done((f32[2,4096]{1,0:T(2,128)S(1)}, f32[2,4096]{1,0:T(2,128)S(1)}, u32[]{:S(2)}, u32[]{:S(2)}) %collective-permute-start.21) | collective-permute-done | bytes 32800 | tf_op jit(solution)/shard_map/ppermute | solution.py:64
  166.1 11.1 %fusion.14 = bf16[256,768]{1,0:T(8,128)(2,1)} fusion(bf16[8192,768]{1,0:T(8,128)(2,1)} %constant_dynamic-update-slice_fusion, f32[256,8192]{1,0:T(8,128)} %get-tuple-element.17, f32[8192]{0:T(1024)S(1)} %bitcast.40), kind=kOutput, calls=%fused_computation.28 | convolution fusion | flops 3225616384 | bytes 21397504 | tf_op jit(solution)/shard_map/dot_general | solution.py:98
  177.2 3.8 %all-to-all-start.2 = ((bf16[16,16,768]{2,1,0:T(8,128)(2,1)}), bf16[16,16,768]{2,1,0:T(8,128)(2,1)S(1)}, u32[]{:S(2)}, u32[]{:S(2)}) async-start(bf16[16,16,768]{2,1,0:T(8,128)(2,1)} %bitcast.6), calls=%async_computation.2 | async-start | bytes 786432 | tf_op jit(solution)/shard_map/all_to_all | solution.py:99
  182.7 6.3 %all-to-all-done.2 = bf16[16,16,768]{2,1,0:T(8,128)(2,1)S(1)} async-done(((bf16[16,16,768]{2,1,0:T(8,128)(2,1)}), bf16[16,16,768]{2,1,0:T(8,128)(2,1)S(1)}, u32[]{:S(2)}, u32[]{:S(2)}) %all-to-all-start.2) | async-done | bytes 393248 | tf_op jit(solution)/shard_map/all_to_all | solution.py:99
  189.0 7.8 %all-to-all-start.4 = ((s32[128,1,16]{2,1,0:T(1,128)}), s32[128,1,16]{2,1,0:T(1,128)S(1)}, u32[]{:S(2)}, u32[]{:S(2)}) async-start(s32[128,1,16]{2,1,0:T(1,128)} %bitcast.8), calls=%async_computation.4 | async-start | bytes 131072 | tf_op jit(solution)/shard_map/all_to_all | solution.py:142
  197.8 8.6 %all-to-all-done.4 = s32[128,1,16]{2,1,0:T(1,128)S(1)} async-done(((s32[128,1,16]{2,1,0:T(1,128)}), s32[128,1,16]{2,1,0:T(1,128)S(1)}, u32[]{:S(2)}, u32[]{:S(2)}) %all-to-all-start.4) | async-done | bytes 8224 | tf_op jit(solution)/shard_map/all_to_all | solution.py:142
  206.3 3.6 %all-to-all-start.3 = ((bf16[16,16,768]{2,1,0:T(8,128)(2,1)}), bf16[16,16,768]{2,1,0:T(8,128)(2,1)S(1)}, u32[]{:S(2)}, u32[]{:S(2)}) async-start(bf16[16,16,768]{2,1,0:T(8,128)(2,1)} %broadcast_in_dim.34), calls=%async_computation.3 | async-start | bytes 786432 | tf_op jit(solution)/shard_map/all_to_all | solution.py:111
  209.9 5.1 %fusion.10 = bf16[2048,768]{1,0:T(8,128)(2,1)} fusion(bf16[1024,768]{1,0:T(8,128)(2,1)S(1)} %get-tuple-element.3, s32[1024]{0:T(1024)S(1)} %get-tuple-element.18), kind=kOutput, calls=%fused_computation.23 | convolution fusion | flops 3224895488 | bytes 4722688 | tf_op jit(solution)/shard_map/dot_general | solution.py:135
  215.0 4.2 %all-to-all-done.3 = bf16[16,16,768]{2,1,0:T(8,128)(2,1)S(1)} async-done(((bf16[16,16,768]{2,1,0:T(8,128)(2,1)}), bf16[16,16,768]{2,1,0:T(8,128)(2,1)S(1)}, u32[]{:S(2)}, u32[]{:S(2)}) %all-to-all-start.3) | async-done | bytes 393248 | tf_op jit(solution)/shard_map/all_to_all | solution.py:111
  219.2 5.9 %all-to-all-start.5 = ((bf16[128,16,768]{2,1,0:T(8,128)(2,1)}), bf16[128,16,768]{2,1,0:T(8,128)(2,1)}, u32[]{:S(2)}, u32[]{:S(2)}) async-start(bf16[128,16,768]{2,1,0:T(8,128)(2,1)} %bitcast.27), calls=%async_computation.5 | async-start | bytes 6291456 | tf_op jit(solution)/shard_map/all_to_all | solution.py:139
  227.9 39.1 %all-to-all-done.5 = bf16[128,16,768]{2,1,0:T(8,128)(2,1)} async-done(((bf16[128,16,768]{2,1,0:T(8,128)(2,1)}), bf16[128,16,768]{2,1,0:T(8,128)(2,1)}, u32[]{:S(2)}, u32[]{:S(2)}) %all-to-all-start.5) | async-done | bytes 3145760 | tf_op jit(solution)/shard_map/all_to_all | solution.py:139
  267.0 14.9 %fusion.4 = bf16[1,2048,2048]{2,1,0:T(8,128)(2,1)} fusion(s32[2048]{0:T(1024)S(1)} %eq.72, pred[2048]{0:T(1024)(128)(4,1)S(1)} %broadcast_compare_fusion, bf16[2048,768]{1,0:T(8,128)(2,1)} %bitcast.10), kind=kOutput, calls=%fused_computation.8 | convolution fusion | flops 6476005376 | bytes 11544576 | tf_op jit(solution)/shard_map/dot_general | solution.py:23
  (104 shorter events, 62.6 us)
Async XLA Ops:
  6.6 22.1 %collective-permute-start.2 = (bf16[512,768]{1,0:T(8,128)(2,1)}, bf16[512,768]{1,0:T(8,128)(2,1)S(1)}, u32[]{:S(2)}, u32[]{:S(2)}) collective-permute-start(bf16[512,768]{1,0:T(8,128)(2,1)} %get-tuple-element.5), channel_id=1, source_target_pairs={{0,1},{1,2},{2,3},{3,0},{4,5},{5,6},{6,7},{7,4},{8,9},{9,10},{10,1... | collective-permute-start | bytes 2359304 | tf_op jit(solution)/shard_map/ppermute | solution.py:64
  9.0 19.6 %collective-permute-start.1 = (bf16[512,768]{1,0:T(8,128)(2,1)}, bf16[512,768]{1,0:T(8,128)(2,1)}, u32[]{:S(2)}, u32[]{:S(2)}) collective-permute-start(bf16[512,768]{1,0:T(8,128)(2,1)} %get-tuple-element.4), channel_id=1, source_target_pairs={{0,3},{1,0},{2,1},{3,2},{4,7},{5,4},{6,5},{7,6},{8,11},{9,8},{10,9... | collective-permute-start | bytes 2359304 | tf_op jit(solution)/shard_map/ppermute | solution.py:64
  11.2 33.5 %collective-permute-start = (bf16[512,768]{1,0:T(8,128)(2,1)}, bf16[512,768]{1,0:T(8,128)(2,1)}, u32[]{:S(2)}, u32[]{:S(2)}) collective-permute-start(bf16[512,768]{1,0:T(8,128)(2,1)} %get-tuple-element.5), channel_id=1, source_target_pairs={{0,3},{1,0},{2,1},{3,2},{4,7},{5,4},{6,5},{7,6},{8,11},{9,8},{10,9... | collective-permute-start | bytes 2359304 | tf_op jit(solution)/shard_map/ppermute | solution.py:64
  28.6 21.0 %collective-permute-start.3 = (bf16[512,768]{1,0:T(8,128)(2,1)S(1)}, bf16[512,768]{1,0:T(8,128)(2,1)}, u32[]{:S(2)}, u32[]{:S(2)}) collective-permute-start(bf16[512,768]{1,0:T(8,128)(2,1)S(1)} %collective-permute-done.2), channel_id=1, source_target_pairs={{0,1},{1,2},{2,3},{3,0},{4,5},{5,6},{6,7},{7,4},{8,9},{9,10},{10,1... | collective-permute-start | bytes 2359304 | tf_op jit(solution)/shard_map/ppermute | solution.py:64
  28.6 32.9 %collective-permute-start.4 = (bf16[512,768]{1,0:T(8,128)(2,1)}, bf16[512,768]{1,0:T(8,128)(2,1)}, u32[]{:S(2)}, u32[]{:S(2)}) collective-permute-start(bf16[512,768]{1,0:T(8,128)(2,1)} %collective-permute-done.1), channel_id=1, source_target_pairs={{0,3},{1,0},{2,1},{3,2},{4,7},{5,4},{6,5},{7,6},{8,11},{9,8},{10,9... | collective-permute-start | bytes 2359304 | tf_op jit(solution)/shard_map/ppermute | solution.py:64
  31.3 34.0 %collective-permute-start.5 = (bf16[512,768]{1,0:T(8,128)(2,1)}, bf16[512,768]{1,0:T(8,128)(2,1)S(1)}, u32[]{:S(2)}, u32[]{:S(2)}) collective-permute-start(bf16[512,768]{1,0:T(8,128)(2,1)} %get-tuple-element.4), channel_id=1, source_target_pairs={{0,1},{1,2},{2,3},{3,0},{4,5},{5,6},{6,7},{7,4},{8,9},{9,10},{10,1... | collective-permute-start | bytes 2359304 | tf_op jit(solution)/shard_map/ppermute | solution.py:64
  31.3 36.3 %collective-permute-start.6 = (bf16[512,768]{1,0:T(8,128)(2,1)}, bf16[512,768]{1,0:T(8,128)(2,1)}, u32[]{:S(2)}, u32[]{:S(2)}) collective-permute-start(bf16[512,768]{1,0:T(8,128)(2,1)} %get-tuple-element.5), channel_id=1, source_target_pairs={{0,4},{1,5},{2,6},{3,7},{4,0},{5,1},{6,2},{7,3},{8,12},{9,13},{10,... | collective-permute-start | bytes 2359304 | tf_op jit(solution)/shard_map/ppermute | solution.py:64
  44.7 23.9 %collective-permute-start.7 = (bf16[512,768]{1,0:T(8,128)(2,1)}, bf16[512,768]{1,0:T(8,128)(2,1)S(1)}, u32[]{:S(2)}, u32[]{:S(2)}) collective-permute-start(bf16[512,768]{1,0:T(8,128)(2,1)} %get-tuple-element.4), channel_id=1, source_target_pairs={{0,4},{1,5},{2,6},{3,7},{4,0},{5,1},{6,2},{7,3},{8,12},{9,13},{10,... | collective-permute-start | bytes 2359304 | tf_op jit(solution)/shard_map/ppermute | solution.py:64
  49.7 21.5 %collective-permute-start.8 = (bf16[512,768]{1,0:T(8,128)(2,1)}, bf16[512,768]{1,0:T(8,128)(2,1)S(1)}, u32[]{:S(2)}, u32[]{:S(2)}) collective-permute-start(bf16[512,768]{1,0:T(8,128)(2,1)} %collective-permute-done), channel_id=1, source_target_pairs={{0,4},{1,5},{2,6},{3,7},{4,0},{5,1},{6,2},{7,3},{8,12},{9,13},{10,... | collective-permute-start | bytes 2359304 | tf_op jit(solution)/shard_map/ppermute | solution.py:64
  61.5 11.6 %collective-permute-start.9 = (bf16[512,768]{1,0:T(8,128)(2,1)}, bf16[512,768]{1,0:T(8,128)(2,1)S(1)}, u32[]{:S(2)}, u32[]{:S(2)}) collective-permute-start(bf16[512,768]{1,0:T(8,128)(2,1)} %collective-permute-done.1), channel_id=1, source_target_pairs={{0,4},{1,5},{2,6},{3,7},{4,0},{5,1},{6,2},{7,3},{8,12},{9,13},{10,... | collective-permute-start | bytes 2359304 | tf_op jit(solution)/shard_map/ppermute | solution.py:64
  65.3 8.9 %collective-permute-start.10 = (bf16[512,768]{1,0:T(8,128)(2,1)}, bf16[512,768]{1,0:T(8,128)(2,1)S(1)}, u32[]{:S(2)}, u32[]{:S(2)}) collective-permute-start(bf16[512,768]{1,0:T(8,128)(2,1)} %collective-permute-done.3), channel_id=1, source_target_pairs={{0,4},{1,5},{2,6},{3,7},{4,0},{5,1},{6,2},{7,3},{8,12},{9,13},{10,... | collective-permute-start | bytes 2359304 | tf_op jit(solution)/shard_map/ppermute | solution.py:64
  67.6 7.5 %collective-permute-start.11 = (bf16[512,768]{1,0:T(8,128)(2,1)}, bf16[512,768]{1,0:T(8,128)(2,1)S(1)}, u32[]{:S(2)}, u32[]{:S(2)}) collective-permute-start(bf16[512,768]{1,0:T(8,128)(2,1)} %collective-permute-done.4), channel_id=1, source_target_pairs={{0,4},{1,5},{2,6},{3,7},{4,0},{5,1},{6,2},{7,3},{8,12},{9,13},{10,... | collective-permute-start | bytes 2359304 | tf_op jit(solution)/shard_map/ppermute | solution.py:64
  68.6 7.5 %collective-permute-start.12 = (bf16[512,768]{1,0:T(8,128)(2,1)S(1)}, bf16[512,768]{1,0:T(8,128)(2,1)S(1)}, u32[]{:S(2)}, u32[]{:S(2)}) collective-permute-start(bf16[512,768]{1,0:T(8,128)(2,1)S(1)} %collective-permute-done.2), channel_id=1, source_target_pairs={{0,4},{1,5},{2,6},{3,7},{4,0},{5,1},{6,2},{7,3},{8,12},{9,13},{10,... | collective-permute-start | bytes 2359304 | tf_op jit(solution)/shard_map/ppermute | solution.py:64
  71.2 5.8 %collective-permute-start.13 = (bf16[512,768]{1,0:T(8,128)(2,1)S(1)}, bf16[512,768]{1,0:T(8,128)(2,1)S(1)}, u32[]{:S(2)}, u32[]{:S(2)}) collective-permute-start(bf16[512,768]{1,0:T(8,128)(2,1)S(1)} %collective-permute-done.5), channel_id=1, source_target_pairs={{0,4},{1,5},{2,6},{3,7},{4,0},{5,1},{6,2},{7,3},{8,12},{9,13},{10,... | collective-permute-start | bytes 2359304 | tf_op jit(solution)/shard_map/ppermute | solution.py:64
  96.6 4.0 %collective-permute-start.17 = (f32[2,4096]{1,0:T(2,128)S(1)}, f32[2,4096]{1,0:T(2,128)S(1)}, u32[]{:S(2)}, u32[]{:S(2)}) collective-permute-start(f32[2,4096]{1,0:T(2,128)S(1)} %pad_maximum_fusion), channel_id=1, source_target_pairs={{0,1},{1,2},{2,3},{3,0},{4,5},{5,6},{6,7},{7,4},{8,9},{9,10},{10,1... | collective-permute-start | bytes 98312 | tf_op jit(solution)/shard_map/ppermute | solution.py:64
  96.6 4.3 %collective-permute-start.16 = (f32[2,4096]{1,0:T(2,128)S(1)}, f32[2,4096]{1,0:T(2,128)S(1)}, u32[]{:S(2)}, u32[]{:S(2)}) collective-permute-start(f32[2,4096]{1,0:T(2,128)S(1)} %pad_maximum_fusion), channel_id=1, source_target_pairs={{0,2},{1,3},{2,0},{3,1},{4,6},{5,7},{6,4},{7,5},{8,10},{9,11},{10,... | collective-permute-start | bytes 98312 | tf_op jit(solution)/shard_map/ppermute | solution.py:64
  127.0 11.8 %all-to-all-start.1 = ((bf16[16,16,768]{2,1,0:T(8,128)(2,1)}), bf16[16,16,768]{2,1,0:T(8,128)(2,1)S(1)}, u32[]{:S(2)}, u32[]{:S(2)}) async-start(bf16[16,16,768]{2,1,0:T(8,128)(2,1)} %broadcast_in_dim.33), calls=%async_computation.1 | async-start | bytes 786432 | tf_op jit(solution)/shard_map/all_to_all | solution.py:111
  153.8 5.0 %collective-permute-start.18 = (f32[8192]{0:T(1024)S(1)}, f32[8192]{0:T(1024)S(1)}, u32[]{:S(2)}, u32[]{:S(2)}) collective-permute-start(f32[8192]{0:T(1024)S(1)} %get-tuple-element.16), channel_id=1, source_target_pairs={{0,4},{1,5},{2,6},{3,7},{4,0},{5,1},{6,2},{7,3},{8,12},{9,13},{10,... | collective-permute-start | bytes 98312 | tf_op jit(solution)/shard_map/ppermute | solution.py:64
  161.7 4.3 %collective-permute-start.20 = (f32[2,4096]{1,0:T(2,128)S(1)}, f32[2,4096]{1,0:T(2,128)S(1)}, u32[]{:S(2)}, u32[]{:S(2)}) collective-permute-start(f32[2,4096]{1,0:T(2,128)S(1)} %pad_maximum_fusion.1), channel_id=1, source_target_pairs={{0,2},{1,3},{2,0},{3,1},{4,6},{5,7},{6,4},{7,5},{8,10},{9,11},{10,... | collective-permute-start | bytes 98312 | tf_op jit(solution)/shard_map/ppermute | solution.py:64
  177.2 11.7 %all-to-all-start.2 = ((bf16[16,16,768]{2,1,0:T(8,128)(2,1)}), bf16[16,16,768]{2,1,0:T(8,128)(2,1)S(1)}, u32[]{:S(2)}, u32[]{:S(2)}) async-start(bf16[16,16,768]{2,1,0:T(8,128)(2,1)} %bitcast.6), calls=%async_computation.2 | async-start | bytes 786432 | tf_op jit(solution)/shard_map/all_to_all | solution.py:99
  189.0 17.4 %all-to-all-start.4 = ((s32[128,1,16]{2,1,0:T(1,128)}), s32[128,1,16]{2,1,0:T(1,128)S(1)}, u32[]{:S(2)}, u32[]{:S(2)}) async-start(s32[128,1,16]{2,1,0:T(1,128)} %bitcast.8), calls=%async_computation.4 | async-start | bytes 131072 | tf_op jit(solution)/shard_map/all_to_all | solution.py:142
  206.3 12.8 %all-to-all-start.3 = ((bf16[16,16,768]{2,1,0:T(8,128)(2,1)}), bf16[16,16,768]{2,1,0:T(8,128)(2,1)S(1)}, u32[]{:S(2)}, u32[]{:S(2)}) async-start(bf16[16,16,768]{2,1,0:T(8,128)(2,1)} %broadcast_in_dim.34), calls=%async_computation.3 | async-start | bytes 786432 | tf_op jit(solution)/shard_map/all_to_all | solution.py:111
  219.2 47.9 %all-to-all-start.5 = ((bf16[128,16,768]{2,1,0:T(8,128)(2,1)}), bf16[128,16,768]{2,1,0:T(8,128)(2,1)}, u32[]{:S(2)}, u32[]{:S(2)}) async-start(bf16[128,16,768]{2,1,0:T(8,128)(2,1)} %bitcast.27), calls=%async_computation.5 | async-start | bytes 6291456 | tf_op jit(solution)/shard_map/all_to_all | solution.py:139
  226.5 55.3 %collective-permute-start.22 = (bf16[256,768]{1,0:T(8,128)(2,1)S(1)}, bf16[256,768]{1,0:T(8,128)(2,1)S(1)}, u32[]{:S(2)}, u32[]{:S(2)}) collective-permute-start(bf16[256,768]{1,0:T(8,128)(2,1)S(1)} %bitcast.28), channel_id=1, source_target_pairs={{0,4},{1,5},{2,6},{3,7},{4,0},{5,1},{6,2},{7,3},{8,12},{9,13},{10,... | collective-permute-start | bytes 1179656 | tf_op jit(solution)/shard_map/ppermute | solution.py:64
  (7 other events, 94.6 us)

commit v2 on v0

v2 whole, which is shorter than its diff:
```python
import functools
import math

import jax
import jax.numpy as jnp
from jax import lax
from jax.experimental import pallas as pl
from jax.experimental.pallas import tpu as pltpu
from jax.sharding import PartitionSpec as P

ROUNDS = 2
AXES = ("dp", "cent")

epsilon = 1e-06
logit_divisor = 0.02
MIB = 1024 * 1024
LABEL_LANES = 128
NEAR_COST = 1_000_000
FAR_COST = 25_000_000_000
FULL = 61


def unit(matrix):
    wide = matrix.astype(jnp.float32)
    return wide / jnp.sqrt(jnp.sum(wide * wide, axis=-1, keepdims=True) + epsilon)


def normalize_rows(matrix):
    return unit(matrix).astype(jnp.bfloat16)


def contract_final_axis(left, right):
    return lax.dot_general(
        left, right, (((1,), (1,)), ((), ())), preferred_element_type=jnp.float32
    )


def whole():
    return pl.BlockSpec(memory_space=pltpu.VMEM)


def in_hbm():
    return pl.BlockSpec(memory_space=pl.ANY)


def call(kernel, name, vmem, flops, **options):
    return pl.pallas_call(
        kernel,
        name=name,
        cost_estimate=pl.CostEstimate(flops=int(flops), bytes_accessed=1 << 20, transcendentals=0),
        compiler_params=pltpu.CompilerParams(vmem_limit_bytes=vmem * MIB),
        **options,
    )


def membership_of(block, rows, scale):
    scores = contract_final_axis(block, rows)
    membership = jnp.exp2(scores * (scale * (math.log2(math.e) / logit_divisor)))
    return membership.astype(jnp.bfloat16), jnp.sum(membership, axis=0, keepdims=True)


def piece_kernel(raw_ref, block_ref, member_ref, total_ref, scale_ref):
    wide = raw_ref[...].astype(jnp.float32)
    squares = jnp.sum(wide * wide, axis=-1, keepdims=True) + epsilon
    scale = (1.0 / jnp.sqrt(jnp.broadcast_to(squares, (squares.shape[0], 8)))).T[:1]
    scale_ref[...] = scale
    member_ref[...], total_ref[...] = membership_of(block_ref[...], raw_ref[...], scale)


def score_piece(raw, block, cost):
    size, width = raw.shape
    count = block.shape[0]
    line = jax.ShapeDtypeStruct((1, size), jnp.float32)
    return call(
        piece_kernel,
        "score_piece",
        12,
        cost,
        in_specs=[whole(), whole()],
        out_specs=[whole()] * 3,
        out_shape=[jax.ShapeDtypeStruct((count, size), jnp.bfloat16), line, line],
    )(raw, block)


def fetches(sources, taken, sems):
    size = sources[1].shape[0]
    parts = [sources[0].at[pl.ds(0, size)], sources[0].at[pl.ds(size, size)]] + list(sources[1:])
    return [
        pltpu.make_async_copy(part, taken.at[pl.ds(i * size, size)], sems.at[i])
        for i, part in enumerate(parts)
    ]


def score_kernel(pieces, scale_ref, own_ref, other_ref, *rest):
    sources, outs = rest[: pieces - 1], rest[pieces - 1 :]
    member_refs, total_ref = outs[:pieces], outs[pieces]
    taken, members, block, in_sem, out_sem = outs[pieces + 1 :]
    half = own_ref.shape[0]
    size = sources[1].shape[0]
    arriving = fetches(sources, taken, in_sem)
    for copy in arriving:
        copy.start()
    block[:half], block[half:] = own_ref[...], other_ref[...]
    leaving = []
    for i in range(pieces):
        arriving[i].wait()
        at = slice(i * size, (i + 1) * size)
        members[i], total_ref[:, at] = membership_of(block[...], taken[at], scale_ref[:, at])
        leaving.append(pltpu.make_async_copy(members.at[i], member_refs[i], out_sem.at[i]))
        leaving[-1].start()
    for copy in leaving:
        copy.wait()


def score_rows(sources, scale, own_half, other_half):
    pieces = len(sources) + 1
    size, width = sources[1].shape
    count = 2 * own_half.shape[0]
    each = pltpu.SemaphoreType.DMA((pieces,))
    out = call(
        functools.partial(score_kernel, pieces),
        "score_rows",
        FULL,
        2 * pieces * size * width * count,
        in_specs=[whole()] * 3 + [in_hbm()] * len(sources),
        out_specs=[in_hbm()] * pieces + [whole()],
        out_shape=[jax.ShapeDtypeStruct((count, size), jnp.bfloat16)] * pieces
        + [jax.ShapeDtypeStruct((1, pieces * size), jnp.float32)],
        scratch_shapes=[
            pltpu.VMEM((pieces * size, width), jnp.bfloat16),
            pltpu.VMEM((pieces, count, size), jnp.bfloat16),
            pltpu.VMEM((count, width), jnp.bfloat16),
            each,
            each,
        ],
    )(scale, own_half, other_half, *sources)
    return out[:pieces], out[pieces]


def sum_kernel(pieces, depth, scale_ref, *rest):
    total_refs, rest = rest[:depth], rest[depth:]
    member_refs, sources = rest[:pieces], rest[pieces : 2 * pieces - 1]
    own_ref, other_ref, members, taken, running, member_sem, row_sem = rest[-7:]
    half = own_ref.shape[0]
    size = sources[1].shape[0]
    arriving = [
        (rows, pltpu.make_async_copy(member_refs[i], members.at[i], member_sem.at[i]))
        for i, rows in enumerate(fetches(sources, taken, row_sem))
    ]
    for pair in arriving:
        for copy in pair:
            copy.start()
    for i in range(pieces):
        for copy in arriving[i]:
            copy.wait()
        at = slice(i * size, (i + 1) * size)
        total = total_refs[0][:, at]
        for k in range(1, depth):
            j = (i + pieces - k * (pieces // depth)) % pieces
            total = total + total_refs[k][:, j * size : (j + 1) * size]
        weights = members[i].astype(jnp.float32) * (scale_ref[:, at] / total)
        product = jnp.dot(
            weights.astype(jnp.bfloat16), taken[at], preferred_element_type=jnp.float32
        )
        if i == 0:
            running[...] = product
        else:
            running[...] += product
    own_ref[...] = running[:half].astype(jnp.bfloat16)
    other_ref[...] = running[half:].astype(jnp.bfloat16)


def weighted_sums(members, sources, scale, totals, after):
    pieces = len(members)
    count, size = members[0].shape
    width = sources[0].shape[1]
    sums = jax.ShapeDtypeStruct((count // 2, width), jnp.bfloat16)
    return call(
        functools.partial(sum_kernel, pieces, len(totals)),
        "weighted_sums",
        FULL,
        2 * pieces * size * width * count,
        in_specs=[whole()] * (1 + len(totals))
        + [in_hbm()] * (2 * pieces - 1)
        + [in_hbm()] * len(after),
        out_specs=[whole()] * 2,
        out_shape=[sums] * 2,
        scratch_shapes=[
            pltpu.VMEM((pieces, count, size), jnp.bfloat16),
            pltpu.VMEM((pieces * size, width), jnp.bfloat16),
            pltpu.VMEM((count, width), jnp.float32),
            pltpu.SemaphoreType.DMA((pieces,)),
            pltpu.SemaphoreType.DMA((pieces,)),
        ],
    )(scale, *totals, *members, *sources, *after)


def combine_kernel(arrived_ref, *rest):
    spread_ref = rest[-1]
    planes = arrived_ref.shape[0]
    total = arrived_ref[0].astype(jnp.float32)
    for i in range(1, planes):
        total = total + arrived_ref[i].astype(jnp.float32)
    share = normalize_rows(total)
    for i in range(planes):
        spread_ref[i] = share


def combine(arrived, after):
    return call(
        combine_kernel,
        "combine",
        FULL,
        2 * arrived.size,
        in_specs=[whole()] + [pl.BlockSpec(memory_space=pl.ANY)] * len(after),
        out_specs=whole(),
        out_shape=jax.ShapeDtypeStruct(arrived.shape, arrived.dtype),
    )(arrived, *after)


def column_of(row):
    return jnp.broadcast_to(row, (8, row.shape[1])).T[:, :1]


def pack_kernel(devices, cent_count, capacity, depth_ref, raw_ref, assign_ref, table_ref, out_ref, rows, place):
    step = pl.program_id(0)
    local_rows, width = raw_ref.shape
    high_count, low_count = table_ref.shape

    @pl.when(step == 0)
    def _():
        rows[:, :width] = normalize_rows(raw_ref[...])
        cluster = assign_ref[...]
        high, low = lax.div(cluster, low_count), lax.rem(cluster, low_count)
        high_hits = lax.broadcasted_iota(jnp.int32, (high_count, local_rows), 0) == high
        by_low = lax.dot_general(
            table_ref[...].astype(jnp.bfloat16),
            jnp.where(high_hits, 1.0, 0.0).astype(jnp.bfloat16),
            (((0,), (0,)), ((), ())),
            preferred_element_type=jnp.float32,
        )
        low_hits = lax.broadcasted_iota(jnp.int32, (low_count, local_rows), 0) == low
        owner = jnp.sum(jnp.where(low_hits, by_low, 0.0), axis=0, keepdims=True).astype(jnp.int32)
        owner_hits = lax.broadcasted_iota(jnp.int32, (devices, local_rows), 0) == owner
        earlier = lax.broadcasted_iota(jnp.int32, (local_rows, local_rows), 0) < (
            lax.broadcasted_iota(jnp.int32, (local_rows, local_rows), 1)
        )
        before = jnp.dot(
            jnp.where(owner_hits, 1.0, 0.0).astype(jnp.bfloat16),
            jnp.where(earlier, 1.0, 0.0).astype(jnp.bfloat16),
            preferred_element_type=jnp.float32,
        )
        slot = jnp.sum(jnp.where(owner_hits, before, 0.0), axis=0, keepdims=True).astype(jnp.int32)
        owner_dp, owner_depth = lax.div(owner, cent_count), lax.rem(owner, cent_count)
        distance = lax.rem(owner_depth + cent_count - depth_ref[0], cent_count)
        place[...] = (owner_dp * cent_count + distance) * capacity + slot
        number = column_of((cluster + 1).astype(jnp.float32)).astype(jnp.int32)
        lane = lax.broadcasted_iota(jnp.int32, (local_rows, LABEL_LANES), 1)
        digits = jnp.where(
            lane == 0, lax.div(number, 256), jnp.where(lane == 1, lax.rem(number, 256), 0)
        )
        rows[:, width:] = digits.astype(jnp.float32).astype(jnp.bfloat16)

    size = out_ref.shape[0]
    taken = lax.broadcasted_iota(jnp.int32, (size, local_rows), 0) + step * size == place[...]
    taken = jnp.where(taken, 1.0, 0.0).astype(jnp.bfloat16)
    out_ref[...] = jnp.dot(taken, rows[...], preferred_element_type=jnp.float32).astype(jnp.bfloat16)


def pack(embeddings, assign, owner_map, depth, devices, cent_count, capacity):
    local_rows, width = embeddings.shape
    slots = devices * capacity
    tile = min(512, slots)
    low_count = 128
    return call(
        functools.partial(pack_kernel, devices, cent_count, capacity),
        "pack",
        FULL,
        2 * slots * width * local_rows,
        grid=(slots // tile,),
        in_specs=[pl.BlockSpec(memory_space=pltpu.SMEM), whole(), whole(), whole()],
        out_specs=pl.BlockSpec((tile, width + LABEL_LANES), lambda i: (i, 0)),
        out_shape=jax.ShapeDtypeStruct((slots, width + LABEL_LANES), jnp.bfloat16),
        scratch_shapes=[
            pltpu.VMEM((local_rows, width + LABEL_LANES), jnp.bfloat16),
            pltpu.VMEM((1, local_rows), jnp.int32),
        ],
    )(
        depth.reshape(1).astype(jnp.int32),
        embeddings,
        assign.reshape(1, local_rows),
        owner_map.reshape(-1, low_count).astype(jnp.float32),
    )


def join_kernel(cent_count, total_ref, label_ref, *rest):
    out_refs = rest[-(cent_count - 1) :]
    group_rows = total_ref.shape[1]
    for k in range(1, cent_count):
        out_refs[k - 1][:, :group_rows] = total_ref[...]
        out_refs[k - 1][:, group_rows:] = label_ref[cent_count - k : cent_count - k + 1]


def join(totals, label, after):
    cent_count, labels = label.shape
    joined = jax.ShapeDtypeStruct((1, totals.shape[1] + labels), jnp.float32)
    return call(
        functools.partial(join_kernel, cent_count),
        "join",
        FULL,
        totals.size,
        in_specs=[whole()] * 2 + [in_hbm()] * len(after),
        out_specs=[whole()] * (cent_count - 1),
        out_shape=[joined] * (cent_count - 1),
    )(totals, label, *after)


def similarity_kernel(cent_count, depth_ref, *rest):
    block_refs = rest[:cent_count]
    row_ref, out_ref, gathered, column, sem = rest[cent_count:]
    step = pl.program_id(0)

    @pl.when(step == 0)
    def _():
        arriving = []
        for k in range(cent_count):
            source = lax.rem(depth_ref[0] + cent_count - k, cent_count)
            block = block_refs[k].at[:, 0, :, pl.ds(0, gathered.shape[-1])] if k == 0 else block_refs[k]
            arriving.append(pltpu.make_async_copy(block, gathered.at[:, source], sem.at[k]))
            arriving[-1].start()
        row = row_ref[...]
        column[...] = column_of(jnp.where(row > 0.0, row, -1.0))
        for copy in arriving:
            copy.wait()

    size = out_ref.shape[1]
    slots, width = out_ref.shape[2], gathered.shape[-1]
    per_step = size // (gathered.shape[1] * gathered.shape[2])
    rows = gathered[pl.ds(step * per_step, per_step)].reshape(size, width)
    inner = contract_final_axis(rows, gathered[...].reshape(slots, width))
    start = pl.multiple_of(step * size, size)
    same = column[pl.ds(start, size)] == row_ref[...]
    out_ref[0] = jnp.where(same, inner * math.sqrt(width), 0.0).astype(jnp.bfloat16)
    main_diagonal = lax.broadcasted_iota(jnp.int32, (size, size), 0) == (
        lax.broadcasted_iota(jnp.int32, (size, size), 1)
    )
    corner = out_ref[0, :, pl.ds(start, size)]
    out_ref[0, :, pl.ds(start, size)] = jnp.where(
        main_diagonal, 0.0, corner.astype(jnp.float32)
    ).astype(jnp.bfloat16)


def similarity_of(blocks, label, depth):
    cent_count = len(blocks)
    dp_count, capacity, width = blocks[1].shape
    slots = cent_count * dp_count * capacity
    tile = min(256, slots)
    return call(
        functools.partial(similarity_kernel, cent_count),
        "similarity",
        FULL,
        2 * slots * slots * width,
        grid=(slots // tile,),
        in_specs=[pl.BlockSpec(memory_space=pltpu.SMEM)]
        + [in_hbm()] * cent_count
        + [pl.BlockSpec((1, slots), lambda i: (0, 0))],
        out_specs=pl.BlockSpec((1, tile, slots), lambda i: (0, i, 0)),
        out_shape=jax.ShapeDtypeStruct((1, slots, slots), jnp.bfloat16),
        scratch_shapes=[
            pltpu.VMEM((dp_count, cent_count, capacity, width), jnp.bfloat16),
            pltpu.VMEM((slots, 1), jnp.float32),
            pltpu.SemaphoreType.DMA((cent_count,)),
        ],
    )(depth.reshape(1).astype(jnp.int32), *blocks, label)


def shards(embeddings, init_centroids, assign, owner_map):
    devices = lax.axis_size(AXES)
    cent_count = lax.axis_size("cent")
    dp_count = lax.axis_size("dp")
    depth = lax.axis_index("cent")
    local_rows, feature_width = embeddings.shape
    planes = dp_count // 2
    core = lax.axis_index("dp") % 2
    half = init_centroids.shape[0] // 2
    share = half // planes
    capacity = 2 * local_rows // devices
    group_rows = cent_count * local_rows

    def send(value, step):
        return lax.ppermute(
            value, "cent", [(z, (z + step) % cent_count) for z in range(cent_count)]
        )

    def exchange(value):
        return lax.all_to_all(value, "dp", 0, 0, tiled=True)

    same_core = [[2 * chip + c for chip in range(planes)] for c in range(2)]
    other_core = [(i, i + 1 - 2 * (i % 2)) for i in range(dp_count)]

    def exchange_plane(value):
        return lax.all_to_all(value, "dp", 0, 0, axis_index_groups=same_core, tiled=True)

    def swap_cores(value):
        return lax.ppermute(value, "dp", other_core)

    cut = local_rows // 2
    first, second = embeddings[:cut], embeddings[cut:]
    below_first, above_second = send(first, 1), send(second, -1)
    below_second, above_first = send(second, 1), send(first, -1)
    far_first, far_second = send(below_first, 1), send(above_second, -1)
    received = [above_first, above_second, far_first, far_second, below_first, below_second]
    sources = [embeddings] + received

    packed = pack(embeddings, assign, owner_map, depth, devices, cent_count, capacity)
    routed = exchange(packed.reshape(dp_count, cent_count * capacity, -1)).reshape(
        dp_count, cent_count, capacity, -1
    )
    digits = routed[..., feature_width : feature_width + 2].astype(jnp.float32)
    routed_label = (
        (digits[..., 0] * 256.0 + digits[..., 1])
        .transpose(1, 0, 2)
        .reshape(cent_count, dp_count * capacity)
    )

    initial = normalize_rows(init_centroids)
    own_half = lax.dynamic_slice_in_dim(initial, core * half, half, 0)
    other_half = lax.dynamic_slice_in_dim(initial, (1 - core) * half, half, 0)
    block = jnp.concatenate([own_half, other_half])
    scored = [
        score_piece(piece, block, FAR_COST if piece is far_first or piece is far_second else NEAR_COST)
        for piece in [first, second] + received
    ]
    members = [member for member, _, _ in scored]
    partial_total = jnp.concatenate([total for _, total, _ in scored], axis=1)
    scale = jnp.concatenate([scale for _, _, scale in scored], axis=1)

    def reduced(members, totals, after):
        own, for_sibling = weighted_sums(members, sources, scale, totals, after)
        both = own.astype(jnp.float32) + swap_cores(for_sibling).astype(jnp.float32)
        return exchange_plane(both.astype(jnp.bfloat16).reshape(planes, share, feature_width))

    totals = [partial_total] + [send(partial_total, -k) for k in range(1, cent_count)]
    arrived = reduced(members, totals, [routed])

    parted = [routed[:, k, :, :feature_width] for k in range(cent_count)]
    blocks = [routed, send(parted[1], 1), None, send(parted[3], -1)]
    blocks[2] = send(parted[2] + blocks[1] * 0, 2)

    own_half = exchange_plane(combine(arrived, [blocks[1], blocks[3]])).reshape(half, feature_width)
    members, partial_total = score_rows(sources, scale, own_half, swap_cores(own_half))
    joined = join(partial_total, routed_label, [blocks[2]])
    totals, label = [partial_total], [routed_label[0].reshape(dp_count, capacity)]
    for k in range(1, cent_count):
        got = send(joined[k - 1], -k)
        totals.append(got)
        label.append(got[:, group_rows:].reshape(dp_count, capacity))
    label = jnp.roll(jnp.stack(label, axis=1), depth, axis=1).reshape(1, -1)
    similarity = similarity_of(blocks, label, depth)
    arrived = reduced(members, totals, [])
    own_half = exchange_plane(combine(arrived, [similarity])).reshape(half, feature_width)
    other_half = swap_cores(own_half)
    centroids = jnp.where(
        core == 0,
        jnp.concatenate([own_half, other_half]),
        jnp.concatenate([other_half, own_half]),
    ).astype(jnp.float32) * math.sqrt(feature_width)
    return (centroids, similarity)


def solution(mesh):
    return jax.shard_map(
        shards,
        mesh=mesh,
        in_specs=(P(AXES, None), P("cent", None), P(AXES), P()),
        out_specs=(P("cent", None), P(AXES, None, None)),
        check_vma=False,
    )
```

time: 604 us -> 205 us (0.34)
  waiting for transfers between devices: 457 us -> 38 us
  Pallas kernels: 0 us -> 61.2 us
  matrix products: 33.5 us -> 0 us
  starting transfers between devices: 16.5 us -> 48.1 us
  blocking collectives: 52.4 us -> 29.6 us
  between operations: 13.9 us -> 1.11 us
  other arithmetic: 19.5 us -> 8.13 us
  local copies, waits for them, and re-layouts: 11 us -> 17.7 us
    reduce_scatter x2 -> x0, waiting for transfers between devices: 334 us -> none  [shards(): lax.psum_scatter(contract_first(weights, unit_rows), ('dp', 'cent'), scat...]
    all_gather x2 -> x0, waiting for transfers between devices: 80.1 us -> none  [shards(): gathered = lax.all_gather(centroid_block, 'cent', axis=0, tiled=True)]
    pallas_call x0 -> x16, Pallas kernels: none -> 61.2 us  [the longest x2 17.4 us: weighted_sums(): call(functools.partial(sum_kernel, pieces, len(totals)), 'weighted_sums',...]
    all_gather x2 -> x0, blocking collectives: 52.4 us -> none  [shards(): centroid_block = lax.all_gather(unit_share, 'dp', axis=0, tiled=True)]
    dot_general x5 -> x0, matrix products: 33.5 us -> none  [the longest x3 19.6 us: contract_final_axis(): lax.dot_general(left, right, (((1,), (1,)), ((), ())), preferred_element_...]
    all_to_all x2 -> x3, waiting for transfers between devices: 42.5 us -> 10.4 us  [the longest x2 5.56 us: exchange_plane(): lax.all_to_all(value, 'dp', 0, 0, axis_index_groups=same_core, tiled=True)]
    all_to_all x0 -> x2, blocking collectives: none -> 29.6 us  [exchange_plane(): lax.all_to_all(value, 'dp', 0, 0, axis_index_groups=same_core, tiled=True)]
    ppermute x0 -> x19, waiting for transfers between devices: none -> 27.5 us  [the longest x15 26.2 us: send(): lax.ppermute(value, 'cent', [(z, (z + step) % cent_count) for z in range(...]
  transfers between devices with their start and end apart: 6 -> 22, of which waited for: 6 -> 10; matrix products, arithmetic and copies ran while one was open for 5% -> 6% of each run, Pallas kernels for 0% -> 19%
where the time goes in v2:
time: 205 us; the launch traced here: 204 us
  Pallas kernels  61.2 us (30%)
  starting transfers between devices  48.1 us (23%)
  waiting for transfers between devices  38 us (19%)
  blocking collectives  29.6 us (14%)
  local copies, waits for them, and re-layouts  17.7 us (9%)
  other arithmetic  8.13 us (4%)
    all_to_all x2, blocking collectives, exchange_plane(): lax.all_to_all(value, 'dp', 0, 0, axis_index_groups=same_core, tiled=True)  29.6 us
    ppermute x15, waiting for transfers between devices, send(): lax.ppermute(value, 'cent', [(z, (z + step) % cent_count) for z in range(...  26.2 us
    ppermute x15, starting transfers between devices, send(): lax.ppermute(value, 'cent', [(z, (z + step) % cent_count) for z in range(...  19.6 us
    pallas_call x2, Pallas kernels, weighted_sums(): call(functools.partial(sum_kernel, pieces, len(totals)), 'weighted_sums',...  17.4 us
    pallas_call x1, Pallas kernels, similarity_of(): call(functools.partial(similarity_kernel, cent_count), 'similarity', FULL...  12.2 us
    all_to_all x2, starting transfers between devices, exchange_plane(): lax.all_to_all(value, 'dp', 0, 0, axis_index_groups=same_core, tiled=True)  12.1 us
    unnamed x75, local copies, waits for them, and re-layouts  9.47 us
    pallas_call x8, Pallas kernels, score_piece(): call(piece_kernel, 'score_piece', 12, cost, in_specs=[whole(), whole()],...  8.87 us
  transfers between devices with their start and end apart: 22, of which 10 were waited for; matrix products, arithmetic and copies ran while one was open for 6% of the time, Pallas kernels for 19%

profile of v2, /device:TPU:1, one launch (start us, length us, event | category | flops | bytes accessed | tf_op | source)
XLA Modules:
  0.0 203.8 jit_solution(11407764510873169249)
XLA Ops:
  2.1 4.7 %collective-permute-start = (bf16[512,768]{1,0:T(8,128)(2,1)S(1)}, bf16[512,768]{1,0:T(8,128)(2,1)S(1)}, u32[]{:S(2)}, u32[]{:S(2)}) collective-permute-start(bf16[512,768]{1,0:T(8,128)(2,1)S(1)} %get-tuple-element.85.raw_ref), channel_id=1, source_target_pairs={{0,3},{1,0},{2,1},{3,2},{4,7},{5,4},{6,5},{7,6},{8,11},{9,8},{10,9... | collective-permute-start | bytes 2359304 | tf_op jit(solution)/shard_map/ppermute | solution.py:391
  6.8 2.7 %collective-permute-start.1 = (bf16[512,768]{1,0:T(8,128)(2,1)S(1)}, bf16[512,768]{1,0:T(8,128)(2,1)}, u32[]{:S(2)}, u32[]{:S(2)}) collective-permute-start(bf16[512,768]{1,0:T(8,128)(2,1)S(1)} %get-tuple-element.84.raw_ref), channel_id=1, source_target_pairs={{0,3},{1,0},{2,1},{3,2},{4,7},{5,4},{6,5},{7,6},{8,11},{9,8},{10,9... | collective-permute-start | bytes 2359304 | tf_op jit(solution)/shard_map/ppermute | solution.py:391
  10.1 8.8 %pack.1 = bf16[2048,896]{1,0:T(8,128)(2,1)} custom-call(s32[1]{0:T(128)} %bitcast.depth_ref, bf16[1024,768]{1,0:T(8,128)(2,1)} %rest_12_.3, s32[1,1024]{1,0:T(1,128)} %bitcast.40, f32[16,128]{1,0:T(8,128)} %convert_bitcast_fusion.table_ref), custom_call_target="tpu_custom_call" | custom-call | flops 3221225472 | bytes 1048576 | tf_op jit(solution)/shard_map/pack/pallas_call | solution.py:275
  18.9 8.7 %all-to-all-start = ((bf16[32,64,896]{2,1,0:T(8,128)(2,1)}), bf16[32,64,896]{2,1,0:T(8,128)(2,1)}, u32[]{:S(2)}, u32[]{:S(2)}) async-start(bf16[32,64,896]{2,1,0:T(8,128)(2,1)} %bitcast.34), calls=%async_computation | async-start | bytes 7340032 | tf_op jit(solution)/shard_map/all_to_all | solution.py:396
  31.9 7.9 %collective-permute-done.1.raw_ref.rest_14_.rest_2_ = bf16[512,768]{1,0:T(8,128)(2,1)} collective-permute-done((bf16[512,768]{1,0:T(8,128)(2,1)S(1)}, bf16[512,768]{1,0:T(8,128)(2,1)}, u32[]{:S(2)}, u32[]{:S(2)}) %collective-permute-start.1) | collective-permute-done | bytes 786464 | tf_op jit(solution)/shard_map/ppermute | solution.py:391
  39.8 3.5 %collective-permute-start.4 = (bf16[512,768]{1,0:T(8,128)(2,1)}, bf16[512,768]{1,0:T(8,128)(2,1)S(1)}, u32[]{:S(2)}, u32[]{:S(2)}) collective-permute-start(bf16[512,768]{1,0:T(8,128)(2,1)} %collective-permute-done.1.raw_ref.rest_14_.rest_2_), channel_id=1, source_target_pairs={{0,3},{1,0},{2,1},{3,2},{4,7},{5,4},{6,5},{7,6},{8,11},{9,8},{10,9... | collective-permute-start | bytes 2359304 | tf_op jit(solution)/shard_map/ppermute | solution.py:391
  49.3 2.0 score_piece.15
  52.1 7.8 %collective-permute-done.3.raw_ref.rest_15_.rest_3_ = bf16[512,768]{1,0:T(8,128)(2,1)S(1)} collective-permute-done((bf16[512,768]{1,0:T(8,128)(2,1)}, bf16[512,768]{1,0:T(8,128)(2,1)S(1)}, u32[]{:S(2)}, u32[]{:S(2)}) %collective-permute-start.3) | collective-permute-done | bytes 786464 | tf_op jit(solution)/shard_map/ppermute | solution.py:391
  65.8 2.9 %collective-permute-done.7.rest_2_ = f32[1,4096]{1,0:T(1,128)S(1)} collective-permute-done((f32[1,4096]{1,0:T(1,128)S(1)}, f32[1,4096]{1,0:T(1,128)S(1)}, u32[]{:S(2)}, u32[]{:S(2)}) %collective-permute-start.7) | collective-permute-done | bytes 16416 | tf_op jit(solution)/shard_map/ppermute | solution.py:391
  68.7 4.9 %all-to-all-done = bf16[32,64,896]{2,1,0:T(8,128)(2,1)} async-done(((bf16[32,64,896]{2,1,0:T(8,128)(2,1)}), bf16[32,64,896]{2,1,0:T(8,128)(2,1)}, u32[]{:S(2)}, u32[]{:S(2)}) %all-to-all-start) | async-done | bytes 3670048 | tf_op jit(solution)/shard_map/all_to_all | solution.py:396
  73.6 8.7 %weighted_sums.2 = (bf16[256,768]{1,0:T(8,128)(2,1)}, bf16[256,768]{1,0:T(8,128)(2,1)}) custom-call(f32[1,4096]{1,0:T(1,128)} %copy-done.18, f32[1,4096]{1,0:T(1,128)} %copy-done.17, f32[1,4096]{1,0:T(1,128)} %copy-done.19, f32[1,4096]{1,0:T(1,128)} %copy-done.20, f32[1,4096]{1,0:T(1,128)} %copy-done.21, bf16[512,512]{1,0:T(8,128)(2,1)} %copy-done.3, ...), custom_call_target="tpu_custom_call" | custom-call | flops 3221225472 | bytes 1048576 | tf_op jit(solution)/shard_map/weighted_sums/pallas_call | solution.py:178
  84.9 3.0 %collective-permute-start.11 = (bf16[32,16,768]{2,1,0:T(8,128)(2,1)S(1)}, bf16[32,16,768]{2,1,0:T(8,128)(2,1)S(1)}, u32[]{:S(2)}, u32[]{:S(2)}) collective-permute-start(bf16[32,16,768]{2,1,0:T(8,128)(2,1)S(1)} %get-tuple-element.82), channel_id=1, source_target_pairs={{0,3},{1,0},{2,1},{3,2},{4,7},{5,4},{6,5},{7,6},{8,11},{9,8},{10,9... | collective-permute-start | bytes 2359304 | tf_op jit(solution)/shard_map/ppermute | solution.py:391
  88.0 14.7 %all_to_all.25.arrived_ref = bf16[16,16,768]{2,1,0:T(8,128)(2,1)} all-to-all(bf16[16,16,768]{2,1,0:T(8,128)(2,1)S(1)} %bitcast.37), channel_id=1, replica_groups={{0,8,16,24,32,40,48,56,64,72,80,88,96,104,112,120},{4,12,20,28,36,44,52..., dimensions={0} | all-to-all | bytes 786432 | tf_op jit(solution)/shard_map/all_to_all | solution.py:402
  102.7 2.9 %collective-permute-done.10.rest_0_.rest_1_ = bf16[32,16,768]{2,1,0:T(8,128)(2,1)S(1)} collective-permute-done((bf16[32,16,768]{2,1,0:T(8,128)(2,1)S(1)}, bf16[32,16,768]{2,1,0:T(8,128)(2,1)S(1)}, u32[]{:S(2)}, u32[]{:S(2)}) %collective-permute-start.10) | collective-permute-done | bytes 786464 | tf_op jit(solution)/shard_map/ppermute | solution.py:391
  109.4 5.5 %all-to-all-start.2 = ((bf16[16,16,768]{2,1,0:T(8,128)(2,1)}), bf16[16,16,768]{2,1,0:T(8,128)(2,1)S(1)}, u32[]{:S(2)}, u32[]{:S(2)}) async-start(bf16[16,16,768]{2,1,0:T(8,128)(2,1)} %combine.2), calls=%async_computation.2 | async-start | bytes 786432 | tf_op jit(solution)/shard_map/all_to_all | solution.py:402
  117.6 5.6 %all-to-all-done.2 = bf16[16,16,768]{2,1,0:T(8,128)(2,1)S(1)} async-done(((bf16[16,16,768]{2,1,0:T(8,128)(2,1)}), bf16[16,16,768]{2,1,0:T(8,128)(2,1)S(1)}, u32[]{:S(2)}, u32[]{:S(2)}) %all-to-all-start.2) | async-done | bytes 393248 | tf_op jit(solution)/shard_map/all_to_all | solution.py:402
  123.2 2.5 %collective-permute-start.12 = (bf16[256,768]{1,0:T(8,128)(2,1)S(1)}, bf16[256,768]{1,0:T(8,128)(2,1)S(1)}, u32[]{:S(2)}, u32[]{:S(2)}) collective-permute-start(bf16[256,768]{1,0:T(8,128)(2,1)S(1)} %bitcast.38), channel_id=1, source_target_pairs={{0,4},{4,0},{8,12},{12,8},{16,20},{20,16},{24,28},{28,24},{32,36},... | collective-permute-start | bytes 1179656 | tf_op jit(solution)/shard_map/ppermute | solution.py:405
  129.0 8.8 %score_rows.1 = (bf16[512,512]{1,0:T(8,128)(2,1)}, bf16[512,512]{1,0:T(8,128)(2,1)}, bf16[512,512]{1,0:T(8,128)(2,1)}, bf16[512,512]{1,0:T(8,128)(2,1)}, bf16[51...) custom-call(f32[1,4096]{1,0:T(1,128)} %copy-done.18, ...), custom_call_target="tpu_custom_call" | custom-call | flops 3221225472 | bytes 1048576 | tf_op jit(solution)/shard_map/score_rows/pallas_call | solution.py:120
  142.9 3.1 %collective-permute-done.15.rest_2_ = f32[1,4608]{1,0:T(1,128)S(1)} collective-permute-done((f32[1,4608]{1,0:T(1,128)}, f32[1,4608]{1,0:T(1,128)S(1)}, u32[]{:S(2)}, u32[]{:S(2)}) %collective-permute-start.15) | collective-permute-done | bytes 18464 | tf_op jit(solution)/shard_map/ppermute | solution.py:391
  146.6 8.7 %weighted_sums.3 = (bf16[256,768]{1,0:T(8,128)(2,1)}, bf16[256,768]{1,0:T(8,128)(2,1)}) custom-call(f32[1,4096]{1,0:T(1,128)} %copy-done.18, f32[1,4096]{1,0:T(1,128)} %get-tuple-element.68.total_ref.rest_0_, f32[1,4608]{1,0:T(1,128)} %copy-done.25, f32[1,4608]{1,0:T(1,128)} %copy-done.24, f32[1,4608]{1,0:T(1,128)} %copy-done.23, ...), custom_call_target="tpu_custom_call" | custom-call | flops 3221225472 | bytes 1048576 | tf_op jit(solution)/shard_map/weighted_sums/pallas_call | solution.py:178
  162.3 6.6 %all-to-all-start.3 = ((bf16[16,16,768]{2,1,0:T(8,128)(2,1)}), bf16[16,16,768]{2,1,0:T(8,128)(2,1)S(1)}, u32[]{:S(2)}, u32[]{:S(2)}) async-start(bf16[16,16,768]{2,1,0:T(8,128)(2,1)} %bitcast.12), calls=%async_computation.3 | async-start | bytes 786432 | tf_op jit(solution)/shard_map/all_to_all | solution.py:402
  168.9 12.2 %similarity.1.rest_0_ = bf16[1,2048,2048]{2,1,0:T(8,128)(2,1)} custom-call(s32[1]{0:T(128)} %bitcast.depth_ref, bf16[32,4,16,896]{3,2,1,0:T(8,128)(2,1)} %bitcast.4.rest_19_.rest_0_, bf16[32,16,768]{2,1,0:T(8,128)(2,1)} %copy-done.11, bf16[32,16,768]{2,1,0:T(8,128)(2,1)} %copy-done.13, bf16[32,16,768]{2,1,0:T(8,128)(2,1)} %copy-done.14, ...), custom_call_target="tpu_custom_call" | custom-call | flops 6442450944 | bytes 1048576 | tf_op jit(solution)/shard_map/similarity/pallas_call | solution.py:358
  183.7 14.9 %all_to_all.26 = bf16[16,16,768]{2,1,0:T(8,128)(2,1)S(1)} all-to-all(bf16[16,16,768]{2,1,0:T(8,128)(2,1)} %combine.3), channel_id=1, replica_groups={{0,8,16,24,32,40,48,56,64,72,80,88,96,104,112,120},{4,12,20,28,36,44,52..., dimensions={0} | all-to-all | bytes 786432 | tf_op jit(solution)/shard_map/all_to_all | solution.py:402
  198.6 2.5 %collective-permute-start.18 = (bf16[256,768]{1,0:T(8,128)(2,1)S(1)}, bf16[256,768]{1,0:T(8,128)(2,1)S(1)}, u32[]{:S(2)}, u32[]{:S(2)}) collective-permute-start(bf16[256,768]{1,0:T(8,128)(2,1)S(1)} %bitcast.35), channel_id=1, source_target_pairs={{0,4},{4,0},{8,12},{12,8},{16,20},{20,16},{24,28},{28,24},{32,36},... | collective-permute-start | bytes 1179656 | tf_op jit(solution)/shard_map/ppermute | solution.py:405
  (145 shorter events, 49.2 us)
Async XLA Ops:
  2.1 46.5 %collective-permute-start = (bf16[512,768]{1,0:T(8,128)(2,1)S(1)}, bf16[512,768]{1,0:T(8,128)(2,1)S(1)}, u32[]{:S(2)}, u32[]{:S(2)}) collective-permute-start(bf16[512,768]{1,0:T(8,128)(2,1)S(1)} %get-tuple-element.85.raw_ref), channel_id=1, source_target_pairs={{0,3},{1,0},{2,1},{3,2},{4,7},{5,4},{6,5},{7,6},{8,11},{9,8},{10,9... | collective-permute-start | bytes 2359304 | tf_op jit(solution)/shard_map/ppermute | solution.py:391
  6.8 23.6 %collective-permute-start.2 = (bf16[512,768]{1,0:T(8,128)(2,1)S(1)}, bf16[512,768]{1,0:T(8,128)(2,1)}, u32[]{:S(2)}, u32[]{:S(2)}) collective-permute-start(bf16[512,768]{1,0:T(8,128)(2,1)S(1)} %get-tuple-element.85.raw_ref), channel_id=1, source_target_pairs={{0,1},{1,2},{2,3},{3,0},{4,5},{5,6},{6,7},{7,4},{8,9},{9,10},{10,1... | collective-permute-start | bytes 2359304 | tf_op jit(solution)/shard_map/ppermute | solution.py:391
  6.8 33.1 %collective-permute-start.1 = (bf16[512,768]{1,0:T(8,128)(2,1)S(1)}, bf16[512,768]{1,0:T(8,128)(2,1)}, u32[]{:S(2)}, u32[]{:S(2)}) collective-permute-start(bf16[512,768]{1,0:T(8,128)(2,1)S(1)} %get-tuple-element.84.raw_ref), channel_id=1, source_target_pairs={{0,3},{1,0},{2,1},{3,2},{4,7},{5,4},{6,5},{7,6},{8,11},{9,8},{10,9... | collective-permute-start | bytes 2359304 | tf_op jit(solution)/shard_map/ppermute | solution.py:391
  9.5 39.8 %collective-permute-start.5 = (bf16[512,768]{1,0:T(8,128)(2,1)S(1)}, bf16[512,768]{1,0:T(8,128)(2,1)}, u32[]{:S(2)}, u32[]{:S(2)}) collective-permute-start(bf16[512,768]{1,0:T(8,128)(2,1)S(1)} %get-tuple-element.84.raw_ref), channel_id=1, source_target_pairs={{0,1},{1,2},{2,3},{3,0},{4,5},{5,6},{6,7},{7,4},{8,9},{9,10},{10,1... | collective-permute-start | bytes 2359304 | tf_op jit(solution)/shard_map/ppermute | solution.py:391
  18.9 54.7 %all-to-all-start = ((bf16[32,64,896]{2,1,0:T(8,128)(2,1)}), bf16[32,64,896]{2,1,0:T(8,128)(2,1)}, u32[]{:S(2)}, u32[]{:S(2)}) async-start(bf16[32,64,896]{2,1,0:T(8,128)(2,1)} %bitcast.34), calls=%async_computation | async-start | bytes 7340032 | tf_op jit(solution)/shard_map/all_to_all | solution.py:396
  30.4 29.5 %collective-permute-start.3 = (bf16[512,768]{1,0:T(8,128)(2,1)}, bf16[512,768]{1,0:T(8,128)(2,1)S(1)}, u32[]{:S(2)}, u32[]{:S(2)}) collective-permute-start(bf16[512,768]{1,0:T(8,128)(2,1)} %collective-permute-done.2.raw_ref.rest_17_.rest_5_), channel_id=1, source_target_pairs={{0,1},{1,2},{2,3},{3,0},{4,5},{5,6},{6,7},{7,4},{8,9},{9,10},{10,1... | collective-permute-start | bytes 2359304 | tf_op jit(solution)/shard_map/ppermute | solution.py:391
  31.2 14.0 %copy-start.3 = (bf16[512,512]{1,0:T(8,128)(2,1)}, bf16[512,512]{1,0:T(8,128)(2,1)S(1)}, u32[]{:S(2)}) copy-start(bf16[512,512]{1,0:T(8,128)(2,1)S(1)} %get-tuple-element.58.rest_4_) | copy-start | bytes 1572868
  31.9 15.9 %copy-start.4 = (bf16[512,512]{1,0:T(8,128)(2,1)}, bf16[512,512]{1,0:T(8,128)(2,1)S(1)}, u32[]{:S(2)}) copy-start(bf16[512,512]{1,0:T(8,128)(2,1)S(1)} %get-tuple-element.59.rest_5_) | copy-start | bytes 1572868
  39.8 20.9 %collective-permute-start.4 = (bf16[512,768]{1,0:T(8,128)(2,1)}, bf16[512,768]{1,0:T(8,128)(2,1)S(1)}, u32[]{:S(2)}, u32[]{:S(2)}) collective-permute-start(bf16[512,768]{1,0:T(8,128)(2,1)} %collective-permute-done.1.raw_ref.rest_14_.rest_2_), channel_id=1, source_target_pairs={{0,3},{1,0},{2,1},{3,2},{4,7},{5,4},{6,5},{7,6},{8,11},{9,8},{10,9... | collective-permute-start | bytes 2359304 | tf_op jit(solution)/shard_map/ppermute | solution.py:391
  62.7 3.1 %collective-permute-start.6 = (f32[1,4096]{1,0:T(1,128)S(1)}, f32[1,4096]{1,0:T(1,128)S(1)}, u32[]{:S(2)}, u32[]{:S(2)}) collective-permute-start(f32[1,4096]{1,0:T(1,128)S(1)} %constant_dynamic-update-slice_fusion.8.rest_0_), channel_id=1, source_target_pairs={{0,3},{1,0},{2,1},{3,2},{4,7},{5,4},{6,5},{7,6},{8,11},{9,8},{10,9... | collective-permute-start | bytes 49160 | tf_op jit(solution)/shard_map/ppermute | solution.py:391
  64.2 4.5 %collective-permute-start.7 = (f32[1,4096]{1,0:T(1,128)S(1)}, f32[1,4096]{1,0:T(1,128)S(1)}, u32[]{:S(2)}, u32[]{:S(2)}) collective-permute-start(f32[1,4096]{1,0:T(1,128)S(1)} %constant_dynamic-update-slice_fusion.8.rest_0_), channel_id=1, source_target_pairs={{0,2},{1,3},{2,0},{3,1},{4,6},{5,7},{6,4},{7,5},{8,10},{9,11},{10,... | collective-permute-start | bytes 49160 | tf_op jit(solution)/shard_map/ppermute | solution.py:391
  64.2 4.5 %collective-permute-start.8 = (f32[1,4096]{1,0:T(1,128)S(1)}, f32[1,4096]{1,0:T(1,128)S(1)}, u32[]{:S(2)}, u32[]{:S(2)}) collective-permute-start(f32[1,4096]{1,0:T(1,128)S(1)} %constant_dynamic-update-slice_fusion.8.rest_0_), channel_id=1, source_target_pairs={{0,1},{1,2},{2,3},{3,0},{4,5},{5,6},{6,7},{7,4},{8,9},{9,10},{10,1... | collective-permute-start | bytes 49160 | tf_op jit(solution)/shard_map/ppermute | solution.py:391
  82.3 5.5 %collective-permute-start.9 = (bf16[256,768]{1,0:T(8,128)(2,1)}, bf16[256,768]{1,0:T(8,128)(2,1)S(1)}, u32[]{:S(2)}, u32[]{:S(2)}) collective-permute-start(bf16[256,768]{1,0:T(8,128)(2,1)} %get-tuple-element.67), channel_id=1, source_target_pairs={{0,4},{4,0},{8,12},{12,8},{16,20},{20,16},{24,28},{28,24},{32,36},... | collective-permute-start | bytes 1179656 | tf_op jit(solution)/shard_map/ppermute | solution.py:405
  84.8 20.9 %collective-permute-start.10 = (bf16[32,16,768]{2,1,0:T(8,128)(2,1)S(1)}, bf16[32,16,768]{2,1,0:T(8,128)(2,1)S(1)}, u32[]{:S(2)}, u32[]{:S(2)}) collective-permute-start(bf16[32,16,768]{2,1,0:T(8,128)(2,1)S(1)} %get-tuple-element.83), channel_id=1, source_target_pairs={{0,1},{1,2},{2,3},{3,0},{4,5},{5,6},{6,7},{7,4},{8,9},{9,10},{10,1... | collective-permute-start | bytes 2359304 | tf_op jit(solution)/shard_map/ppermute | solution.py:391
  84.9 20.8 %collective-permute-start.11 = (bf16[32,16,768]{2,1,0:T(8,128)(2,1)S(1)}, bf16[32,16,768]{2,1,0:T(8,128)(2,1)S(1)}, u32[]{:S(2)}, u32[]{:S(2)}) collective-permute-start(bf16[32,16,768]{2,1,0:T(8,128)(2,1)S(1)} %get-tuple-element.82), channel_id=1, source_target_pairs={{0,3},{1,0},{2,1},{3,2},{4,7},{5,4},{6,5},{7,6},{8,11},{9,8},{10,9... | collective-permute-start | bytes 2359304 | tf_op jit(solution)/shard_map/ppermute | solution.py:391
  109.4 13.8 %all-to-all-start.2 = ((bf16[16,16,768]{2,1,0:T(8,128)(2,1)}), bf16[16,16,768]{2,1,0:T(8,128)(2,1)S(1)}, u32[]{:S(2)}, u32[]{:S(2)}) async-start(bf16[16,16,768]{2,1,0:T(8,128)(2,1)} %combine.2), calls=%async_computation.2 | async-start | bytes 786432 | tf_op jit(solution)/shard_map/all_to_all | solution.py:402
  116.4 21.4 %collective-permute-start.13 = (bf16[32,16,768]{2,1,0:T(8,128)(2,1)S(1)}, bf16[32,16,768]{2,1,0:T(8,128)(2,1)S(1)}, u32[]{:S(2)}, u32[]{:S(2)}) collective-permute-start(bf16[32,16,768]{2,1,0:T(8,128)(2,1)S(1)} %fusion.2), channel_id=1, source_target_pairs={{0,2},{1,3},{2,0},{3,1},{4,6},{5,7},{6,4},{7,5},{8,10},{9,11},{10,... | collective-permute-start | bytes 2359304 | tf_op jit(solution)/shard_map/ppermute | solution.py:391
  123.2 5.1 %collective-permute-start.12 = (bf16[256,768]{1,0:T(8,128)(2,1)S(1)}, bf16[256,768]{1,0:T(8,128)(2,1)S(1)}, u32[]{:S(2)}, u32[]{:S(2)}) collective-permute-start(bf16[256,768]{1,0:T(8,128)(2,1)S(1)} %bitcast.38), channel_id=1, source_target_pairs={{0,4},{4,0},{8,12},{12,8},{16,20},{20,16},{24,28},{28,24},{32,36},... | collective-permute-start | bytes 1179656 | tf_op jit(solution)/shard_map/ppermute | solution.py:405
  140.1 2.8 %collective-permute-start.14 = (f32[1,4608]{1,0:T(1,128)}, f32[1,4608]{1,0:T(1,128)S(1)}, u32[]{:S(2)}, u32[]{:S(2)}) collective-permute-start(f32[1,4608]{1,0:T(1,128)} %get-tuple-element.69), channel_id=1, source_target_pairs={{0,3},{1,0},{2,1},{3,2},{4,7},{5,4},{6,5},{7,6},{8,11},{9,8},{10,9... | collective-permute-start | bytes 55304 | tf_op jit(solution)/shard_map/ppermute | solution.py:391
  141.7 4.3 %collective-permute-start.15 = (f32[1,4608]{1,0:T(1,128)}, f32[1,4608]{1,0:T(1,128)S(1)}, u32[]{:S(2)}, u32[]{:S(2)}) collective-permute-start(f32[1,4608]{1,0:T(1,128)} %get-tuple-element.70), channel_id=1, source_target_pairs={{0,2},{1,3},{2,0},{3,1},{4,6},{5,7},{6,4},{7,5},{8,10},{9,11},{10,... | collective-permute-start | bytes 55304 | tf_op jit(solution)/shard_map/ppermute | solution.py:391
  141.7 4.3 %collective-permute-start.16 = (f32[1,4608]{1,0:T(1,128)}, f32[1,4608]{1,0:T(1,128)S(1)}, u32[]{:S(2)}, u32[]{:S(2)}) collective-permute-start(f32[1,4608]{1,0:T(1,128)} %get-tuple-element.71), channel_id=1, source_target_pairs={{0,1},{1,2},{2,3},{3,0},{4,5},{5,6},{6,7},{7,4},{8,9},{9,10},{10,1... | collective-permute-start | bytes 55304 | tf_op jit(solution)/shard_map/ppermute | solution.py:391
  155.3 5.1 %collective-permute-start.17 = (bf16[256,768]{1,0:T(8,128)(2,1)}, bf16[256,768]{1,0:T(8,128)(2,1)S(1)}, u32[]{:S(2)}, u32[]{:S(2)}) collective-permute-start(bf16[256,768]{1,0:T(8,128)(2,1)} %get-tuple-element.81), channel_id=1, source_target_pairs={{0,4},{4,0},{8,12},{12,8},{16,20},{20,16},{24,28},{28,24},{32,36},... | collective-permute-start | bytes 1179656 | tf_op jit(solution)/shard_map/ppermute | solution.py:405
  162.3 18.8 %all-to-all-start.3 = ((bf16[16,16,768]{2,1,0:T(8,128)(2,1)}), bf16[16,16,768]{2,1,0:T(8,128)(2,1)S(1)}, u32[]{:S(2)}, u32[]{:S(2)}) async-start(bf16[16,16,768]{2,1,0:T(8,128)(2,1)} %bitcast.12), calls=%async_computation.3 | async-start | bytes 786432 | tf_op jit(solution)/shard_map/all_to_all | solution.py:402
  198.6 3.9 %collective-permute-start.18 = (bf16[256,768]{1,0:T(8,128)(2,1)S(1)}, bf16[256,768]{1,0:T(8,128)(2,1)S(1)}, u32[]{:S(2)}, u32[]{:S(2)}) collective-permute-start(bf16[256,768]{1,0:T(8,128)(2,1)S(1)} %bitcast.35), channel_id=1, source_target_pairs={{0,4},{4,0},{8,12},{12,8},{16,20},{20,16},{24,28},{28,24},{32,36},... | collective-permute-start | bytes 1179656 | tf_op jit(solution)/shard_map/ppermute | solution.py:405
  (25 other events, 85.2 us)

commit v3 on v2

--- a/solution.py
+++ b/solution.py
@@ -16,13 +16,14 @@
 MIB = 1024 * 1024
 LABEL_LANES = 128
 NEAR_COST = 1_000_000
+OWN_COST = 6_000_000_000
 FAR_COST = 25_000_000_000
 FULL = 61
 
 
 def unit(matrix):
     wide = matrix.astype(jnp.float32)
-    return wide / jnp.sqrt(jnp.sum(wide * wide, axis=-1, keepdims=True) + epsilon)
+    return wide * (1.0 / jnp.sqrt(jnp.sum(wide * wide, axis=-1, keepdims=True) + epsilon))
 
 
 def normalize_rows(matrix):
@@ -59,15 +60,19 @@
     return membership.astype(jnp.bfloat16), jnp.sum(membership, axis=0, keepdims=True)
 
 
-def piece_kernel(raw_ref, block_ref, member_ref, total_ref, scale_ref):
+def piece_kernel(raw_ref, block_ref, *rest):
+    *member_refs, total_ref, scale_ref = rest
     wide = raw_ref[...].astype(jnp.float32)
     squares = jnp.sum(wide * wide, axis=-1, keepdims=True) + epsilon
     scale = (1.0 / jnp.sqrt(jnp.broadcast_to(squares, (squares.shape[0], 8)))).T[:1]
     scale_ref[...] = scale
-    member_ref[...], total_ref[...] = membership_of(block_ref[...], raw_ref[...], scale)
-
-
-def score_piece(raw, block, cost):
+    size = raw_ref.shape[0] // len(member_refs)
+    for i, member_ref in enumerate(member_refs):
+        at = slice(i * size, (i + 1) * size)
+        member_ref[...], total_ref[:, at] = membership_of(block_ref[...], raw_ref[at], scale[:, at])
+
+
+def score_piece(raw, block, pieces, cost):
     size, width = raw.shape
     count = block.shape[0]
     line = jax.ShapeDtypeStruct((1, size), jnp.float32)
@@ -77,8 +82,8 @@
         12,
         cost,
         in_specs=[whole(), whole()],
-        out_specs=[whole()] * 3,
-        out_shape=[jax.ShapeDtypeStruct((count, size), jnp.bfloat16), line, line],
+        out_specs=[whole()] * (pieces + 2),
+        out_shape=[jax.ShapeDtypeStruct((count, size // pieces), jnp.bfloat16)] * pieces + [line] * 2,
     )(raw, block)
 
 
@@ -121,7 +126,7 @@
         functools.partial(score_kernel, pieces),
         "score_rows",
         FULL,
-        2 * pieces * size * width * count,
+        NEAR_COST,
         in_specs=[whole()] * 3 + [in_hbm()] * len(sources),
         out_specs=[in_hbm()] * pieces + [whole()],
         out_shape=[jax.ShapeDtypeStruct((count, size), jnp.bfloat16)] * pieces
@@ -137,11 +142,11 @@
     return out[:pieces], out[pieces]
 
 
-def sum_kernel(pieces, depth, scale_ref, *rest):
+def sum_kernel(pieces, depth, core_ref, scale_ref, *rest):
     total_refs, rest = rest[:depth], rest[depth:]
     member_refs, sources = rest[:pieces], rest[pieces : 2 * pieces - 1]
-    own_ref, other_ref, members, taken, running, member_sem, row_sem = rest[-7:]
-    half = own_ref.shape[0]
+    sums_ref, members, taken, running, member_sem, row_sem = rest[-6:]
+    half = running.shape[0] // 2
     size = sources[1].shape[0]
     arriving = [
         (rows, pltpu.make_async_copy(member_refs[i], members.at[i], member_sem.at[i]))
@@ -166,25 +171,27 @@
             running[...] = product
         else:
             running[...] += product
-    own_ref[...] = running[:half].astype(jnp.bfloat16)
-    other_ref[...] = running[half:].astype(jnp.bfloat16)
-
-
-def weighted_sums(members, sources, scale, totals, after):
+    own, other = running[:half].astype(jnp.bfloat16), running[half:].astype(jnp.bfloat16)
+    chips, _, share, width = sums_ref.shape
+    sums_ref[:, core_ref[0]] = own.reshape(chips, share, width)
+    sums_ref[:, 1 - core_ref[0]] = other.reshape(chips, share, width)
+
+
+def weighted_sums(members, sources, scale, totals, core, chips, after):
     pieces = len(members)
     count, size = members[0].shape
     width = sources[0].shape[1]
-    sums = jax.ShapeDtypeStruct((count // 2, width), jnp.bfloat16)
     return call(
         functools.partial(sum_kernel, pieces, len(totals)),
         "weighted_sums",
         FULL,
         2 * pieces * size * width * count,
-        in_specs=[whole()] * (1 + len(totals))
+        in_specs=[pl.BlockSpec(memory_space=pltpu.SMEM)]
+        + [whole()] * (1 + len(totals))
         + [in_hbm()] * (2 * pieces - 1)
         + [in_hbm()] * len(after),
-        out_specs=[whole()] * 2,
-        out_shape=[sums] * 2,
+        out_specs=whole(),
+        out_shape=jax.ShapeDtypeStruct((chips, 2, count // 2 // chips, width), jnp.bfloat16),
         scratch_shapes=[
             pltpu.VMEM((pieces, count, size), jnp.bfloat16),
             pltpu.VMEM((pieces * size, width), jnp.bfloat16),
@@ -192,34 +199,50 @@
             pltpu.SemaphoreType.DMA((pieces,)),
             pltpu.SemaphoreType.DMA((pieces,)),
         ],
-    )(scale, *totals, *members, *sources, *after)
+    )(core.reshape(1).astype(jnp.int32), scale, *totals, *members, *sources, *after)
 
 
 def combine_kernel(arrived_ref, *rest):
     spread_ref = rest[-1]
-    planes = arrived_ref.shape[0]
     total = arrived_ref[0].astype(jnp.float32)
-    for i in range(1, planes):
+    for i in range(1, arrived_ref.shape[0]):
         total = total + arrived_ref[i].astype(jnp.float32)
     share = normalize_rows(total)
-    for i in range(planes):
+    for i in range(spread_ref.shape[0]):
         spread_ref[i] = share
 
 
-def combine(arrived, after):
+def combine(arrived, receivers, after):
     return call(
         combine_kernel,
         "combine",
-        FULL,
+        8,
         2 * arrived.size,
-        in_specs=[whole()] + [pl.BlockSpec(memory_space=pl.ANY)] * len(after),
+        in_specs=[whole()] + [in_hbm()] * len(after),
         out_specs=whole(),
-        out_shape=jax.ShapeDtypeStruct(arrived.shape, arrived.dtype),
+        out_shape=jax.ShapeDtypeStruct((receivers,) + arrived.shape[1:], arrived.dtype),
     )(arrived, *after)
 
 
-def column_of(row):
-    return jnp.broadcast_to(row, (8, row.shape[1])).T[:, :1]
+def finish_kernel(core_ref, own_ref, other_ref, out_ref):
+    half, width = own_ref.shape
+    core = core_ref[0]
+    for side, ref in ((core, own_ref), (1 - core, other_ref)):
+        at = pl.ds(pl.multiple_of(side * half, half), half)
+        out_ref[at] = ref[...].astype(jnp.float32) * math.sqrt(width)
+
+
+def finish(own_half, other_half, core):
+    half, width = own_half.shape
+    return call(
+        finish_kernel,
+        "finish",
+        8,
+        own_half.size,
+        in_specs=[pl.BlockSpec(memory_space=pltpu.SMEM), whole(), whole()],
+        out_specs=whole(),
+        out_shape=jax.ShapeDtypeStruct((2 * half, width), jnp.float32),
+    )(core.reshape(1).astype(jnp.int32), own_half, other_half)
 
 
 def pack_kernel(devices, cent_count, capacity, depth_ref, raw_ref, assign_ref, table_ref, out_ref, rows, place):
@@ -242,24 +265,30 @@
         low_hits = lax.broadcasted_iota(jnp.int32, (low_count, local_rows), 0) == low
         owner = jnp.sum(jnp.where(low_hits, by_low, 0.0), axis=0, keepdims=True).astype(jnp.int32)
         owner_hits = lax.broadcasted_iota(jnp.int32, (devices, local_rows), 0) == owner
-        earlier = lax.broadcasted_iota(jnp.int32, (local_rows, local_rows), 0) < (
-            lax.broadcasted_iota(jnp.int32, (local_rows, local_rows), 1)
+        group = min(128, local_rows)
+        earlier = lax.broadcasted_iota(jnp.int32, (group, group), 0) < (
+            lax.broadcasted_iota(jnp.int32, (group, group), 1)
         )
-        before = jnp.dot(
-            jnp.where(owner_hits, 1.0, 0.0).astype(jnp.bfloat16),
-            jnp.where(earlier, 1.0, 0.0).astype(jnp.bfloat16),
-            preferred_element_type=jnp.float32,
-        )
+        earlier = jnp.where(earlier, 1.0, 0.0).astype(jnp.bfloat16)
+        ones = jnp.where(owner_hits, 1.0, 0.0)
+        before, seen = [], jnp.zeros((devices, 1), jnp.float32)
+        for at in range(0, local_rows, group):
+            some = ones[:, at : at + group]
+            before.append(
+                jnp.dot(some.astype(jnp.bfloat16), earlier, preferred_element_type=jnp.float32) + seen
+            )
+            seen = seen + jnp.sum(some, axis=1, keepdims=True)
+        before = jnp.concatenate(before, axis=1)
         slot = jnp.sum(jnp.where(owner_hits, before, 0.0), axis=0, keepdims=True).astype(jnp.int32)
         owner_dp, owner_depth = lax.div(owner, cent_count), lax.rem(owner, cent_count)
         distance = lax.rem(owner_depth + cent_count - depth_ref[0], cent_count)
         place[...] = (owner_dp * cent_count + distance) * capacity + slot
-        number = column_of((cluster + 1).astype(jnp.float32)).astype(jnp.int32)
-        lane = lax.broadcasted_iota(jnp.int32, (local_rows, LABEL_LANES), 1)
+        number = cluster + 1
+        lane = lax.broadcasted_iota(jnp.int32, (LABEL_LANES, local_rows), 0)
         digits = jnp.where(
             lane == 0, lax.div(number, 256), jnp.where(lane == 1, lax.rem(number, 256), 0)
         )
-        rows[:, width:] = digits.astype(jnp.float32).astype(jnp.bfloat16)
+        rows[:, width:] = digits.astype(jnp.float32).T.astype(jnp.bfloat16)
 
     size = out_ref.shape[0]
     taken = lax.broadcasted_iota(jnp.int32, (size, local_rows), 0) + step * size == place[...]
@@ -293,54 +322,72 @@
     )
 
 
-def join_kernel(cent_count, total_ref, label_ref, *rest):
-    out_refs = rest[-(cent_count - 1) :]
-    group_rows = total_ref.shape[1]
-    for k in range(1, cent_count):
-        out_refs[k - 1][:, :group_rows] = total_ref[...]
-        out_refs[k - 1][:, group_rows:] = label_ref[cent_count - k : cent_count - k + 1]
-
-
-def join(totals, label, after):
-    cent_count, labels = label.shape
-    joined = jax.ShapeDtypeStruct((1, totals.shape[1] + labels), jnp.float32)
-    return call(
-        functools.partial(join_kernel, cent_count),
-        "join",
+def order_kernel(*refs):
+    del refs
+
+
+def order(value, after):
+    return call(
+        order_kernel,
+        "order",
         FULL,
-        totals.size,
-        in_specs=[whole()] * 2 + [in_hbm()] * len(after),
-        out_specs=[whole()] * (cent_count - 1),
-        out_shape=[joined] * (cent_count - 1),
-    )(totals, label, *after)
-
-
-def similarity_kernel(cent_count, depth_ref, *rest):
+        1,
+        in_specs=[in_hbm()] * (1 + len(after)),
+        out_specs=in_hbm(),
+        out_shape=jax.ShapeDtypeStruct(value.shape, value.dtype),
+        input_output_aliases={0: 0},
+    )(value, *after)
+
+
+def hold_kernel(value_ref, *rest):
+    rest[-1][...] = value_ref[...]
+
+
+def hold(value, after):
+    return call(
+        hold_kernel,
+        "hold",
+        8,
+        value.size,
+        in_specs=[whole()] + [in_hbm()] * len(after),
+        out_specs=whole(),
+        out_shape=jax.ShapeDtypeStruct(value.shape, value.dtype),
+    )(value, *after)
+
+
+def similarity_kernel(cent_count, first, depth_ref, *rest):
     block_refs = rest[:cent_count]
-    row_ref, out_ref, gathered, column, sem = rest[cent_count:]
+    out_ref, flag_ref, gathered, column, row, sem = rest[-6:]
     step = pl.program_id(0)
+    dp_count, _, capacity, lanes = gathered.shape
+    size, slots = out_ref.shape[1:]
+    width = lanes - LABEL_LANES
 
     @pl.when(step == 0)
     def _():
         arriving = []
         for k in range(cent_count):
             source = lax.rem(depth_ref[0] + cent_count - k, cent_count)
-            block = block_refs[k].at[:, 0, :, pl.ds(0, gathered.shape[-1])] if k == 0 else block_refs[k]
+            block = block_refs[k].at[:, 0] if k == 0 else block_refs[k]
             arriving.append(pltpu.make_async_copy(block, gathered.at[:, source], sem.at[k]))
             arriving[-1].start()
-        row = row_ref[...]
-        column[...] = column_of(jnp.where(row > 0.0, row, -1.0))
         for copy in arriving:
             copy.wait()
-
-    size = out_ref.shape[1]
-    slots, width = out_ref.shape[2], gathered.shape[-1]
-    per_step = size // (gathered.shape[1] * gathered.shape[2])
-    rows = gathered[pl.ds(step * per_step, per_step)].reshape(size, width)
-    inner = contract_final_axis(rows, gathered[...].reshape(slots, width))
-    start = pl.multiple_of(step * size, size)
-    same = column[pl.ds(start, size)] == row_ref[...]
-    out_ref[0] = jnp.where(same, inner * math.sqrt(width), 0.0).astype(jnp.bfloat16)
+        digits = gathered[:, :, :, width:].reshape(slots, LABEL_LANES).astype(jnp.float32)
+        number = digits[:, 0:1] * 256.0 + digits[:, 1:2]
+        column[...] = jnp.where(number > 0.0, number, -1.0)
+        across = digits.T
+        row[...] = across[0:1] * 256.0 + across[1:2]
+        flag_ref[...] = jnp.zeros_like(flag_ref)
+
+    per_step = size // (cent_count * capacity)
+    start = pl.multiple_of((first + step) * size, size)
+    rows = gathered[pl.ds((first + step) * per_step, per_step), :, :, :width].reshape(size, width)
+    every = gathered[:, :, :, :width].reshape(slots, width)
+    same = column[pl.ds(start, size)] == row[...]
+    out_ref[0] = jnp.where(
+        same, contract_final_axis(rows, every) * math.sqrt(width), 0.0
+    ).astype(jnp.bfloat16)
     main_diagonal = lax.broadcasted_iota(jnp.int32, (size, size), 0) == (
         lax.broadcasted_iota(jnp.int32, (size, size), 1)
     )
@@ -350,28 +397,36 @@
     ).astype(jnp.bfloat16)
 
 
-def similarity_of(blocks, label, depth):
+def similarity_of(blocks, depth, part, parts, held):
     cent_count = len(blocks)
-    dp_count, capacity, width = blocks[1].shape
+    dp_count, capacity, lanes = blocks[1].shape
     slots = cent_count * dp_count * capacity
-    tile = min(256, slots)
-    return call(
-        functools.partial(similarity_kernel, cent_count),
+    tile = min(256, slots // parts)
+    steps = slots // tile // parts
+    aliased = [] if held is None else [held]
+    return call(
+        functools.partial(similarity_kernel, cent_count, part * steps),
         "similarity",
         FULL,
-        2 * slots * slots * width,
-        grid=(slots // tile,),
-        in_specs=[pl.BlockSpec(memory_space=pltpu.SMEM)]
-        + [in_hbm()] * cent_count
-        + [pl.BlockSpec((1, slots), lambda i: (0, 0))],
-        out_specs=pl.BlockSpec((1, tile, slots), lambda i: (0, i, 0)),
-        out_shape=jax.ShapeDtypeStruct((1, slots, slots), jnp.bfloat16),
+        2 * slots * slots * lanes // parts,
+        grid=(steps,),
+        in_specs=[pl.BlockSpec(memory_space=pltpu.SMEM)] + [in_hbm()] * (cent_count + len(aliased)),
+        out_specs=[
+            pl.BlockSpec((1, tile, slots), lambda i: (0, part * steps + i, 0)),
+            pl.BlockSpec((8, 128), lambda i: (0, 0)),
+        ],
+        out_shape=[
+            jax.ShapeDtypeStruct((1, slots, slots), jnp.bfloat16),
+            jax.ShapeDtypeStruct((8, 128), jnp.float32),
+        ],
         scratch_shapes=[
-            pltpu.VMEM((dp_count, cent_count, capacity, width), jnp.bfloat16),
+            pltpu.VMEM((dp_count, cent_count, capacity, lanes), jnp.bfloat16),
             pltpu.VMEM((slots, 1), jnp.float32),
+            pltpu.VMEM((1, slots), jnp.float32),
             pltpu.SemaphoreType.DMA((cent_count,)),
         ],
-    )(depth.reshape(1).astype(jnp.int32), *blocks, label)
+        input_output_aliases={1 + cent_count: 0} if aliased else {},
+    )(depth.reshape(1).astype(jnp.int32), *blocks, *aliased)
 
 
 def shards(embeddings, init_centroids, assign, owner_map):
@@ -416,56 +471,36 @@
     routed = exchange(packed.reshape(dp_count, cent_count * capacity, -1)).reshape(
         dp_count, cent_count, capacity, -1
     )
-    digits = routed[..., feature_width : feature_width + 2].astype(jnp.float32)
-    routed_label = (
-        (digits[..., 0] * 256.0 + digits[..., 1])
-        .transpose(1, 0, 2)
-        .reshape(cent_count, dp_count * capacity)
-    )
-
     initial = normalize_rows(init_centroids)
     own_half = lax.dynamic_slice_in_dim(initial, core * half, half, 0)
     other_half = lax.dynamic_slice_in_dim(initial, (1 - core) * half, half, 0)
     block = jnp.concatenate([own_half, other_half])
-    scored = [
-        score_piece(piece, block, FAR_COST if piece is far_first or piece is far_second else NEAR_COST)
-        for piece in [first, second] + received
+    scored = [score_piece(embeddings, block, 2, OWN_COST)] + [
+        score_piece(piece, block, 1, FAR_COST if piece is far_first or piece is far_second else NEAR_COST)
+        for piece in received
     ]
-    members = [member for member, _, _ in scored]
-    partial_total = jnp.concatenate([total for _, total, _ in scored], axis=1)
-    scale = jnp.concatenate([scale for _, _, scale in scored], axis=1)
-
-    def reduced(members, totals, after):
-        own, for_sibling = weighted_sums(members, sources, scale, totals, after)
-        both = own.astype(jnp.float32) + swap_cores(for_sibling).astype(jnp.float32)
-        return exchange_plane(both.astype(jnp.bfloat16).reshape(planes, share, feature_width))
+    members = [member for *parts, _, _ in scored for member in parts]
+    partial_total = jnp.concatenate([total for *_, total, _ in scored], axis=1)
+    scale = jnp.concatenate([scale for *_, scale in scored], axis=1)
 
     totals = [partial_total] + [send(partial_total, -k) for k in range(1, cent_count)]
-    arrived = reduced(members, totals, [routed])
-
-    parted = [routed[:, k, :, :feature_width] for k in range(cent_count)]
+    parted = [routed[:, k] for k in range(cent_count)]
+    sums = weighted_sums(members, sources, scale, totals, core, planes, parted[1:])
+    arrived = exchange(sums.reshape(dp_count, share, feature_width))
+
     blocks = [routed, send(parted[1], 1), None, send(parted[3], -1)]
-    blocks[2] = send(parted[2] + blocks[1] * 0, 2)
-
-    own_half = exchange_plane(combine(arrived, [blocks[1], blocks[3]])).reshape(half, feature_width)
+    blocks[2] = send(order(parted[2], [blocks[1], blocks[3]]), 2)
+
+    own_half = exchange_plane(combine(arrived, planes, [])).reshape(half, feature_width)
     members, partial_total = score_rows(sources, scale, own_half, swap_cores(own_half))
-    joined = join(partial_total, routed_label, [blocks[2]])
-    totals, label = [partial_total], [routed_label[0].reshape(dp_count, capacity)]
-    for k in range(1, cent_count):
-        got = send(joined[k - 1], -k)
-        totals.append(got)
-        label.append(got[:, group_rows:].reshape(dp_count, capacity))
-    label = jnp.roll(jnp.stack(label, axis=1), depth, axis=1).reshape(1, -1)
-    similarity = similarity_of(blocks, label, depth)
-    arrived = reduced(members, totals, [])
-    own_half = exchange_plane(combine(arrived, [similarity])).reshape(half, feature_width)
-    other_half = swap_cores(own_half)
-    centroids = jnp.where(
-        core == 0,
-        jnp.concatenate([own_half, other_half]),
-        jnp.concatenate([other_half, own_half]),
-    ).astype(jnp.float32) * math.sqrt(feature_width)
-    return (centroids, similarity)
+    totals = [partial_total] + [send(partial_total, -k) for k in range(1, cent_count)]
+    sums = weighted_sums(members, sources, scale, totals, core, planes, [blocks[2]])
+    arrived = exchange(sums.reshape(dp_count, share, feature_width))
+    similarity, upper = similarity_of(blocks, depth, 0, 2, None)
+    spread = combine(arrived, planes, [upper])
+    similarity, lower = similarity_of(blocks, depth, 1, 2, similarity)
+    own_half = hold(exchange_plane(spread).reshape(half, feature_width), [lower])
+    return (finish(own_half, swap_cores(own_half), core), similarity)
 
 
 def solution(mesh):

time: 205 us -> 190 us (0.927)
  blocking collectives: 29.6 us -> 12.2 us
  waiting for transfers between devices: 38 us -> 51.6 us
  other arithmetic: 8.13 us -> 1.07 us
  local copies, waits for them, and re-layouts: 17.7 us -> 14.3 us
    all_to_all x2 -> x1, blocking collectives: 29.6 us -> 12.2 us  [exchange_plane(): lax.all_to_all(value, 'dp', 0, 0, axis_index_groups=same_core, tiled=True)]
    all_to_all x1 -> x3, waiting for transfers between devices: 4.88 us -> 20.5 us  [exchange(): return lax.all_to_all(value, 'dp', 0, 0, tiled=True)]
    all_to_all x1 -> x3, starting transfers between devices: 8.65 us -> 21.5 us  [exchange(): return lax.all_to_all(value, 'dp', 0, 0, tiled=True)]
    all_to_all x2 -> x1, starting transfers between devices: 12.1 us -> 3.55 us  [exchange_plane(): lax.all_to_all(value, 'dp', 0, 0, axis_index_groups=same_core, tiled=True)]
    ppermute x4 -> x2, starting transfers between devices: 7.71 us -> 3.1 us  [swap_cores(): return lax.ppermute(value, 'dp', other_core)]
    all_to_all x2 -> x1, waiting for transfers between devices: 5.56 us -> 1.49 us  [exchange_plane(): lax.all_to_all(value, 'dp', 0, 0, axis_index_groups=same_core, tiled=True)]
    slice x4 -> x0, local copies, waits for them, and re-layouts: 3.11 us -> none  [the longest x3 2.04 us: shards(): label.append(got[:, group_rows:].reshape(dp_count, capacity))]
    pallas_call x5 -> x8, Pallas kernels: 26.1 us -> 26.7 us  [the longest x2 15.4 us: similarity_of(): call(functools.partial(similarity_kernel, cent_count, part * steps), 'sim...]
  transfers between devices with their start and end apart: 22 -> 21, of which waited for: 10 -> 14; matrix products, arithmetic and copies ran while one was open for 6% -> 2% of each run, Pallas kernels for 19% -> 27%
where the time goes in v3:
time: 190 us; the launch traced here: 189 us
  Pallas kernels  61.4 us (32%)
  waiting for transfers between devices  51.6 us (27%)
  starting transfers between devices  47.7 us (25%)
  local copies, waits for them, and re-layouts  14.3 us (8%)
  blocking collectives  12.2 us (6%)
    ppermute x15, waiting for transfers between devices, send(): lax.ppermute(value, 'cent', [(z, (z + step) % cent_count) for z in range(...  26.9 us
    all_to_all x3, starting transfers between devices, exchange(): return lax.all_to_all(value, 'dp', 0, 0, tiled=True)  21.5 us
    all_to_all x3, waiting for transfers between devices, exchange(): return lax.all_to_all(value, 'dp', 0, 0, tiled=True)  20.5 us
    ppermute x15, starting transfers between devices, send(): lax.ppermute(value, 'cent', [(z, (z + step) % cent_count) for z in range(...  19.5 us
    pallas_call x2, Pallas kernels, weighted_sums(): call(functools.partial(sum_kernel, pieces, len(totals)), 'weighted_sums',...  17.5 us
    pallas_call x2, Pallas kernels, similarity_of(): call(functools.partial(similarity_kernel, cent_count, part * steps), 'sim...  15.4 us
    all_to_all x1, blocking collectives, exchange_plane(): lax.all_to_all(value, 'dp', 0, 0, axis_index_groups=same_core, tiled=True)  12.2 us
    unnamed x69, local copies, waits for them, and re-layouts  8.95 us
  transfers between devices with their start and end apart: 21, of which 14 were waited for; matrix products, arithmetic and copies ran while one was open for 2% of the time, Pallas kernels for 27%

profile of v3, /device:TPU:1, one launch (start us, length us, event | category | flops | bytes accessed | tf_op | source)
XLA Modules:
  0.0 189.2 jit_solution(4968077651620637657)
XLA Ops:
  0.6 2.4 %fusion.2 = (bf16[512,768]{1,0:T(8,128)(2,1)}, bf16[512,768]{1,0:T(8,128)(2,1)S(1)}) fusion(bf16[1024,768]{1,0:T(8,128)(2,1)} %rest_12_.3), kind=kLoop, calls=%fused_computation.26 | loop fusion | bytes 3145728 | tf_op jit(solution)/shard_map/slice | solution.py:463
  3.0 2.5 %collective-permute-start.5 = (bf16[512,768]{1,0:T(8,128)(2,1)}, bf16[512,768]{1,0:T(8,128)(2,1)S(1)}, u32[]{:S(2)}, u32[]{:S(2)}) collective-permute-start(bf16[512,768]{1,0:T(8,128)(2,1)} %get-tuple-element.75), channel_id=1, source_target_pairs={{0,1},{1,2},{2,3},{3,0},{4,5},{5,6},{6,7},{7,4},{8,9},{9,10},{10,1... | collective-permute-start | bytes 2359304 | tf_op jit(solution)/shard_map/ppermute | solution.py:446
  7.6 2.7 %collective-permute-start = (bf16[512,768]{1,0:T(8,128)(2,1)S(1)}, bf16[512,768]{1,0:T(8,128)(2,1)}, u32[]{:S(2)}, u32[]{:S(2)}) collective-permute-start(bf16[512,768]{1,0:T(8,128)(2,1)S(1)} %get-tuple-element.76), channel_id=1, source_target_pairs={{0,3},{1,0},{2,1},{3,2},{4,7},{5,4},{6,5},{7,6},{8,11},{9,8},{10,9... | collective-permute-start | bytes 2359304 | tf_op jit(solution)/shard_map/ppermute | solution.py:446
  10.9 8.5 %pack.1 = bf16[2048,896]{1,0:T(8,128)(2,1)} custom-call(s32[1]{0:T(128)} %bitcast.1.depth_ref, bf16[1024,768]{1,0:T(8,128)(2,1)} %rest_12_.3, s32[1,1024]{1,0:T(1,128)} %bitcast.29, f32[16,128]{1,0:T(8,128)} %convert_bitcast_fusion.table_ref), custom_call_target="tpu_custom_call" | custom-call | flops 3221225472 | bytes 1048576 | tf_op jit(solution)/shard_map/pack/pallas_call | solution.py:304
  19.3 8.8 %all-to-all-start = ((bf16[32,64,896]{2,1,0:T(8,128)(2,1)}), bf16[32,64,896]{2,1,0:T(8,128)(2,1)}, u32[]{:S(2)}, u32[]{:S(2)}) async-start(bf16[32,64,896]{2,1,0:T(8,128)(2,1)} %bitcast.24), calls=%async_computation | async-start | bytes 7340032 | tf_op jit(solution)/shard_map/all_to_all | solution.py:451
  28.7 13.3 %collective-permute-done.2.raw_ref.rest_17_.rest_5_ = bf16[512,768]{1,0:T(8,128)(2,1)} collective-permute-done((bf16[512,768]{1,0:T(8,128)(2,1)S(1)}, bf16[512,768]{1,0:T(8,128)(2,1)}, u32[]{:S(2)}, u32[]{:S(2)}) %collective-permute-start.2) | collective-permute-done | bytes 786464 | tf_op jit(solution)/shard_map/ppermute | solution.py:446
  44.8 2.7 %collective-permute-start.4 = (bf16[512,768]{1,0:T(8,128)(2,1)}, bf16[512,768]{1,0:T(8,128)(2,1)S(1)}, u32[]{:S(2)}, u32[]{:S(2)}) collective-permute-start(bf16[512,768]{1,0:T(8,128)(2,1)} %collective-permute-done.1.raw_ref.rest_14_.rest_2_), channel_id=1, source_target_pairs={{0,3},{1,0},{2,1},{3,2},{4,7},{5,4},{6,5},{7,6},{8,11},{9,8},{10,9... | collective-permute-start | bytes 2359304 | tf_op jit(solution)/shard_map/ppermute | solution.py:446
  56.3 5.1 %collective-permute-done.3.raw_ref.rest_15_.rest_3_ = bf16[512,768]{1,0:T(8,128)(2,1)S(1)} collective-permute-done((bf16[512,768]{1,0:T(8,128)(2,1)}, bf16[512,768]{1,0:T(8,128)(2,1)S(1)}, u32[]{:S(2)}, u32[]{:S(2)}) %collective-permute-start.3) | collective-permute-done | bytes 786464 | tf_op jit(solution)/shard_map/ppermute | solution.py:446
  64.9 4.6 %collective-permute-start.7 = (f32[1,4096]{1,0:T(1,128)S(1)}, f32[1,4096]{1,0:T(1,128)S(1)}, u32[]{:S(2)}, u32[]{:S(2)}) collective-permute-start(f32[1,4096]{1,0:T(1,128)S(1)} %constant_dynamic-update-slice_fusion.7.rest_0_), channel_id=1, source_target_pairs={{0,2},{1,3},{2,0},{3,1},{4,6},{5,7},{6,4},{7,5},{8,10},{9,11},{10,... | collective-permute-start | bytes 49160 | tf_op jit(solution)/shard_map/ppermute | solution.py:446
  69.6 4.5 %all-to-all-done = bf16[32,64,896]{2,1,0:T(8,128)(2,1)} async-done(((bf16[32,64,896]{2,1,0:T(8,128)(2,1)}), bf16[32,64,896]{2,1,0:T(8,128)(2,1)}, u32[]{:S(2)}, u32[]{:S(2)}) %all-to-all-start) | async-done | bytes 3670048 | tf_op jit(solution)/shard_map/all_to_all | solution.py:451
  74.1 2.9 %slice_bitcast_fusion = (bf16[32,16,896]{2,1,0:T(8,128)(2,1)S(1)}, bf16[32,16,896]{2,1,0:T(8,128)(2,1)}, bf16[32,16,896]{2,1,0:T(8,128)(2,1)S(1)}) fusion(bf16[32,4,16,896]{3,2,1,0:T(8,128)(2,1)} %bitcast.5.rest_0_), kind=kLoop, calls=%fused_computation.4 | loop fusion | bytes 5505024 | tf_op jit(solution)/shard_map/squeeze | solution.py:487
  79.2 8.7 %weighted_sums.2 = bf16[16,2,16,768]{3,2,1,0:T(8,128)(2,1)} custom-call(s32[1]{0:T(128)} %bitcast.core_ref, f32[1,4096]{1,0:T(1,128)} %copy-done.20, f32[1,4096]{1,0:T(1,128)} %copy-done.21, f32[1,4096]{1,0:T(1,128)} %copy-done.24, f32[1,4096]{1,0:T(1,128)} %copy-done.23, f32[1,4096]{1,0:T(1,128)} %copy-done.22, bf16[512,512]{1,0:T(8,128)(2,1)} %copy-done.4, ...), custom_call_target="tpu_custom_call" | custom-call | flops 3221225472 | bytes 1048576 | tf_op jit(solution)/shard_map/weighted_sums/pallas_call | solution.py:184
  87.9 7.3 %all-to-all-start.1 = ((bf16[32,16,768]{2,1,0:T(8,128)(2,1)}), bf16[32,16,768]{2,1,0:T(8,128)(2,1)S(1)}, u32[]{:S(2)}, u32[]{:S(2)}) async-start(bf16[32,16,768]{2,1,0:T(8,128)(2,1)} %bitcast.25), calls=%async_computation.1 | async-start | bytes 1572864 | tf_op jit(solution)/shard_map/all_to_all | solution.py:451
  95.2 2.9 %collective-permute-done.14.refs_2_.rest_3_ = bf16[32,16,896]{2,1,0:T(8,128)(2,1)} collective-permute-done((bf16[32,16,896]{2,1,0:T(8,128)(2,1)S(1)}, bf16[32,16,896]{2,1,0:T(8,128)(2,1)}, u32[]{:S(2)}, u32[]{:S(2)}) %collective-permute-start.14) | collective-permute-done | bytes 917536 | tf_op jit(solution)/shard_map/ppermute | solution.py:446
  100.0 9.5 %all-to-all-done.1.arrived_ref = bf16[32,16,768]{2,1,0:T(8,128)(2,1)S(1)} async-done(((bf16[32,16,768]{2,1,0:T(8,128)(2,1)}), bf16[32,16,768]{2,1,0:T(8,128)(2,1)S(1)}, u32[]{:S(2)}, u32[]{:S(2)}) %all-to-all-start.1) | async-done | bytes 786464 | tf_op jit(solution)/shard_map/all_to_all | solution.py:451
  109.7 12.2 %all_to_all.25 = bf16[16,16,768]{2,1,0:T(8,128)(2,1)S(1)} all-to-all(bf16[16,16,768]{2,1,0:T(8,128)(2,1)S(1)} %combine.2), channel_id=1, replica_groups={{0,8,16,24,32,40,48,56,64,72,80,88,96,104,112,120},{4,12,20,28,36,44,52..., dimensions={0} | all-to-all | bytes 786432 | tf_op jit(solution)/shard_map/all_to_all | solution.py:457
  125.5 8.8 %score_rows.1 = (bf16[512,512]{1,0:T(8,128)(2,1)}, bf16[512,512]{1,0:T(8,128)(2,1)}, bf16[512,512]{1,0:T(8,128)(2,1)}, bf16[512,512]{1,0:T(8,128)(2,1)}, bf16[51...) custom-call(f32[1,4096]{1,0:T(1,128)} %copy-done.20, ...), custom_call_target="tpu_custom_call" | custom-call | flops 1000000 | bytes 1048576 | tf_op jit(solution)/shard_map/score_rows/pallas_call | solution.py:125
  134.8 2.5 %collective-permute-start.11 = (f32[1,4096]{1,0:T(1,128)}, f32[1,4096]{1,0:T(1,128)S(1)}, u32[]{:S(2)}, u32[]{:S(2)}) collective-permute-start(f32[1,4096]{1,0:T(1,128)} %get-tuple-element.59.rest_0_), channel_id=1, source_target_pairs={{0,2},{1,3},{2,0},{3,1},{4,6},{5,7},{6,4},{7,5},{8,10},{9,11},{10,... | collective-permute-start | bytes 49160 | tf_op jit(solution)/shard_map/ppermute | solution.py:446
  141.4 8.8 %weighted_sums.3 = bf16[16,2,16,768]{3,2,1,0:T(8,128)(2,1)} custom-call(s32[1]{0:T(128)} %bitcast.core_ref, f32[1,4096]{1,0:T(1,128)} %copy-done.20, f32[1,4096]{1,0:T(1,128)} %get-tuple-element.59.rest_0_, f32[1,4096]{1,0:T(1,128)} %copy-done.27, f32[1,4096]{1,0:T(1,128)} %copy-done.26, f32[1,4096]{1,0:T(1,128)} %copy-done.25, ...), custom_call_target="tpu_custom_call" | custom-call | flops 3221225472 | bytes 1048576 | tf_op jit(solution)/shard_map/weighted_sums/pallas_call | solution.py:184
  150.2 5.4 %all-to-all-start.3 = ((bf16[32,16,768]{2,1,0:T(8,128)(2,1)}), bf16[32,16,768]{2,1,0:T(8,128)(2,1)S(1)}, u32[]{:S(2)}, u32[]{:S(2)}) async-start(bf16[32,16,768]{2,1,0:T(8,128)(2,1)} %bitcast.26), calls=%async_computation.3 | async-start | bytes 1572864 | tf_op jit(solution)/shard_map/all_to_all | solution.py:451
  155.7 7.7 %similarity.2 = (bf16[1,2048,2048]{2,1,0:T(8,128)(2,1)}, f32[8,128]{1,0:T(8,128)}) custom-call(s32[1]{0:T(128)} %bitcast.1.depth_ref, bf16[32,4,16,896]{3,2,1,0:T(8,128)(2,1)} %bitcast.5.rest_0_, bf16[32,16,896]{2,1,0:T(8,128)(2,1)} %collective-permute-done.13.refs_1_.rest_1_, bf16[32,16,896]{2,1,0:T(8,128)(2,1)} %copy-done.14, ...), custom_call_target="tpu_custom_call" | custom-call | flops 3758096384 | bytes 1048576 | tf_op jit(solution)/shard_map/similarity/pallas_call | solution.py:407
  163.4 6.5 %all-to-all-done.3.arrived_ref = bf16[32,16,768]{2,1,0:T(8,128)(2,1)S(1)} async-done(((bf16[32,16,768]{2,1,0:T(8,128)(2,1)}), bf16[32,16,768]{2,1,0:T(8,128)(2,1)S(1)}, u32[]{:S(2)}, u32[]{:S(2)}) %all-to-all-start.3) | async-done | bytes 786464 | tf_op jit(solution)/shard_map/all_to_all | solution.py:451
  171.6 3.6 %all-to-all-start.4 = ((bf16[16,16,768]{2,1,0:T(8,128)(2,1)}), bf16[16,16,768]{2,1,0:T(8,128)(2,1)S(1)}, u32[]{:S(2)}, u32[]{:S(2)}) async-start(bf16[16,16,768]{2,1,0:T(8,128)(2,1)} %combine.3), calls=%async_computation.4 | async-start | bytes 786432 | tf_op jit(solution)/shard_map/all_to_all | solution.py:457
  175.1 7.7 %similarity.3 = (bf16[1,2048,2048]{2,1,0:T(8,128)(2,1)}, f32[8,128]{1,0:T(8,128)}) custom-call(s32[1]{0:T(128)} %bitcast.1.depth_ref, bf16[32,4,16,896]{3,2,1,0:T(8,128)(2,1)} %bitcast.5.rest_0_, bf16[32,16,896]{2,1,0:T(8,128)(2,1)} %collective-permute-done.13.refs_1_.rest_1_, bf16[32,16,896]{2,1,0:T(8,128)(2,1)} %copy-done.14, ...), custom_call_target="tpu_custom_call", output_to_operand_aliasing={{0}: (5, {})} | custom-call | flops 3758096384 | bytes 1048576 | tf_op jit(solution)/shard_map/similarity/pallas_call | solution.py:407
  (116 shorter events, 38.8 us)
Async XLA Ops:
  0.6 9.6 %copy-start.28 = (s32[2048]{0:T(1024)S(1)}, s32[2048]{0:T(1024)}, u32[]{:S(2)}) copy-start(s32[2048]{0:T(1024)} %param.7) | copy-start | bytes 24580
  3.0 49.8 %collective-permute-start.5 = (bf16[512,768]{1,0:T(8,128)(2,1)}, bf16[512,768]{1,0:T(8,128)(2,1)S(1)}, u32[]{:S(2)}, u32[]{:S(2)}) collective-permute-start(bf16[512,768]{1,0:T(8,128)(2,1)} %get-tuple-element.75), channel_id=1, source_target_pairs={{0,1},{1,2},{2,3},{3,0},{4,5},{5,6},{6,7},{7,4},{8,9},{9,10},{10,1... | collective-permute-start | bytes 2359304 | tf_op jit(solution)/shard_map/ppermute | solution.py:446
  5.5 39.4 %collective-permute-start.1 = (bf16[512,768]{1,0:T(8,128)(2,1)}, bf16[512,768]{1,0:T(8,128)(2,1)}, u32[]{:S(2)}, u32[]{:S(2)}) collective-permute-start(bf16[512,768]{1,0:T(8,128)(2,1)} %get-tuple-element.75), channel_id=1, source_target_pairs={{0,3},{1,0},{2,1},{3,2},{4,7},{5,4},{6,5},{7,6},{8,11},{9,8},{10,9... | collective-permute-start | bytes 2359304 | tf_op jit(solution)/shard_map/ppermute | solution.py:446
  7.6 34.4 %collective-permute-start.2 = (bf16[512,768]{1,0:T(8,128)(2,1)S(1)}, bf16[512,768]{1,0:T(8,128)(2,1)}, u32[]{:S(2)}, u32[]{:S(2)}) collective-permute-start(bf16[512,768]{1,0:T(8,128)(2,1)S(1)} %get-tuple-element.76), channel_id=1, source_target_pairs={{0,1},{1,2},{2,3},{3,0},{4,5},{5,6},{6,7},{7,4},{8,9},{9,10},{10,1... | collective-permute-start | bytes 2359304 | tf_op jit(solution)/shard_map/ppermute | solution.py:446
  7.6 45.9 %collective-permute-start = (bf16[512,768]{1,0:T(8,128)(2,1)S(1)}, bf16[512,768]{1,0:T(8,128)(2,1)}, u32[]{:S(2)}, u32[]{:S(2)}) collective-permute-start(bf16[512,768]{1,0:T(8,128)(2,1)S(1)} %get-tuple-element.76), channel_id=1, source_target_pairs={{0,3},{1,0},{2,1},{3,2},{4,7},{5,4},{6,5},{7,6},{8,11},{9,8},{10,9... | collective-permute-start | bytes 2359304 | tf_op jit(solution)/shard_map/ppermute | solution.py:446
  19.3 54.8 %all-to-all-start = ((bf16[32,64,896]{2,1,0:T(8,128)(2,1)}), bf16[32,64,896]{2,1,0:T(8,128)(2,1)}, u32[]{:S(2)}, u32[]{:S(2)}) async-start(bf16[32,64,896]{2,1,0:T(8,128)(2,1)} %bitcast.24), calls=%async_computation | async-start | bytes 7340032 | tf_op jit(solution)/shard_map/all_to_all | solution.py:451
  28.6 13.4 %copy-start = (bf16[1024,768]{1,0:T(8,128)(2,1)S(1)}, bf16[1024,768]{1,0:T(8,128)(2,1)}, u32[]{:S(2)}) copy-start(bf16[1024,768]{1,0:T(8,128)(2,1)} %rest_12_.3) | copy-start | bytes 4718596
  42.0 19.3 %collective-permute-start.3 = (bf16[512,768]{1,0:T(8,128)(2,1)}, bf16[512,768]{1,0:T(8,128)(2,1)S(1)}, u32[]{:S(2)}, u32[]{:S(2)}) collective-permute-start(bf16[512,768]{1,0:T(8,128)(2,1)} %collective-permute-done.2.raw_ref.rest_17_.rest_5_), channel_id=1, source_target_pairs={{0,1},{1,2},{2,3},{3,0},{4,5},{5,6},{6,7},{7,4},{8,9},{9,10},{10,1... | collective-permute-start | bytes 2359304 | tf_op jit(solution)/shard_map/ppermute | solution.py:446
  44.8 18.3 %collective-permute-start.4 = (bf16[512,768]{1,0:T(8,128)(2,1)}, bf16[512,768]{1,0:T(8,128)(2,1)S(1)}, u32[]{:S(2)}, u32[]{:S(2)}) collective-permute-start(bf16[512,768]{1,0:T(8,128)(2,1)} %collective-permute-done.1.raw_ref.rest_14_.rest_2_), channel_id=1, source_target_pairs={{0,3},{1,0},{2,1},{3,2},{4,7},{5,4},{6,5},{7,6},{8,11},{9,8},{10,9... | collective-permute-start | bytes 2359304 | tf_op jit(solution)/shard_map/ppermute | solution.py:446
  64.9 12.1 %copy-start.21 = (f32[1,4096]{1,0:T(1,128)}, f32[1,4096]{1,0:T(1,128)S(1)}, u32[]{:S(2)}) copy-start(f32[1,4096]{1,0:T(1,128)S(1)} %constant_dynamic-update-slice_fusion.7.rest_0_) | copy-start | bytes 49156
  64.9 13.7 %collective-permute-start.8 = (f32[1,4096]{1,0:T(1,128)S(1)}, f32[1,4096]{1,0:T(1,128)S(1)}, u32[]{:S(2)}, u32[]{:S(2)}) collective-permute-start(f32[1,4096]{1,0:T(1,128)S(1)} %constant_dynamic-update-slice_fusion.7.rest_0_), channel_id=1, source_target_pairs={{0,1},{1,2},{2,3},{3,0},{4,5},{5,6},{6,7},{7,4},{8,9},{9,10},{10,1... | collective-permute-start | bytes 49160 | tf_op jit(solution)/shard_map/ppermute | solution.py:446
  64.9 13.6 %collective-permute-start.7 = (f32[1,4096]{1,0:T(1,128)S(1)}, f32[1,4096]{1,0:T(1,128)S(1)}, u32[]{:S(2)}, u32[]{:S(2)}) collective-permute-start(f32[1,4096]{1,0:T(1,128)S(1)} %constant_dynamic-update-slice_fusion.7.rest_0_), channel_id=1, source_target_pairs={{0,2},{1,3},{2,0},{3,1},{4,6},{5,7},{6,4},{7,5},{8,10},{9,11},{10,... | collective-permute-start | bytes 49160 | tf_op jit(solution)/shard_map/ppermute | solution.py:446
  69.5 9.1 %collective-permute-start.6 = (f32[1,4096]{1,0:T(1,128)S(1)}, f32[1,4096]{1,0:T(1,128)S(1)}, u32[]{:S(2)}, u32[]{:S(2)}) collective-permute-start(f32[1,4096]{1,0:T(1,128)S(1)} %constant_dynamic-update-slice_fusion.7.rest_0_), channel_id=1, source_target_pairs={{0,3},{1,0},{2,1},{3,2},{4,7},{5,4},{6,5},{7,6},{8,11},{9,8},{10,9... | collective-permute-start | bytes 49160 | tf_op jit(solution)/shard_map/ppermute | solution.py:446
  77.0 21.2 %collective-permute-start.14 = (bf16[32,16,896]{2,1,0:T(8,128)(2,1)S(1)}, bf16[32,16,896]{2,1,0:T(8,128)(2,1)}, u32[]{:S(2)}, u32[]{:S(2)}) collective-permute-start(bf16[32,16,896]{2,1,0:T(8,128)(2,1)S(1)} %get-tuple-element.72.rest_21_), channel_id=1, source_target_pairs={{0,3},{1,0},{2,1},{3,2},{4,7},{5,4},{6,5},{7,6},{8,11},{9,8},{10,9... | collective-permute-start | bytes 2752520 | tf_op jit(solution)/shard_map/ppermute | solution.py:446
  77.6 22.0 %collective-permute-start.13 = (bf16[32,16,896]{2,1,0:T(8,128)(2,1)S(1)}, bf16[32,16,896]{2,1,0:T(8,128)(2,1)}, u32[]{:S(2)}, u32[]{:S(2)}) collective-permute-start(bf16[32,16,896]{2,1,0:T(8,128)(2,1)S(1)} %get-tuple-element.74.rest_19_), channel_id=1, source_target_pairs={{0,1},{1,2},{2,3},{3,0},{4,5},{5,6},{6,7},{7,4},{8,9},{9,10},{10,1... | collective-permute-start | bytes 2752520 | tf_op jit(solution)/shard_map/ppermute | solution.py:446
  87.9 21.5 %all-to-all-start.1 = ((bf16[32,16,768]{2,1,0:T(8,128)(2,1)}), bf16[32,16,768]{2,1,0:T(8,128)(2,1)S(1)}, u32[]{:S(2)}, u32[]{:S(2)}) async-start(bf16[32,16,768]{2,1,0:T(8,128)(2,1)} %bitcast.25), calls=%async_computation.1 | async-start | bytes 1572864 | tf_op jit(solution)/shard_map/all_to_all | solution.py:451
  99.6 40.9 %collective-permute-start.15 = (bf16[32,16,896]{2,1,0:T(8,128)(2,1)}, bf16[32,16,896]{2,1,0:T(8,128)(2,1)S(1)}, u32[]{:S(2)}, u32[]{:S(2)}) collective-permute-start(bf16[32,16,896]{2,1,0:T(8,128)(2,1)} %order.1), channel_id=1, source_target_pairs={{0,2},{1,3},{2,0},{3,1},{4,6},{5,7},{6,4},{7,5},{8,10},{9,11},{10,... | collective-permute-start | bytes 2752520 | tf_op jit(solution)/shard_map/ppermute | solution.py:446
  121.9 2.9 %collective-permute-start.9 = (bf16[256,768]{1,0:T(8,128)(2,1)S(1)}, bf16[256,768]{1,0:T(8,128)(2,1)S(1)}, u32[]{:S(2)}, u32[]{:S(2)}) collective-permute-start(bf16[256,768]{1,0:T(8,128)(2,1)S(1)} %bitcast.27), channel_id=1, source_target_pairs={{0,4},{4,0},{8,12},{12,8},{16,20},{20,16},{24,28},{28,24},{32,36},... | collective-permute-start | bytes 1179656 | tf_op jit(solution)/shard_map/ppermute | solution.py:460
  134.3 4.1 %collective-permute-start.12 = (f32[1,4096]{1,0:T(1,128)}, f32[1,4096]{1,0:T(1,128)S(1)}, u32[]{:S(2)}, u32[]{:S(2)}) collective-permute-start(f32[1,4096]{1,0:T(1,128)} %get-tuple-element.59.rest_0_), channel_id=1, source_target_pairs={{0,1},{1,2},{2,3},{3,0},{4,5},{5,6},{6,7},{7,4},{8,9},{9,10},{10,1... | collective-permute-start | bytes 49160 | tf_op jit(solution)/shard_map/ppermute | solution.py:446
  134.8 4.3 %collective-permute-start.11 = (f32[1,4096]{1,0:T(1,128)}, f32[1,4096]{1,0:T(1,128)S(1)}, u32[]{:S(2)}, u32[]{:S(2)}) collective-permute-start(f32[1,4096]{1,0:T(1,128)} %get-tuple-element.59.rest_0_), channel_id=1, source_target_pairs={{0,2},{1,3},{2,0},{3,1},{4,6},{5,7},{6,4},{7,5},{8,10},{9,11},{10,... | collective-permute-start | bytes 49160 | tf_op jit(solution)/shard_map/ppermute | solution.py:446
  137.3 3.2 %collective-permute-start.10 = (f32[1,4096]{1,0:T(1,128)}, f32[1,4096]{1,0:T(1,128)S(1)}, u32[]{:S(2)}, u32[]{:S(2)}) collective-permute-start(f32[1,4096]{1,0:T(1,128)} %get-tuple-element.59.rest_0_), channel_id=1, source_target_pairs={{0,3},{1,0},{2,1},{3,2},{4,7},{5,4},{6,5},{7,6},{8,11},{9,8},{10,9... | collective-permute-start | bytes 49160 | tf_op jit(solution)/shard_map/ppermute | solution.py:446
  150.2 19.7 %all-to-all-start.3 = ((bf16[32,16,768]{2,1,0:T(8,128)(2,1)}), bf16[32,16,768]{2,1,0:T(8,128)(2,1)S(1)}, u32[]{:S(2)}, u32[]{:S(2)}) async-start(bf16[32,16,768]{2,1,0:T(8,128)(2,1)} %bitcast.26), calls=%async_computation.3 | async-start | bytes 1572864 | tf_op jit(solution)/shard_map/all_to_all | solution.py:451
  171.6 12.8 %all-to-all-start.4 = ((bf16[16,16,768]{2,1,0:T(8,128)(2,1)}), bf16[16,16,768]{2,1,0:T(8,128)(2,1)S(1)}, u32[]{:S(2)}, u32[]{:S(2)}) async-start(bf16[16,16,768]{2,1,0:T(8,128)(2,1)} %combine.3), calls=%async_computation.4 | async-start | bytes 786432 | tf_op jit(solution)/shard_map/all_to_all | solution.py:457
  185.1 2.9 %collective-permute-start.16 = (bf16[256,768]{1,0:T(8,128)(2,1)S(1)}, bf16[256,768]{1,0:T(8,128)(2,1)S(1)}, u32[]{:S(2)}, u32[]{:S(2)}) collective-permute-start(bf16[256,768]{1,0:T(8,128)(2,1)S(1)} %hold.1.own_ref), channel_id=1, source_target_pairs={{0,4},{4,0},{8,12},{12,8},{16,20},{20,16},{24,28},{28,24},{32,36},... | collective-permute-start | bytes 1179656 | tf_op jit(solution)/shard_map/ppermute | solution.py:460
  (26 other events, 51.6 us)

commit v4 on v3

--- a/solution.py
+++ b/solution.py
@@ -17,7 +17,7 @@
 LABEL_LANES = 128
 NEAR_COST = 1_000_000
 OWN_COST = 6_000_000_000
-FAR_COST = 25_000_000_000
+FAR_COST = 50_000_000_000
 FULL = 61
 
 
@@ -60,36 +60,41 @@
     return membership.astype(jnp.bfloat16), jnp.sum(membership, axis=0, keepdims=True)
 
 
-def piece_kernel(raw_ref, block_ref, *rest):
-    *member_refs, total_ref, scale_ref = rest
-    wide = raw_ref[...].astype(jnp.float32)
-    squares = jnp.sum(wide * wide, axis=-1, keepdims=True) + epsilon
-    scale = (1.0 / jnp.sqrt(jnp.broadcast_to(squares, (squares.shape[0], 8)))).T[:1]
-    scale_ref[...] = scale
-    size = raw_ref.shape[0] // len(member_refs)
-    for i, member_ref in enumerate(member_refs):
+def piece_kernel(sources, block_ref, *rest):
+    raw_refs, member_refs = rest[:sources], rest[sources:-2]
+    total_ref, scale_ref = rest[-2:]
+    size = member_refs[0].shape[1]
+    parts = [(ref, at) for ref in raw_refs for at in range(0, ref.shape[0], size)]
+    for i, (ref, start) in enumerate(parts):
+        raw = ref[start : start + size]
         at = slice(i * size, (i + 1) * size)
-        member_ref[...], total_ref[:, at] = membership_of(block_ref[...], raw_ref[at], scale[:, at])
-
-
-def score_piece(raw, block, pieces, cost):
-    size, width = raw.shape
+        wide = raw.astype(jnp.float32)
+        squares = jnp.sum(wide * wide, axis=-1, keepdims=True) + epsilon
+        scale = (1.0 / jnp.sqrt(jnp.broadcast_to(squares, (size, 8)))).T[:1]
+        scale_ref[:, at] = scale
+        member_refs[i][...], total_ref[:, at] = membership_of(block_ref[...], raw, scale)
+
+
+def score_piece(raws, block, size, cost):
+    rows = sum(raw.shape[0] for raw in raws)
     count = block.shape[0]
-    line = jax.ShapeDtypeStruct((1, size), jnp.float32)
-    return call(
-        piece_kernel,
+    line = jax.ShapeDtypeStruct((1, rows), jnp.float32)
+    pieces = rows // size
+    return call(
+        functools.partial(piece_kernel, len(raws)),
         "score_piece",
         12,
         cost,
-        in_specs=[whole(), whole()],
+        in_specs=[whole()] * (1 + len(raws)),
         out_specs=[whole()] * (pieces + 2),
-        out_shape=[jax.ShapeDtypeStruct((count, size // pieces), jnp.bfloat16)] * pieces + [line] * 2,
-    )(raw, block)
-
-
-def fetches(sources, taken, sems):
-    size = sources[1].shape[0]
-    parts = [sources[0].at[pl.ds(0, size)], sources[0].at[pl.ds(size, size)]] + list(sources[1:])
+        out_shape=[jax.ShapeDtypeStruct((count, size), jnp.bfloat16)] * pieces + [line] * 2,
+    )(block, *raws)
+
+
+def fetches(sources, size, taken, sems):
+    parts = [
+        source.at[pl.ds(at, size)] for source in sources for at in range(0, source.shape[0], size)
+    ]
     return [
         pltpu.make_async_copy(part, taken.at[pl.ds(i * size, size)], sems.at[i])
         for i, part in enumerate(parts)
@@ -97,12 +102,11 @@
 
 
 def score_kernel(pieces, scale_ref, own_ref, other_ref, *rest):
-    sources, outs = rest[: pieces - 1], rest[pieces - 1 :]
-    member_refs, total_ref = outs[:pieces], outs[pieces]
-    taken, members, block, in_sem, out_sem = outs[pieces + 1 :]
+    *sources, total_ref, taken, members, block, in_sem, out_sem = rest
+    sources, member_refs = sources[:-pieces], sources[-pieces:]
     half = own_ref.shape[0]
-    size = sources[1].shape[0]
-    arriving = fetches(sources, taken, in_sem)
+    size = members.shape[2]
+    arriving = fetches(sources, size, taken, in_sem)
     for copy in arriving:
         copy.start()
     block[:half], block[half:] = own_ref[...], other_ref[...]
@@ -117,9 +121,9 @@
         copy.wait()
 
 
-def score_rows(sources, scale, own_half, other_half):
-    pieces = len(sources) + 1
-    size, width = sources[1].shape
+def score_rows(sources, scale, own_half, other_half, size):
+    pieces = scale.shape[1] // size
+    width = sources[0].shape[1]
     count = 2 * own_half.shape[0]
     each = pltpu.SemaphoreType.DMA((pieces,))
     out = call(
@@ -142,15 +146,15 @@
     return out[:pieces], out[pieces]
 
 
-def sum_kernel(pieces, depth, core_ref, scale_ref, *rest):
+def sum_kernel(pieces, depth, source_count, core_ref, scale_ref, *rest):
     total_refs, rest = rest[:depth], rest[depth:]
-    member_refs, sources = rest[:pieces], rest[pieces : 2 * pieces - 1]
     sums_ref, members, taken, running, member_sem, row_sem = rest[-6:]
+    member_refs, sources = rest[:pieces], rest[pieces : pieces + source_count]
     half = running.shape[0] // 2
-    size = sources[1].shape[0]
+    size = members.shape[2]
     arriving = [
         (rows, pltpu.make_async_copy(member_refs[i], members.at[i], member_sem.at[i]))
-        for i, rows in enumerate(fetches(sources, taken, row_sem))
+        for i, rows in enumerate(fetches(sources, size, taken, row_sem))
     ]
     for pair in arriving:
         for copy in pair:
@@ -182,13 +186,13 @@
     count, size = members[0].shape
     width = sources[0].shape[1]
     return call(
-        functools.partial(sum_kernel, pieces, len(totals)),
+        functools.partial(sum_kernel, pieces, len(totals), len(sources)),
         "weighted_sums",
         FULL,
         2 * pieces * size * width * count,
         in_specs=[pl.BlockSpec(memory_space=pltpu.SMEM)]
         + [whole()] * (1 + len(totals))
-        + [in_hbm()] * (2 * pieces - 1)
+        + [in_hbm()] * (pieces + len(sources))
         + [in_hbm()] * len(after),
         out_specs=whole(),
         out_shape=jax.ShapeDtypeStruct((chips, 2, count // 2 // chips, width), jnp.bfloat16),
@@ -257,7 +261,7 @@
         high, low = lax.div(cluster, low_count), lax.rem(cluster, low_count)
         high_hits = lax.broadcasted_iota(jnp.int32, (high_count, local_rows), 0) == high
         by_low = lax.dot_general(
-            table_ref[...].astype(jnp.bfloat16),
+            table_ref[...].astype(jnp.float32).astype(jnp.bfloat16),
             jnp.where(high_hits, 1.0, 0.0).astype(jnp.bfloat16),
             (((0,), (0,)), ((), ())),
             preferred_element_type=jnp.float32,
@@ -318,7 +322,7 @@
         depth.reshape(1).astype(jnp.int32),
         embeddings,
         assign.reshape(1, local_rows),
-        owner_map.reshape(-1, low_count).astype(jnp.float32),
+        owner_map.reshape(-1, low_count),
     )
 
 
@@ -460,12 +464,9 @@
         return lax.ppermute(value, "dp", other_core)
 
     cut = local_rows // 2
-    first, second = embeddings[:cut], embeddings[cut:]
-    below_first, above_second = send(first, 1), send(second, -1)
-    below_second, above_first = send(second, 1), send(first, -1)
-    far_first, far_second = send(below_first, 1), send(above_second, -1)
-    received = [above_first, above_second, far_first, far_second, below_first, below_second]
-    sources = [embeddings] + received
+    below, above = send(embeddings, 1), send(embeddings, -1)
+    far_first, far_second = send(below[:cut], 1), send(above[cut:], -1)
+    sources = [embeddings, above, far_first, far_second, below]
 
     packed = pack(embeddings, assign, owner_map, depth, devices, cent_count, capacity)
     routed = exchange(packed.reshape(dp_count, cent_count * capacity, -1)).reshape(
@@ -475,9 +476,14 @@
     own_half = lax.dynamic_slice_in_dim(initial, core * half, half, 0)
     other_half = lax.dynamic_slice_in_dim(initial, (1 - core) * half, half, 0)
     block = jnp.concatenate([own_half, other_half])
-    scored = [score_piece(embeddings, block, 2, OWN_COST)] + [
-        score_piece(piece, block, 1, FAR_COST if piece is far_first or piece is far_second else NEAR_COST)
-        for piece in received
+    scored = [
+        score_piece(raws, block, cut, cost)
+        for raws, cost in [
+            ([embeddings], OWN_COST),
+            ([above], NEAR_COST),
+            ([far_first, far_second], FAR_COST),
+            ([below], NEAR_COST),
+        ]
     ]
     members = [member for *parts, _, _ in scored for member in parts]
     partial_total = jnp.concatenate([total for *_, total, _ in scored], axis=1)
@@ -492,7 +498,7 @@
     blocks[2] = send(order(parted[2], [blocks[1], blocks[3]]), 2)
 
     own_half = exchange_plane(combine(arrived, planes, [])).reshape(half, feature_width)
-    members, partial_total = score_rows(sources, scale, own_half, swap_cores(own_half))
+    members, partial_total = score_rows(sources, scale, own_half, swap_cores(own_half), cut)
     totals = [partial_total] + [send(partial_total, -k) for k in range(1, cent_count)]
     sums = weighted_sums(members, sources, scale, totals, core, planes, [blocks[2]])
     arrived = exchange(sums.reshape(dp_count, share, feature_width))

time: 190 us -> 186 us (0.979)
  Pallas kernels: 61.4 us -> 59.2 us
    ppermute x15 -> x13, waiting for transfers between devices: 26.9 us -> 29.9 us  [send(): lax.ppermute(value, 'cent', [(z, (z + step) % cent_count) for z in range(...]
    ppermute x15 -> x13, starting transfers between devices: 19.5 us -> 17.2 us  [send(): lax.ppermute(value, 'cent', [(z, (z + step) % cent_count) for z in range(...]
    pallas_call x9 -> x6, Pallas kernels: 26.2 us -> 24 us  [the longest x2 17.3 us: weighted_sums(): call(functools.partial(sum_kernel, pieces, len(totals), len(sources)), 'w...]
    unnamed x69 -> x61, local copies, waits for them, and re-layouts: 8.95 us -> 7.9 us
  transfers between devices with their start and end apart: 21 -> 19, of which waited for: 14 -> 12; matrix products, arithmetic and copies ran while one was open for 2% -> 3% of each run, Pallas kernels for 27% -> 26%
where the time goes in v4:
time: 186 us; the launch traced here: 185 us
  Pallas kernels  59.2 us (32%)
  waiting for transfers between devices  52.7 us (28%)
  starting transfers between devices  47 us (25%)
  local copies, waits for them, and re-layouts  12.5 us (7%)
  blocking collectives  12.2 us (7%)
    ppermute x13, waiting for transfers between devices, send(): lax.ppermute(value, 'cent', [(z, (z + step) % cent_count) for z in range(...  29.9 us
    all_to_all x3, starting transfers between devices, exchange(): return lax.all_to_all(value, 'dp', 0, 0, tiled=True)  23.1 us
    all_to_all x3, waiting for transfers between devices, exchange(): return lax.all_to_all(value, 'dp', 0, 0, tiled=True)  18.7 us
    pallas_call x2, Pallas kernels, weighted_sums(): call(functools.partial(sum_kernel, pieces, len(totals), len(sources)), 'w...  17.3 us
    ppermute x13, starting transfers between devices, send(): lax.ppermute(value, 'cent', [(z, (z + step) % cent_count) for z in range(...  17.2 us
    pallas_call x2, Pallas kernels, similarity_of(): call(functools.partial(similarity_kernel, cent_count, part * steps), 'sim...  15.5 us
    all_to_all x1, blocking collectives, exchange_plane(): lax.all_to_all(value, 'dp', 0, 0, axis_index_groups=same_core, tiled=True)  12.2 us
    pallas_call x1, Pallas kernels, score_rows(): call(functools.partial(score_kernel, pieces), 'score_rows', FULL, NEAR_CO...  8.77 us
  transfers between devices with their start and end apart: 19, of which 12 were waited for; matrix products, arithmetic and copies ran while one was open for 3% of the time, Pallas kernels for 26%

profile of v4, /device:TPU:1, one launch (start us, length us, event | category | flops | bytes accessed | tf_op | source)
XLA Modules:
  0.0 185.1 jit_solution(15925268270299274196)
XLA Ops:
  0.6 2.5 %collective-permute-start.1 = (bf16[1024,768]{1,0:T(8,128)(2,1)}, bf16[1024,768]{1,0:T(8,128)(2,1)S(1)}, u32[]{:S(2)}, u32[]{:S(2)}) collective-permute-start(bf16[1024,768]{1,0:T(8,128)(2,1)} %rest_12_.3), channel_id=1, source_target_pairs={{0,1},{1,2},{2,3},{3,0},{4,5},{5,6},{6,7},{7,4},{8,9},{9,10},{10,1... | collective-permute-start | bytes 4718600 | tf_op jit(solution)/shard_map/ppermute | solution.py:450
  3.2 2.2 %collective-permute-start = (bf16[1024,768]{1,0:T(8,128)(2,1)}, bf16[1024,768]{1,0:T(8,128)(2,1)}, u32[]{:S(2)}, u32[]{:S(2)}) collective-permute-start(bf16[1024,768]{1,0:T(8,128)(2,1)} %rest_12_.3), channel_id=1, source_target_pairs={{0,3},{1,0},{2,1},{3,2},{4,7},{5,4},{6,5},{7,6},{8,11},{9,8},{10,9... | collective-permute-start | bytes 4718600 | tf_op jit(solution)/shard_map/ppermute | solution.py:450
  5.4 8.5 %pack.1 = bf16[2048,896]{1,0:T(8,128)(2,1)} custom-call(s32[1]{0:T(128)} %bitcast.1.depth_ref, bf16[1024,768]{1,0:T(8,128)(2,1)} %rest_12_.3, s32[1,1024]{1,0:T(1,128)} %bitcast.29, s32[16,128]{1,0:T(8,128)} %bitcast.28), custom_call_target="tpu_custom_call" | custom-call | flops 3221225472 | bytes 1048576 | tf_op jit(solution)/shard_map/pack/pallas_call | solution.py:308
  13.8 8.2 %all-to-all-start = ((bf16[32,64,896]{2,1,0:T(8,128)(2,1)}), bf16[32,64,896]{2,1,0:T(8,128)(2,1)}, u32[]{:S(2)}, u32[]{:S(2)}) async-start(bf16[32,64,896]{2,1,0:T(8,128)(2,1)} %bitcast.23), calls=%async_computation | async-start | bytes 7340032 | tf_op jit(solution)/shard_map/all_to_all | solution.py:455
  22.7 17.0 %collective-permute-done.1.rest_0_.rest_16_.rest_4_ = bf16[1024,768]{1,0:T(8,128)(2,1)S(1)} collective-permute-done((bf16[1024,768]{1,0:T(8,128)(2,1)}, bf16[1024,768]{1,0:T(8,128)(2,1)S(1)}, u32[]{:S(2)}, u32[]{:S(2)}) %collective-permute-start.1) | collective-permute-done | bytes 1572896 | tf_op jit(solution)/shard_map/ppermute | solution.py:450
  41.5 2.3 %collective-permute-start.3 = (bf16[512,768]{1,0:T(8,128)(2,1)S(1)}, bf16[512,768]{1,0:T(8,128)(2,1)S(1)}, u32[]{:S(2)}, u32[]{:S(2)}) collective-permute-start(bf16[512,768]{1,0:T(8,128)(2,1)S(1)} %slice.21), channel_id=1, source_target_pairs={{0,3},{1,0},{2,1},{3,2},{4,7},{5,4},{6,5},{7,6},{8,11},{9,8},{10,9... | collective-permute-start | bytes 2359304 | tf_op jit(solution)/shard_map/ppermute | solution.py:450
  47.2 3.0 %score_piece.5 = (bf16[512,512]{1,0:T(8,128)(2,1)S(1)}, bf16[512,512]{1,0:T(8,128)(2,1)S(1)}, f32[1,1024]{1,0:T(1,128)S(1)}, f32[1,1024]{1,0:T(1,128)S(1)}) custom-call(bf16[512,768]{1,0:T(8,128)(2,1)S(1)} %pad_maximum_fusion.block_ref, bf16[1024,768]{1,0:T(8,128)(2,1)} %collective-permute-done.rest_0_.rest_13_.rest_1_), custom_call_target="tpu_custom_call" | custom-call | flops 1000000 | bytes 1048576 | tf_op jit(solution)/shard_map/score_piece/pallas_call | solution.py:83
  51.8 7.2 %collective-permute-done.2.rest_0_.rest_14_.rest_2_ = bf16[512,768]{1,0:T(8,128)(2,1)S(1)} collective-permute-done((bf16[512,768]{1,0:T(8,128)(2,1)S(1)}, bf16[512,768]{1,0:T(8,128)(2,1)S(1)}, u32[]{:S(2)}, u32[]{:S(2)}) %collective-permute-start.2) | collective-permute-done | bytes 786464 | tf_op jit(solution)/shard_map/ppermute | solution.py:450
  62.6 4.2 %collective-permute-start.5 = (f32[1,4096]{1,0:T(1,128)S(1)}, f32[1,4096]{1,0:T(1,128)S(1)}, u32[]{:S(2)}, u32[]{:S(2)}) collective-permute-start(f32[1,4096]{1,0:T(1,128)S(1)} %constant_dynamic-update-slice_fusion.4.rest_0_), channel_id=1, source_target_pairs={{0,2},{1,3},{2,0},{3,1},{4,6},{5,7},{6,4},{7,5},{8,10},{9,11},{10,... | collective-permute-start | bytes 49160 | tf_op jit(solution)/shard_map/ppermute | solution.py:450
  68.1 2.9 %slice_bitcast_fusion = (bf16[32,16,896]{2,1,0:T(8,128)(2,1)S(1)}, bf16[32,16,896]{2,1,0:T(8,128)(2,1)}, bf16[32,16,896]{2,1,0:T(8,128)(2,1)S(1)}) fusion(bf16[32,4,16,896]{3,2,1,0:T(8,128)(2,1)} %bitcast.5.rest_0_), kind=kLoop, calls=%fused_computation.4 | loop fusion | bytes 5505024 | tf_op jit(solution)/shard_map/squeeze | solution.py:493
  71.0 1.7 collective-permute-start.12
  73.4 8.7 %weighted_sums.2 = bf16[16,2,16,768]{3,2,1,0:T(8,128)(2,1)} custom-call(s32[1]{0:T(128)} %bitcast.core_ref, f32[1,4096]{1,0:T(1,128)} %copy-done.20, f32[1,4096]{1,0:T(1,128)} %copy-done.21, f32[1,4096]{1,0:T(1,128)} %copy-done.24, f32[1,4096]{1,0:T(1,128)} %copy-done.23, f32[1,4096]{1,0:T(1,128)} %copy-done.22, bf16[512,512]{1,0:T(8,128)(2,1)} %copy-done.4, ...), custom_call_target="tpu_custom_call" | custom-call | flops 3221225472 | bytes 1048576 | tf_op jit(solution)/shard_map/weighted_sums/pallas_call | solution.py:188
  82.1 9.4 %all-to-all-start.1 = ((bf16[32,16,768]{2,1,0:T(8,128)(2,1)}), bf16[32,16,768]{2,1,0:T(8,128)(2,1)S(1)}, u32[]{:S(2)}, u32[]{:S(2)}) async-start(bf16[32,16,768]{2,1,0:T(8,128)(2,1)} %bitcast.24), calls=%async_computation.1 | async-start | bytes 1572864 | tf_op jit(solution)/shard_map/all_to_all | solution.py:455
  91.5 3.2 %collective-permute-done.11.refs_1_.rest_1_ = bf16[32,16,896]{2,1,0:T(8,128)(2,1)} collective-permute-done((bf16[32,16,896]{2,1,0:T(8,128)(2,1)S(1)}, bf16[32,16,896]{2,1,0:T(8,128)(2,1)}, u32[]{:S(2)}, u32[]{:S(2)}) %collective-permute-start.11) | collective-permute-done | bytes 917536 | tf_op jit(solution)/shard_map/ppermute | solution.py:450
  94.7 10.9 %all-to-all-done.1.arrived_ref = bf16[32,16,768]{2,1,0:T(8,128)(2,1)S(1)} async-done(((bf16[32,16,768]{2,1,0:T(8,128)(2,1)}), bf16[32,16,768]{2,1,0:T(8,128)(2,1)S(1)}, u32[]{:S(2)}, u32[]{:S(2)}) %all-to-all-start.1) | async-done | bytes 786464 | tf_op jit(solution)/shard_map/all_to_all | solution.py:455
  105.9 12.2 %all_to_all.25 = bf16[16,16,768]{2,1,0:T(8,128)(2,1)S(1)} all-to-all(bf16[16,16,768]{2,1,0:T(8,128)(2,1)S(1)} %combine.2), channel_id=1, replica_groups={{0,8,16,24,32,40,48,56,64,72,80,88,96,104,112,120},{4,12,20,28,36,44,52..., dimensions={0} | all-to-all | bytes 786432 | tf_op jit(solution)/shard_map/all_to_all | solution.py:461
  121.8 8.8 %score_rows.1 = (bf16[512,512]{1,0:T(8,128)(2,1)}, bf16[512,512]{1,0:T(8,128)(2,1)}, bf16[512,512]{1,0:T(8,128)(2,1)}, bf16[512,512]{1,0:T(8,128)(2,1)}, bf16[51...) custom-call(f32[1,4096]{1,0:T(1,128)} %copy-done.20, ...), custom_call_target="tpu_custom_call" | custom-call | flops 1000000 | bytes 1048576 | tf_op jit(solution)/shard_map/score_rows/pallas_call | solution.py:129
  134.6 1.8 collective-permute-done.9.rest_2_
  137.5 8.5 %weighted_sums.3 = bf16[16,2,16,768]{3,2,1,0:T(8,128)(2,1)} custom-call(s32[1]{0:T(128)} %bitcast.core_ref, f32[1,4096]{1,0:T(1,128)} %copy-done.20, f32[1,4096]{1,0:T(1,128)} %get-tuple-element.47.rest_0_, f32[1,4096]{1,0:T(1,128)} %copy-done.27, f32[1,4096]{1,0:T(1,128)} %copy-done.26, f32[1,4096]{1,0:T(1,128)} %copy-done.25, ...), custom_call_target="tpu_custom_call" | custom-call | flops 3221225472 | bytes 1048576 | tf_op jit(solution)/shard_map/weighted_sums/pallas_call | solution.py:188
  146.0 5.6 %all-to-all-start.3 = ((bf16[32,16,768]{2,1,0:T(8,128)(2,1)}), bf16[32,16,768]{2,1,0:T(8,128)(2,1)S(1)}, u32[]{:S(2)}, u32[]{:S(2)}) async-start(bf16[32,16,768]{2,1,0:T(8,128)(2,1)} %bitcast.25), calls=%async_computation.3 | async-start | bytes 1572864 | tf_op jit(solution)/shard_map/all_to_all | solution.py:455
  151.6 7.7 %similarity.2 = (bf16[1,2048,2048]{2,1,0:T(8,128)(2,1)}, f32[8,128]{1,0:T(8,128)}) custom-call(s32[1]{0:T(128)} %bitcast.1.depth_ref, bf16[32,4,16,896]{3,2,1,0:T(8,128)(2,1)} %bitcast.5.rest_0_, bf16[32,16,896]{2,1,0:T(8,128)(2,1)} %collective-permute-done.11.refs_1_.rest_1_, bf16[32,16,896]{2,1,0:T(8,128)(2,1)} %copy-done.14, ...), custom_call_target="tpu_custom_call" | custom-call | flops 3758096384 | bytes 1048576 | tf_op jit(solution)/shard_map/similarity/pallas_call | solution.py:411
  159.3 6.5 %all-to-all-done.3.arrived_ref = bf16[32,16,768]{2,1,0:T(8,128)(2,1)S(1)} async-done(((bf16[32,16,768]{2,1,0:T(8,128)(2,1)}), bf16[32,16,768]{2,1,0:T(8,128)(2,1)S(1)}, u32[]{:S(2)}, u32[]{:S(2)}) %all-to-all-start.3) | async-done | bytes 786464 | tf_op jit(solution)/shard_map/all_to_all | solution.py:455
  167.5 3.6 %all-to-all-start.4 = ((bf16[16,16,768]{2,1,0:T(8,128)(2,1)}), bf16[16,16,768]{2,1,0:T(8,128)(2,1)S(1)}, u32[]{:S(2)}, u32[]{:S(2)}) async-start(bf16[16,16,768]{2,1,0:T(8,128)(2,1)} %combine.3), calls=%async_computation.4 | async-start | bytes 786432 | tf_op jit(solution)/shard_map/all_to_all | solution.py:461
  171.0 7.7 %similarity.3 = (bf16[1,2048,2048]{2,1,0:T(8,128)(2,1)}, f32[8,128]{1,0:T(8,128)}) custom-call(s32[1]{0:T(128)} %bitcast.1.depth_ref, bf16[32,4,16,896]{3,2,1,0:T(8,128)(2,1)} %bitcast.5.rest_0_, bf16[32,16,896]{2,1,0:T(8,128)(2,1)} %collective-permute-done.11.refs_1_.rest_1_, bf16[32,16,896]{2,1,0:T(8,128)(2,1)} %copy-done.14, ...), custom_call_target="tpu_custom_call", output_to_operand_aliasing={{0}: (5, {})} | custom-call | flops 3758096384 | bytes 1048576 | tf_op jit(solution)/shard_map/similarity/pallas_call | solution.py:411
  (101 shorter events, 29.7 us)
Async XLA Ops:
  0.6 39.1 %collective-permute-start.1 = (bf16[1024,768]{1,0:T(8,128)(2,1)}, bf16[1024,768]{1,0:T(8,128)(2,1)S(1)}, u32[]{:S(2)}, u32[]{:S(2)}) collective-permute-start(bf16[1024,768]{1,0:T(8,128)(2,1)} %rest_12_.3), channel_id=1, source_target_pairs={{0,1},{1,2},{2,3},{3,0},{4,5},{5,6},{6,7},{7,4},{8,9},{9,10},{10,1... | collective-permute-start | bytes 4718600 | tf_op jit(solution)/shard_map/ppermute | solution.py:450
  3.2 36.7 %collective-permute-start = (bf16[1024,768]{1,0:T(8,128)(2,1)}, bf16[1024,768]{1,0:T(8,128)(2,1)}, u32[]{:S(2)}, u32[]{:S(2)}) collective-permute-start(bf16[1024,768]{1,0:T(8,128)(2,1)} %rest_12_.3), channel_id=1, source_target_pairs={{0,3},{1,0},{2,1},{3,2},{4,7},{5,4},{6,5},{7,6},{8,11},{9,8},{10,9... | collective-permute-start | bytes 4718600 | tf_op jit(solution)/shard_map/ppermute | solution.py:450
  13.8 8.2 %copy-start.17 = (bf16[512,768]{1,0:T(8,128)(2,1)S(1)}, bf16[512,768]{1,0:T(8,128)(2,1)}, u32[]{:S(2)}) copy-start(bf16[512,768]{1,0:T(8,128)(2,1)} %param.5) | copy-start | bytes 2359300
  13.8 54.2 %all-to-all-start = ((bf16[32,64,896]{2,1,0:T(8,128)(2,1)}), bf16[32,64,896]{2,1,0:T(8,128)(2,1)}, u32[]{:S(2)}, u32[]{:S(2)}) async-start(bf16[32,64,896]{2,1,0:T(8,128)(2,1)} %bitcast.23), calls=%async_computation | async-start | bytes 7340032 | tf_op jit(solution)/shard_map/all_to_all | solution.py:455
  22.7 21.1 %copy-start.1 = (bf16[1024,768]{1,0:T(8,128)(2,1)S(1)}, bf16[1024,768]{1,0:T(8,128)(2,1)}, u32[]{:S(2)}) copy-start(bf16[1024,768]{1,0:T(8,128)(2,1)} %rest_12_.3) | copy-start | bytes 4718596
  39.8 19.3 %collective-permute-start.2 = (bf16[512,768]{1,0:T(8,128)(2,1)S(1)}, bf16[512,768]{1,0:T(8,128)(2,1)S(1)}, u32[]{:S(2)}, u32[]{:S(2)}) collective-permute-start(bf16[512,768]{1,0:T(8,128)(2,1)S(1)} %slice.20), channel_id=1, source_target_pairs={{0,1},{1,2},{2,3},{3,0},{4,5},{5,6},{6,7},{7,4},{8,9},{9,10},{10,1... | collective-permute-start | bytes 2359304 | tf_op jit(solution)/shard_map/ppermute | solution.py:450
  41.5 18.1 %collective-permute-start.3 = (bf16[512,768]{1,0:T(8,128)(2,1)S(1)}, bf16[512,768]{1,0:T(8,128)(2,1)S(1)}, u32[]{:S(2)}, u32[]{:S(2)}) collective-permute-start(bf16[512,768]{1,0:T(8,128)(2,1)S(1)} %slice.21), channel_id=1, source_target_pairs={{0,3},{1,0},{2,1},{3,2},{4,7},{5,4},{6,5},{7,6},{8,11},{9,8},{10,9... | collective-permute-start | bytes 2359304 | tf_op jit(solution)/shard_map/ppermute | solution.py:450
  47.1 13.7 %copy-start.6 = (bf16[512,512]{1,0:T(8,128)(2,1)}, bf16[512,512]{1,0:T(8,128)(2,1)S(1)}, u32[]{:S(2)}) copy-start(bf16[512,512]{1,0:T(8,128)(2,1)S(1)} %get-tuple-element.45.rest_10_) | copy-start | bytes 1572868
  47.2 13.7 %copy-start.7 = (bf16[512,512]{1,0:T(8,128)(2,1)}, bf16[512,512]{1,0:T(8,128)(2,1)S(1)}, u32[]{:S(2)}) copy-start(bf16[512,512]{1,0:T(8,128)(2,1)S(1)} %get-tuple-element.46.rest_11_) | copy-start | bytes 1572868
  62.5 8.4 %copy-start.21 = (f32[1,4096]{1,0:T(1,128)}, f32[1,4096]{1,0:T(1,128)S(1)}, u32[]{:S(2)}) copy-start(f32[1,4096]{1,0:T(1,128)S(1)} %constant_dynamic-update-slice_fusion.4.rest_0_) | copy-start | bytes 49156
  62.5 10.2 %collective-permute-start.6 = (f32[1,4096]{1,0:T(1,128)S(1)}, f32[1,4096]{1,0:T(1,128)S(1)}, u32[]{:S(2)}, u32[]{:S(2)}) collective-permute-start(f32[1,4096]{1,0:T(1,128)S(1)} %constant_dynamic-update-slice_fusion.4.rest_0_), channel_id=1, source_target_pairs={{0,1},{1,2},{2,3},{3,0},{4,5},{5,6},{6,7},{7,4},{8,9},{9,10},{10,1... | collective-permute-start | bytes 49160 | tf_op jit(solution)/shard_map/ppermute | solution.py:450
  62.6 10.1 %collective-permute-start.5 = (f32[1,4096]{1,0:T(1,128)S(1)}, f32[1,4096]{1,0:T(1,128)S(1)}, u32[]{:S(2)}, u32[]{:S(2)}) collective-permute-start(f32[1,4096]{1,0:T(1,128)S(1)} %constant_dynamic-update-slice_fusion.4.rest_0_), channel_id=1, source_target_pairs={{0,2},{1,3},{2,0},{3,1},{4,6},{5,7},{6,4},{7,5},{8,10},{9,11},{10,... | collective-permute-start | bytes 49160 | tf_op jit(solution)/shard_map/ppermute | solution.py:450
  66.8 5.9 %collective-permute-start.4 = (f32[1,4096]{1,0:T(1,128)S(1)}, f32[1,4096]{1,0:T(1,128)S(1)}, u32[]{:S(2)}, u32[]{:S(2)}) collective-permute-start(f32[1,4096]{1,0:T(1,128)S(1)} %constant_dynamic-update-slice_fusion.4.rest_0_), channel_id=1, source_target_pairs={{0,3},{1,0},{2,1},{3,2},{4,7},{5,4},{6,5},{7,6},{8,11},{9,8},{10,9... | collective-permute-start | bytes 49160 | tf_op jit(solution)/shard_map/ppermute | solution.py:450
  71.0 20.5 %collective-permute-start.12 = (bf16[32,16,896]{2,1,0:T(8,128)(2,1)S(1)}, bf16[32,16,896]{2,1,0:T(8,128)(2,1)}, u32[]{:S(2)}, u32[]{:S(2)}) collective-permute-start(bf16[32,16,896]{2,1,0:T(8,128)(2,1)S(1)} %get-tuple-element.60.rest_19_), channel_id=1, source_target_pairs={{0,3},{1,0},{2,1},{3,2},{4,7},{5,4},{6,5},{7,6},{8,11},{9,8},{10,9... | collective-permute-start | bytes 2752520 | tf_op jit(solution)/shard_map/ppermute | solution.py:450
  72.7 22.0 %collective-permute-start.11 = (bf16[32,16,896]{2,1,0:T(8,128)(2,1)S(1)}, bf16[32,16,896]{2,1,0:T(8,128)(2,1)}, u32[]{:S(2)}, u32[]{:S(2)}) collective-permute-start(bf16[32,16,896]{2,1,0:T(8,128)(2,1)S(1)} %get-tuple-element.62.rest_17_), channel_id=1, source_target_pairs={{0,1},{1,2},{2,3},{3,0},{4,5},{5,6},{6,7},{7,4},{8,9},{9,10},{10,1... | collective-permute-start | bytes 2752520 | tf_op jit(solution)/shard_map/ppermute | solution.py:450
  82.1 23.6 %all-to-all-start.1 = ((bf16[32,16,768]{2,1,0:T(8,128)(2,1)}), bf16[32,16,768]{2,1,0:T(8,128)(2,1)S(1)}, u32[]{:S(2)}, u32[]{:S(2)}) async-start(bf16[32,16,768]{2,1,0:T(8,128)(2,1)} %bitcast.24), calls=%async_computation.1 | async-start | bytes 1572864 | tf_op jit(solution)/shard_map/all_to_all | solution.py:455
  94.7 41.7 %collective-permute-start.13 = (bf16[32,16,896]{2,1,0:T(8,128)(2,1)}, bf16[32,16,896]{2,1,0:T(8,128)(2,1)S(1)}, u32[]{:S(2)}, u32[]{:S(2)}) collective-permute-start(bf16[32,16,896]{2,1,0:T(8,128)(2,1)} %order.1), channel_id=1, source_target_pairs={{0,2},{1,3},{2,0},{3,1},{4,6},{5,7},{6,4},{7,5},{8,10},{9,11},{10,... | collective-permute-start | bytes 2752520 | tf_op jit(solution)/shard_map/ppermute | solution.py:450
  118.1 2.9 %collective-permute-start.7 = (bf16[256,768]{1,0:T(8,128)(2,1)S(1)}, bf16[256,768]{1,0:T(8,128)(2,1)S(1)}, u32[]{:S(2)}, u32[]{:S(2)}) collective-permute-start(bf16[256,768]{1,0:T(8,128)(2,1)S(1)} %bitcast.26), channel_id=1, source_target_pairs={{0,4},{4,0},{8,12},{12,8},{16,20},{20,16},{24,28},{28,24},{32,36},... | collective-permute-start | bytes 1179656 | tf_op jit(solution)/shard_map/ppermute | solution.py:464
  130.6 4.1 %collective-permute-start.10 = (f32[1,4096]{1,0:T(1,128)}, f32[1,4096]{1,0:T(1,128)S(1)}, u32[]{:S(2)}, u32[]{:S(2)}) collective-permute-start(f32[1,4096]{1,0:T(1,128)} %get-tuple-element.47.rest_0_), channel_id=1, source_target_pairs={{0,1},{1,2},{2,3},{3,0},{4,5},{5,6},{6,7},{7,4},{8,9},{9,10},{10,1... | collective-permute-start | bytes 49160 | tf_op jit(solution)/shard_map/ppermute | solution.py:450
  132.1 4.3 %collective-permute-start.9 = (f32[1,4096]{1,0:T(1,128)}, f32[1,4096]{1,0:T(1,128)S(1)}, u32[]{:S(2)}, u32[]{:S(2)}) collective-permute-start(f32[1,4096]{1,0:T(1,128)} %get-tuple-element.47.rest_0_), channel_id=1, source_target_pairs={{0,2},{1,3},{2,0},{3,1},{4,6},{5,7},{6,4},{7,5},{8,10},{9,11},{10,... | collective-permute-start | bytes 49160 | tf_op jit(solution)/shard_map/ppermute | solution.py:450
  133.0 3.4 %collective-permute-start.8 = (f32[1,4096]{1,0:T(1,128)}, f32[1,4096]{1,0:T(1,128)S(1)}, u32[]{:S(2)}, u32[]{:S(2)}) collective-permute-start(f32[1,4096]{1,0:T(1,128)} %get-tuple-element.47.rest_0_), channel_id=1, source_target_pairs={{0,3},{1,0},{2,1},{3,2},{4,7},{5,4},{6,5},{7,6},{8,11},{9,8},{10,9... | collective-permute-start | bytes 49160 | tf_op jit(solution)/shard_map/ppermute | solution.py:450
  146.0 19.8 %all-to-all-start.3 = ((bf16[32,16,768]{2,1,0:T(8,128)(2,1)}), bf16[32,16,768]{2,1,0:T(8,128)(2,1)S(1)}, u32[]{:S(2)}, u32[]{:S(2)}) async-start(bf16[32,16,768]{2,1,0:T(8,128)(2,1)} %bitcast.25), calls=%async_computation.3 | async-start | bytes 1572864 | tf_op jit(solution)/shard_map/all_to_all | solution.py:455
  167.5 12.8 %all-to-all-start.4 = ((bf16[16,16,768]{2,1,0:T(8,128)(2,1)}), bf16[16,16,768]{2,1,0:T(8,128)(2,1)S(1)}, u32[]{:S(2)}, u32[]{:S(2)}) async-start(bf16[16,16,768]{2,1,0:T(8,128)(2,1)} %combine.3), calls=%async_computation.4 | async-start | bytes 786432 | tf_op jit(solution)/shard_map/all_to_all | solution.py:461
  181.0 2.9 %collective-permute-start.14 = (bf16[256,768]{1,0:T(8,128)(2,1)S(1)}, bf16[256,768]{1,0:T(8,128)(2,1)S(1)}, u32[]{:S(2)}, u32[]{:S(2)}) collective-permute-start(bf16[256,768]{1,0:T(8,128)(2,1)S(1)} %hold.1.own_ref), channel_id=1, source_target_pairs={{0,4},{4,0},{8,12},{12,8},{16,20},{20,16},{24,28},{28,24},{32,36},... | collective-permute-start | bytes 1179656 | tf_op jit(solution)/shard_map/ppermute | solution.py:464
  (23 other events, 36.2 us)

commit v5 on v4

--- a/solution.py
+++ b/solution.py
@@ -146,9 +146,10 @@
     return out[:pieces], out[pieces]
 
 
-def sum_kernel(pieces, depth, source_count, core_ref, scale_ref, *rest):
+def sum_kernel(pieces, depth, source_count, outs, core_ref, scale_ref, *rest):
     total_refs, rest = rest[:depth], rest[depth:]
-    sums_ref, members, taken, running, member_sem, row_sem = rest[-6:]
+    *rest, members, taken, running, member_sem, row_sem = rest
+    out_refs = rest[-outs:]
     member_refs, sources = rest[:pieces], rest[pieces : pieces + source_count]
     half = running.shape[0] // 2
     size = members.shape[2]
@@ -176,17 +177,22 @@
         else:
             running[...] += product
     own, other = running[:half].astype(jnp.bfloat16), running[half:].astype(jnp.bfloat16)
-    chips, _, share, width = sums_ref.shape
-    sums_ref[:, core_ref[0]] = own.reshape(chips, share, width)
-    sums_ref[:, 1 - core_ref[0]] = other.reshape(chips, share, width)
+    if outs == 2:
+        out_refs[0][...], out_refs[1][...] = own, other
+    else:
+        chips, _, share, width = out_refs[0].shape
+        out_refs[0][:, core_ref[0]] = own.reshape(chips, share, width)
+        out_refs[0][:, 1 - core_ref[0]] = other.reshape(chips, share, width)
 
 
 def weighted_sums(members, sources, scale, totals, core, chips, after):
     pieces = len(members)
     count, size = members[0].shape
     width = sources[0].shape[1]
-    return call(
-        functools.partial(sum_kernel, pieces, len(totals), len(sources)),
+    half = count // 2
+    shapes = [(chips, 2, half // chips, width)] if chips else [(half, width)] * 2
+    return call(
+        functools.partial(sum_kernel, pieces, len(totals), len(sources), len(shapes)),
         "weighted_sums",
         FULL,
         2 * pieces * size * width * count,
@@ -194,8 +200,8 @@
         + [whole()] * (1 + len(totals))
         + [in_hbm()] * (pieces + len(sources))
         + [in_hbm()] * len(after),
-        out_specs=whole(),
-        out_shape=jax.ShapeDtypeStruct((chips, 2, count // 2 // chips, width), jnp.bfloat16),
+        out_specs=[whole()] * len(shapes),
+        out_shape=[jax.ShapeDtypeStruct(shape, jnp.bfloat16) for shape in shapes],
         scratch_shapes=[
             pltpu.VMEM((pieces, count, size), jnp.bfloat16),
             pltpu.VMEM((pieces * size, width), jnp.bfloat16),
@@ -491,8 +497,9 @@
 
     totals = [partial_total] + [send(partial_total, -k) for k in range(1, cent_count)]
     parted = [routed[:, k] for k in range(cent_count)]
-    sums = weighted_sums(members, sources, scale, totals, core, planes, parted[1:])
-    arrived = exchange(sums.reshape(dp_count, share, feature_width))
+    own, for_sibling = weighted_sums(members, sources, scale, totals, core, 0, parted[1:])
+    both = (own.astype(jnp.float32) + swap_cores(for_sibling).astype(jnp.float32)).astype(jnp.bfloat16)
+    arrived = exchange_plane(both.reshape(planes, share, feature_width))
 
     blocks = [routed, send(parted[1], 1), None, send(parted[3], -1)]
     blocks[2] = send(order(parted[2], [blocks[1], blocks[3]]), 2)
@@ -500,7 +507,7 @@
     own_half = exchange_plane(combine(arrived, planes, [])).reshape(half, feature_width)
     members, partial_total = score_rows(sources, scale, own_half, swap_cores(own_half), cut)
     totals = [partial_total] + [send(partial_total, -k) for k in range(1, cent_count)]
-    sums = weighted_sums(members, sources, scale, totals, core, planes, [blocks[2]])
+    (sums,) = weighted_sums(members, sources, scale, totals, core, planes, [blocks[2]])
     arrived = exchange(sums.reshape(dp_count, share, feature_width))
     similarity, upper = similarity_of(blocks, depth, 0, 2, None)
     spread = combine(arrived, planes, [upper])

time: 186 us -> 185 us (level)
  waiting for transfers between devices: 52.7 us -> 47.8 us
  starting transfers between devices: 47 us -> 49.7 us
  other arithmetic: 0.49 us -> 2.37 us
    all_to_all x3 -> x2, waiting for transfers between devices: 18.7 us -> 7.71 us  [exchange(): return lax.all_to_all(value, 'dp', 0, 0, tiled=True)]
    all_to_all x3 -> x2, starting transfers between devices: 23.1 us -> 13.8 us  [exchange(): return lax.all_to_all(value, 'dp', 0, 0, tiled=True)]
    all_to_all x1 -> x2, waiting for transfers between devices: 1.49 us -> 9.08 us  [exchange_plane(): lax.all_to_all(value, 'dp', 0, 0, axis_index_groups=same_core, tiled=True)]
    all_to_all x1 -> x2, starting transfers between devices: 3.55 us -> 10.3 us  [exchange_plane(): lax.all_to_all(value, 'dp', 0, 0, axis_index_groups=same_core, tiled=True)]
    ppermute x2 -> x3, starting transfers between devices: 3.1 us -> 6.88 us  [swap_cores(): return lax.ppermute(value, 'dp', other_core)]
    ppermute x13, waiting for transfers between devices: 29.9 us -> 26.7 us  [send(): lax.ppermute(value, 'cent', [(z, (z + step) % cent_count) for z in range(...]
    convert_element_type x0 -> x1, other arithmetic: none -> 1.88 us  [shards(): (own.astype(jnp.float32) + swap_cores(for_sibling).astype(jnp.float32)).a...]
    ppermute x2 -> x3, waiting for transfers between devices: 2.7 us -> 4.26 us  [swap_cores(): return lax.ppermute(value, 'dp', other_core)]
  transfers between devices with their start and end apart: 19 -> 20, of which waited for: 12 -> 12; matrix products, arithmetic and copies ran while one was open for 3% -> 4% of each run, Pallas kernels for 26% -> 26%
where the time goes in v5:
time: 185 us; the launch traced here: 184 us
  Pallas kernels  59.1 us (32%)
  starting transfers between devices  49.7 us (27%)
  waiting for transfers between devices  47.8 us (26%)
  local copies, waits for them, and re-layouts  12.5 us (7%)
  blocking collectives  11.2 us (6%)
  other arithmetic  2.37 us (1%)
    ppermute x13, waiting for transfers between devices, send(): lax.ppermute(value, 'cent', [(z, (z + step) % cent_count) for z in range(...  26.7 us
    ppermute x13, starting transfers between devices, send(): lax.ppermute(value, 'cent', [(z, (z + step) % cent_count) for z in range(...  18.7 us
    pallas_call x2, Pallas kernels, weighted_sums(): call(functools.partial(sum_kernel, pieces, len(totals), len(sources), len...  17.2 us
    pallas_call x2, Pallas kernels, similarity_of(): call(functools.partial(similarity_kernel, cent_count, part * steps), 'sim...  15.4 us
    all_to_all x2, starting transfers between devices, exchange(): return lax.all_to_all(value, 'dp', 0, 0, tiled=True)  13.8 us
    all_to_all x1, blocking collectives, exchange_plane(): lax.all_to_all(value, 'dp', 0, 0, axis_index_groups=same_core, tiled=True)  11.2 us
    all_to_all x2, starting transfers between devices, exchange_plane(): lax.all_to_all(value, 'dp', 0, 0, axis_index_groups=same_core, tiled=True)  10.3 us
    all_to_all x2, waiting for transfers between devices, exchange_plane(): lax.all_to_all(value, 'dp', 0, 0, axis_index_groups=same_core, tiled=True)  9.08 us
  transfers between devices with their start and end apart: 20, of which 12 were waited for; matrix products, arithmetic and copies ran while one was open for 4% of the time, Pallas kernels for 26%

profile of v5, /device:TPU:1, one launch (start us, length us, event | category | flops | bytes accessed | tf_op | source)
XLA Modules:
  0.0 183.7 jit_solution(3039244236913642769)
XLA Ops:
  0.6 2.5 %collective-permute-start.1 = (bf16[1024,768]{1,0:T(8,128)(2,1)}, bf16[1024,768]{1,0:T(8,128)(2,1)S(1)}, u32[]{:S(2)}, u32[]{:S(2)}) collective-permute-start(bf16[1024,768]{1,0:T(8,128)(2,1)} %rest_12_.3), channel_id=1, source_target_pairs={{0,1},{1,2},{2,3},{3,0},{4,5},{5,6},{6,7},{7,4},{8,9},{9,10},{10,1... | collective-permute-start | bytes 4718600 | tf_op jit(solution)/shard_map/ppermute | solution.py:456
  3.2 2.2 %collective-permute-start = (bf16[1024,768]{1,0:T(8,128)(2,1)}, bf16[1024,768]{1,0:T(8,128)(2,1)}, u32[]{:S(2)}, u32[]{:S(2)}) collective-permute-start(bf16[1024,768]{1,0:T(8,128)(2,1)} %rest_12_.3), channel_id=1, source_target_pairs={{0,3},{1,0},{2,1},{3,2},{4,7},{5,4},{6,5},{7,6},{8,11},{9,8},{10,9... | collective-permute-start | bytes 4718600 | tf_op jit(solution)/shard_map/ppermute | solution.py:456
  5.4 8.5 %pack.1 = bf16[2048,896]{1,0:T(8,128)(2,1)} custom-call(s32[1]{0:T(128)} %bitcast.1.depth_ref, bf16[1024,768]{1,0:T(8,128)(2,1)} %rest_12_.3, s32[1,1024]{1,0:T(1,128)} %bitcast.28, s32[16,128]{1,0:T(8,128)} %bitcast.27), custom_call_target="tpu_custom_call" | custom-call | flops 3221225472 | bytes 1048576 | tf_op jit(solution)/shard_map/pack/pallas_call | solution.py:314
  13.8 8.2 %all-to-all-start = ((bf16[32,64,896]{2,1,0:T(8,128)(2,1)}), bf16[32,64,896]{2,1,0:T(8,128)(2,1)}, u32[]{:S(2)}, u32[]{:S(2)}) async-start(bf16[32,64,896]{2,1,0:T(8,128)(2,1)} %bitcast.23), calls=%async_computation | async-start | bytes 7340032 | tf_op jit(solution)/shard_map/all_to_all | solution.py:461
  22.7 17.0 %collective-permute-done.1.rest_0_.rest_16_.rest_4_ = bf16[1024,768]{1,0:T(8,128)(2,1)S(1)} collective-permute-done((bf16[1024,768]{1,0:T(8,128)(2,1)}, bf16[1024,768]{1,0:T(8,128)(2,1)S(1)}, u32[]{:S(2)}, u32[]{:S(2)}) %collective-permute-start.1) | collective-permute-done | bytes 1572896 | tf_op jit(solution)/shard_map/ppermute | solution.py:456
  41.5 2.3 %collective-permute-start.3 = (bf16[512,768]{1,0:T(8,128)(2,1)S(1)}, bf16[512,768]{1,0:T(8,128)(2,1)S(1)}, u32[]{:S(2)}, u32[]{:S(2)}) collective-permute-start(bf16[512,768]{1,0:T(8,128)(2,1)S(1)} %slice.21), channel_id=1, source_target_pairs={{0,3},{1,0},{2,1},{3,2},{4,7},{5,4},{6,5},{7,6},{8,11},{9,8},{10,9... | collective-permute-start | bytes 2359304 | tf_op jit(solution)/shard_map/ppermute | solution.py:456
  47.1 3.0 %score_piece.5 = (bf16[512,512]{1,0:T(8,128)(2,1)S(1)}, bf16[512,512]{1,0:T(8,128)(2,1)S(1)}, f32[1,1024]{1,0:T(1,128)S(1)}, f32[1,1024]{1,0:T(1,128)S(1)}) custom-call(bf16[512,768]{1,0:T(8,128)(2,1)S(1)} %pad_maximum_fusion.block_ref, bf16[1024,768]{1,0:T(8,128)(2,1)} %collective-permute-done.rest_0_.rest_13_.rest_1_), custom_call_target="tpu_custom_call" | custom-call | flops 1000000 | bytes 1048576 | tf_op jit(solution)/shard_map/score_piece/pallas_call | solution.py:83
  51.8 7.2 %collective-permute-done.2.rest_0_.rest_14_.rest_2_ = bf16[512,768]{1,0:T(8,128)(2,1)S(1)} collective-permute-done((bf16[512,768]{1,0:T(8,128)(2,1)S(1)}, bf16[512,768]{1,0:T(8,128)(2,1)S(1)}, u32[]{:S(2)}, u32[]{:S(2)}) %collective-permute-start.2) | collective-permute-done | bytes 786464 | tf_op jit(solution)/shard_map/ppermute | solution.py:456
  62.6 4.2 %collective-permute-start.5 = (f32[1,4096]{1,0:T(1,128)S(1)}, f32[1,4096]{1,0:T(1,128)S(1)}, u32[]{:S(2)}, u32[]{:S(2)}) collective-permute-start(f32[1,4096]{1,0:T(1,128)S(1)} %constant_dynamic-update-slice_fusion.4.rest_0_), channel_id=1, source_target_pairs={{0,2},{1,3},{2,0},{3,1},{4,6},{5,7},{6,4},{7,5},{8,10},{9,11},{10,... | collective-permute-start | bytes 49160 | tf_op jit(solution)/shard_map/ppermute | solution.py:456
  68.1 2.9 %slice_bitcast_fusion = (bf16[32,16,896]{2,1,0:T(8,128)(2,1)S(1)}, bf16[32,16,896]{2,1,0:T(8,128)(2,1)}, bf16[32,16,896]{2,1,0:T(8,128)(2,1)S(1)}) fusion(bf16[32,4,16,896]{3,2,1,0:T(8,128)(2,1)} %bitcast.5.rest_0_), kind=kLoop, calls=%fused_computation.4 | loop fusion | bytes 5505024 | tf_op jit(solution)/shard_map/squeeze | solution.py:499
  73.4 8.7 %weighted_sums.2 = (bf16[256,768]{1,0:T(8,128)(2,1)}, bf16[256,768]{1,0:T(8,128)(2,1)}) custom-call(s32[1]{0:T(128)} %bitcast.core_ref, f32[1,4096]{1,0:T(1,128)} %copy-done.20, f32[1,4096]{1,0:T(1,128)} %copy-done.21, f32[1,4096]{1,0:T(1,128)} %copy-done.24, f32[1,4096]{1,0:T(1,128)} %copy-done.23, f32[1,4096]{1,0:T(1,128)} %copy-done.22, ...), custom_call_target="tpu_custom_call" | custom-call | flops 3221225472 | bytes 1048576 | tf_op jit(solution)/shard_map/weighted_sums/pallas_call | solution.py:194
  82.1 2.4 %collective-permute-start.7 = (bf16[256,768]{1,0:T(8,128)(2,1)}, bf16[256,768]{1,0:T(8,128)(2,1)S(1)}, u32[]{:S(2)}, u32[]{:S(2)}) collective-permute-start(bf16[256,768]{1,0:T(8,128)(2,1)} %get-tuple-element.50), channel_id=1, source_target_pairs={{0,4},{4,0},{8,12},{12,8},{16,20},{20,16},{24,28},{28,24},{32,36},... | collective-permute-start | bytes 1179656 | tf_op jit(solution)/shard_map/ppermute | solution.py:470
  86.0 1.9 %add_convert_fusion = bf16[256,768]{1,0:T(8,128)(2,1)} fusion(bf16[256,768]{1,0:T(8,128)(2,1)S(1)} %collective-permute-done.7, bf16[256,768]{1,0:T(8,128)(2,1)} %get-tuple-element.49), kind=kLoop, calls=%fused_computation.8 | loop fusion | flops 786432 | bytes 1179648 | tf_op jit(solution)/shard_map/convert_element_type | solution.py:501
  87.9 6.7 %all-to-all-start.1 = ((bf16[16,16,768]{2,1,0:T(8,128)(2,1)}), bf16[16,16,768]{2,1,0:T(8,128)(2,1)S(1)}, u32[]{:S(2)}, u32[]{:S(2)}) async-start(bf16[16,16,768]{2,1,0:T(8,128)(2,1)} %bitcast.9), calls=%async_computation.1 | async-start | bytes 786432 | tf_op jit(solution)/shard_map/all_to_all | solution.py:467
  96.3 7.6 %all-to-all-done.1.arrived_ref = bf16[16,16,768]{2,1,0:T(8,128)(2,1)S(1)} async-done(((bf16[16,16,768]{2,1,0:T(8,128)(2,1)}), bf16[16,16,768]{2,1,0:T(8,128)(2,1)S(1)}, u32[]{:S(2)}, u32[]{:S(2)}) %all-to-all-start.1) | async-done | bytes 393248 | tf_op jit(solution)/shard_map/all_to_all | solution.py:467
  104.0 11.2 %all_to_all.25 = bf16[16,16,768]{2,1,0:T(8,128)(2,1)S(1)} all-to-all(bf16[16,16,768]{2,1,0:T(8,128)(2,1)S(1)} %combine.2), channel_id=1, replica_groups={{0,8,16,24,32,40,48,56,64,72,80,88,96,104,112,120},{4,12,20,28,36,44,52..., dimensions={0} | all-to-all | bytes 786432 | tf_op jit(solution)/shard_map/all_to_all | solution.py:467
  115.2 3.0 %collective-permute-start.8 = (bf16[256,768]{1,0:T(8,128)(2,1)S(1)}, bf16[256,768]{1,0:T(8,128)(2,1)S(1)}, u32[]{:S(2)}, u32[]{:S(2)}) collective-permute-start(bf16[256,768]{1,0:T(8,128)(2,1)S(1)} %bitcast.25), channel_id=1, source_target_pairs={{0,4},{4,0},{8,12},{12,8},{16,20},{20,16},{24,28},{28,24},{32,36},... | collective-permute-start | bytes 1179656 | tf_op jit(solution)/shard_map/ppermute | solution.py:470
  120.4 8.8 %score_rows.1 = (bf16[512,512]{1,0:T(8,128)(2,1)}, bf16[512,512]{1,0:T(8,128)(2,1)}, bf16[512,512]{1,0:T(8,128)(2,1)}, bf16[512,512]{1,0:T(8,128)(2,1)}, bf16[51...) custom-call(f32[1,4096]{1,0:T(1,128)} %copy-done.20, ...), custom_call_target="tpu_custom_call" | custom-call | flops 1000000 | bytes 1048576 | tf_op jit(solution)/shard_map/score_rows/pallas_call | solution.py:129
  136.0 8.6 %weighted_sums.3 = bf16[16,2,16,768]{3,2,1,0:T(8,128)(2,1)} custom-call(s32[1]{0:T(128)} %bitcast.core_ref, f32[1,4096]{1,0:T(1,128)} %copy-done.20, f32[1,4096]{1,0:T(1,128)} %get-tuple-element.51.rest_0_, f32[1,4096]{1,0:T(1,128)} %copy-done.27, f32[1,4096]{1,0:T(1,128)} %copy-done.26, f32[1,4096]{1,0:T(1,128)} %copy-done.25, ...), custom_call_target="tpu_custom_call" | custom-call | flops 3221225472 | bytes 1048576 | tf_op jit(solution)/shard_map/weighted_sums/pallas_call | solution.py:194
  144.6 5.6 %all-to-all-start.3 = ((bf16[32,16,768]{2,1,0:T(8,128)(2,1)}), bf16[32,16,768]{2,1,0:T(8,128)(2,1)S(1)}, u32[]{:S(2)}, u32[]{:S(2)}) async-start(bf16[32,16,768]{2,1,0:T(8,128)(2,1)} %bitcast.24), calls=%async_computation.3 | async-start | bytes 1572864 | tf_op jit(solution)/shard_map/all_to_all | solution.py:461
  150.2 7.7 %similarity.2 = (bf16[1,2048,2048]{2,1,0:T(8,128)(2,1)}, f32[8,128]{1,0:T(8,128)}) custom-call(s32[1]{0:T(128)} %bitcast.1.depth_ref, bf16[32,4,16,896]{3,2,1,0:T(8,128)(2,1)} %bitcast.5.rest_0_, bf16[32,16,896]{2,1,0:T(8,128)(2,1)} %collective-permute-done.12.refs_1_.rest_1_, bf16[32,16,896]{2,1,0:T(8,128)(2,1)} %copy-done.14, ...), custom_call_target="tpu_custom_call" | custom-call | flops 3758096384 | bytes 1048576 | tf_op jit(solution)/shard_map/similarity/pallas_call | solution.py:417
  157.9 6.5 %all-to-all-done.3.arrived_ref = bf16[32,16,768]{2,1,0:T(8,128)(2,1)S(1)} async-done(((bf16[32,16,768]{2,1,0:T(8,128)(2,1)}), bf16[32,16,768]{2,1,0:T(8,128)(2,1)S(1)}, u32[]{:S(2)}, u32[]{:S(2)}) %all-to-all-start.3) | async-done | bytes 786464 | tf_op jit(solution)/shard_map/all_to_all | solution.py:461
  166.1 3.6 %all-to-all-start.4 = ((bf16[16,16,768]{2,1,0:T(8,128)(2,1)}), bf16[16,16,768]{2,1,0:T(8,128)(2,1)S(1)}, u32[]{:S(2)}, u32[]{:S(2)}) async-start(bf16[16,16,768]{2,1,0:T(8,128)(2,1)} %combine.3), calls=%async_computation.4 | async-start | bytes 786432 | tf_op jit(solution)/shard_map/all_to_all | solution.py:467
  169.6 7.7 %similarity.3 = (bf16[1,2048,2048]{2,1,0:T(8,128)(2,1)}, f32[8,128]{1,0:T(8,128)}) custom-call(s32[1]{0:T(128)} %bitcast.1.depth_ref, bf16[32,4,16,896]{3,2,1,0:T(8,128)(2,1)} %bitcast.5.rest_0_, bf16[32,16,896]{2,1,0:T(8,128)(2,1)} %collective-permute-done.12.refs_1_.rest_1_, bf16[32,16,896]{2,1,0:T(8,128)(2,1)} %copy-done.14, ...), custom_call_target="tpu_custom_call", output_to_operand_aliasing={{0}: (5, {})} | custom-call | flops 3758096384 | bytes 1048576 | tf_op jit(solution)/shard_map/similarity/pallas_call | solution.py:417
  (104 shorter events, 34.7 us)
Async XLA Ops:
  0.6 39.1 %collective-permute-start.1 = (bf16[1024,768]{1,0:T(8,128)(2,1)}, bf16[1024,768]{1,0:T(8,128)(2,1)S(1)}, u32[]{:S(2)}, u32[]{:S(2)}) collective-permute-start(bf16[1024,768]{1,0:T(8,128)(2,1)} %rest_12_.3), channel_id=1, source_target_pairs={{0,1},{1,2},{2,3},{3,0},{4,5},{5,6},{6,7},{7,4},{8,9},{9,10},{10,1... | collective-permute-start | bytes 4718600 | tf_op jit(solution)/shard_map/ppermute | solution.py:456
  3.2 36.7 %collective-permute-start = (bf16[1024,768]{1,0:T(8,128)(2,1)}, bf16[1024,768]{1,0:T(8,128)(2,1)}, u32[]{:S(2)}, u32[]{:S(2)}) collective-permute-start(bf16[1024,768]{1,0:T(8,128)(2,1)} %rest_12_.3), channel_id=1, source_target_pairs={{0,3},{1,0},{2,1},{3,2},{4,7},{5,4},{6,5},{7,6},{8,11},{9,8},{10,9... | collective-permute-start | bytes 4718600 | tf_op jit(solution)/shard_map/ppermute | solution.py:456
  13.8 54.2 %all-to-all-start = ((bf16[32,64,896]{2,1,0:T(8,128)(2,1)}), bf16[32,64,896]{2,1,0:T(8,128)(2,1)}, u32[]{:S(2)}, u32[]{:S(2)}) async-start(bf16[32,64,896]{2,1,0:T(8,128)(2,1)} %bitcast.23), calls=%async_computation | async-start | bytes 7340032 | tf_op jit(solution)/shard_map/all_to_all | solution.py:461
  22.7 21.1 %copy-start.1 = (bf16[1024,768]{1,0:T(8,128)(2,1)S(1)}, bf16[1024,768]{1,0:T(8,128)(2,1)}, u32[]{:S(2)}) copy-start(bf16[1024,768]{1,0:T(8,128)(2,1)} %rest_12_.3) | copy-start | bytes 4718596
  39.8 19.3 %collective-permute-start.2 = (bf16[512,768]{1,0:T(8,128)(2,1)S(1)}, bf16[512,768]{1,0:T(8,128)(2,1)S(1)}, u32[]{:S(2)}, u32[]{:S(2)}) collective-permute-start(bf16[512,768]{1,0:T(8,128)(2,1)S(1)} %slice.20), channel_id=1, source_target_pairs={{0,1},{1,2},{2,3},{3,0},{4,5},{5,6},{6,7},{7,4},{8,9},{9,10},{10,1... | collective-permute-start | bytes 2359304 | tf_op jit(solution)/shard_map/ppermute | solution.py:456
  41.5 18.1 %collective-permute-start.3 = (bf16[512,768]{1,0:T(8,128)(2,1)S(1)}, bf16[512,768]{1,0:T(8,128)(2,1)S(1)}, u32[]{:S(2)}, u32[]{:S(2)}) collective-permute-start(bf16[512,768]{1,0:T(8,128)(2,1)S(1)} %slice.21), channel_id=1, source_target_pairs={{0,3},{1,0},{2,1},{3,2},{4,7},{5,4},{6,5},{7,6},{8,11},{9,8},{10,9... | collective-permute-start | bytes 2359304 | tf_op jit(solution)/shard_map/ppermute | solution.py:456
  47.1 13.7 %copy-start.6 = (bf16[512,512]{1,0:T(8,128)(2,1)}, bf16[512,512]{1,0:T(8,128)(2,1)S(1)}, u32[]{:S(2)}) copy-start(bf16[512,512]{1,0:T(8,128)(2,1)S(1)} %get-tuple-element.47.rest_10_) | copy-start | bytes 1572868
  47.1 13.7 %copy-start.7 = (bf16[512,512]{1,0:T(8,128)(2,1)}, bf16[512,512]{1,0:T(8,128)(2,1)S(1)}, u32[]{:S(2)}) copy-start(bf16[512,512]{1,0:T(8,128)(2,1)S(1)} %get-tuple-element.48.rest_11_) | copy-start | bytes 1572868
  62.5 8.4 %copy-start.21 = (f32[1,4096]{1,0:T(1,128)}, f32[1,4096]{1,0:T(1,128)S(1)}, u32[]{:S(2)}) copy-start(f32[1,4096]{1,0:T(1,128)S(1)} %constant_dynamic-update-slice_fusion.4.rest_0_) | copy-start | bytes 49156
  62.5 10.2 %collective-permute-start.6 = (f32[1,4096]{1,0:T(1,128)S(1)}, f32[1,4096]{1,0:T(1,128)S(1)}, u32[]{:S(2)}, u32[]{:S(2)}) collective-permute-start(f32[1,4096]{1,0:T(1,128)S(1)} %constant_dynamic-update-slice_fusion.4.rest_0_), channel_id=1, source_target_pairs={{0,1},{1,2},{2,3},{3,0},{4,5},{5,6},{6,7},{7,4},{8,9},{9,10},{10,1... | collective-permute-start | bytes 49160 | tf_op jit(solution)/shard_map/ppermute | solution.py:456
  62.6 10.1 %collective-permute-start.5 = (f32[1,4096]{1,0:T(1,128)S(1)}, f32[1,4096]{1,0:T(1,128)S(1)}, u32[]{:S(2)}, u32[]{:S(2)}) collective-permute-start(f32[1,4096]{1,0:T(1,128)S(1)} %constant_dynamic-update-slice_fusion.4.rest_0_), channel_id=1, source_target_pairs={{0,2},{1,3},{2,0},{3,1},{4,6},{5,7},{6,4},{7,5},{8,10},{9,11},{10,... | collective-permute-start | bytes 49160 | tf_op jit(solution)/shard_map/ppermute | solution.py:456
  66.8 5.9 %collective-permute-start.4 = (f32[1,4096]{1,0:T(1,128)S(1)}, f32[1,4096]{1,0:T(1,128)S(1)}, u32[]{:S(2)}, u32[]{:S(2)}) collective-permute-start(f32[1,4096]{1,0:T(1,128)S(1)} %constant_dynamic-update-slice_fusion.4.rest_0_), channel_id=1, source_target_pairs={{0,3},{1,0},{2,1},{3,2},{4,7},{5,4},{6,5},{7,6},{8,11},{9,8},{10,9... | collective-permute-start | bytes 49160 | tf_op jit(solution)/shard_map/ppermute | solution.py:456
  71.0 23.6 %collective-permute-start.13 = (bf16[32,16,896]{2,1,0:T(8,128)(2,1)S(1)}, bf16[32,16,896]{2,1,0:T(8,128)(2,1)}, u32[]{:S(2)}, u32[]{:S(2)}) collective-permute-start(bf16[32,16,896]{2,1,0:T(8,128)(2,1)S(1)} %get-tuple-element.64.rest_19_), channel_id=1, source_target_pairs={{0,3},{1,0},{2,1},{3,2},{4,7},{5,4},{6,5},{7,6},{8,11},{9,8},{10,9... | collective-permute-start | bytes 2752520 | tf_op jit(solution)/shard_map/ppermute | solution.py:456
  72.7 22.0 %collective-permute-start.12 = (bf16[32,16,896]{2,1,0:T(8,128)(2,1)S(1)}, bf16[32,16,896]{2,1,0:T(8,128)(2,1)}, u32[]{:S(2)}, u32[]{:S(2)}) collective-permute-start(bf16[32,16,896]{2,1,0:T(8,128)(2,1)S(1)} %get-tuple-element.66.rest_17_), channel_id=1, source_target_pairs={{0,1},{1,2},{2,3},{3,0},{4,5},{5,6},{6,7},{7,4},{8,9},{9,10},{10,1... | collective-permute-start | bytes 2752520 | tf_op jit(solution)/shard_map/ppermute | solution.py:456
  82.1 3.9 %collective-permute-start.7 = (bf16[256,768]{1,0:T(8,128)(2,1)}, bf16[256,768]{1,0:T(8,128)(2,1)S(1)}, u32[]{:S(2)}, u32[]{:S(2)}) collective-permute-start(bf16[256,768]{1,0:T(8,128)(2,1)} %get-tuple-element.50), channel_id=1, source_target_pairs={{0,4},{4,0},{8,12},{12,8},{16,20},{20,16},{24,28},{28,24},{32,36},... | collective-permute-start | bytes 1179656 | tf_op jit(solution)/shard_map/ppermute | solution.py:470
  87.9 16.0 %all-to-all-start.1 = ((bf16[16,16,768]{2,1,0:T(8,128)(2,1)}), bf16[16,16,768]{2,1,0:T(8,128)(2,1)S(1)}, u32[]{:S(2)}, u32[]{:S(2)}) async-start(bf16[16,16,768]{2,1,0:T(8,128)(2,1)} %bitcast.9), calls=%async_computation.1 | async-start | bytes 786432 | tf_op jit(solution)/shard_map/all_to_all | solution.py:467
  94.7 40.3 %collective-permute-start.14 = (bf16[32,16,896]{2,1,0:T(8,128)(2,1)}, bf16[32,16,896]{2,1,0:T(8,128)(2,1)S(1)}, u32[]{:S(2)}, u32[]{:S(2)}) collective-permute-start(bf16[32,16,896]{2,1,0:T(8,128)(2,1)} %order.1), channel_id=1, source_target_pairs={{0,2},{1,3},{2,0},{3,1},{4,6},{5,7},{6,4},{7,5},{8,10},{9,11},{10,... | collective-permute-start | bytes 2752520 | tf_op jit(solution)/shard_map/ppermute | solution.py:456
  115.2 4.3 %collective-permute-start.8 = (bf16[256,768]{1,0:T(8,128)(2,1)S(1)}, bf16[256,768]{1,0:T(8,128)(2,1)S(1)}, u32[]{:S(2)}, u32[]{:S(2)}) collective-permute-start(bf16[256,768]{1,0:T(8,128)(2,1)S(1)} %bitcast.25), channel_id=1, source_target_pairs={{0,4},{4,0},{8,12},{12,8},{16,20},{20,16},{24,28},{28,24},{32,36},... | collective-permute-start | bytes 1179656 | tf_op jit(solution)/shard_map/ppermute | solution.py:470
  129.1 4.1 %collective-permute-start.11 = (f32[1,4096]{1,0:T(1,128)}, f32[1,4096]{1,0:T(1,128)S(1)}, u32[]{:S(2)}, u32[]{:S(2)}) collective-permute-start(f32[1,4096]{1,0:T(1,128)} %get-tuple-element.51.rest_0_), channel_id=1, source_target_pairs={{0,1},{1,2},{2,3},{3,0},{4,5},{5,6},{6,7},{7,4},{8,9},{9,10},{10,1... | collective-permute-start | bytes 49160 | tf_op jit(solution)/shard_map/ppermute | solution.py:456
  130.7 4.3 %collective-permute-start.10 = (f32[1,4096]{1,0:T(1,128)}, f32[1,4096]{1,0:T(1,128)S(1)}, u32[]{:S(2)}, u32[]{:S(2)}) collective-permute-start(f32[1,4096]{1,0:T(1,128)} %get-tuple-element.51.rest_0_), channel_id=1, source_target_pairs={{0,2},{1,3},{2,0},{3,1},{4,6},{5,7},{6,4},{7,5},{8,10},{9,11},{10,... | collective-permute-start | bytes 49160 | tf_op jit(solution)/shard_map/ppermute | solution.py:456
  131.6 3.4 %collective-permute-start.9 = (f32[1,4096]{1,0:T(1,128)}, f32[1,4096]{1,0:T(1,128)S(1)}, u32[]{:S(2)}, u32[]{:S(2)}) collective-permute-start(f32[1,4096]{1,0:T(1,128)} %get-tuple-element.51.rest_0_), channel_id=1, source_target_pairs={{0,3},{1,0},{2,1},{3,2},{4,7},{5,4},{6,5},{7,6},{8,11},{9,8},{10,9... | collective-permute-start | bytes 49160 | tf_op jit(solution)/shard_map/ppermute | solution.py:456
  144.6 19.8 %all-to-all-start.3 = ((bf16[32,16,768]{2,1,0:T(8,128)(2,1)}), bf16[32,16,768]{2,1,0:T(8,128)(2,1)S(1)}, u32[]{:S(2)}, u32[]{:S(2)}) async-start(bf16[32,16,768]{2,1,0:T(8,128)(2,1)} %bitcast.24), calls=%async_computation.3 | async-start | bytes 1572864 | tf_op jit(solution)/shard_map/all_to_all | solution.py:461
  166.1 12.8 %all-to-all-start.4 = ((bf16[16,16,768]{2,1,0:T(8,128)(2,1)}), bf16[16,16,768]{2,1,0:T(8,128)(2,1)S(1)}, u32[]{:S(2)}, u32[]{:S(2)}) async-start(bf16[16,16,768]{2,1,0:T(8,128)(2,1)} %combine.3), calls=%async_computation.4 | async-start | bytes 786432 | tf_op jit(solution)/shard_map/all_to_all | solution.py:467
  179.5 2.9 %collective-permute-start.15 = (bf16[256,768]{1,0:T(8,128)(2,1)S(1)}, bf16[256,768]{1,0:T(8,128)(2,1)S(1)}, u32[]{:S(2)}, u32[]{:S(2)}) collective-permute-start(bf16[256,768]{1,0:T(8,128)(2,1)S(1)} %hold.1.own_ref), channel_id=1, source_target_pairs={{0,4},{4,0},{8,12},{12,8},{16,20},{20,16},{24,28},{28,24},{32,36},... | collective-permute-start | bytes 1179656 | tf_op jit(solution)/shard_map/ppermute | solution.py:470
  (24 other events, 45.9 us)

commit v6 on v5

--- a/solution.py
+++ b/solution.py
@@ -60,10 +60,9 @@
     return membership.astype(jnp.bfloat16), jnp.sum(membership, axis=0, keepdims=True)
 
 
-def piece_kernel(sources, block_ref, *rest):
+def piece_kernel(sources, size, block_ref, *rest):
     raw_refs, member_refs = rest[:sources], rest[sources:-2]
     total_ref, scale_ref = rest[-2:]
-    size = member_refs[0].shape[1]
     parts = [(ref, at) for ref in raw_refs for at in range(0, ref.shape[0], size)]
     for i, (ref, start) in enumerate(parts):
         raw = ref[start : start + size]
@@ -72,16 +71,18 @@
         squares = jnp.sum(wide * wide, axis=-1, keepdims=True) + epsilon
         scale = (1.0 / jnp.sqrt(jnp.broadcast_to(squares, (size, 8)))).T[:1]
         scale_ref[:, at] = scale
-        member_refs[i][...], total_ref[:, at] = membership_of(block_ref[...], raw, scale)
-
-
-def score_piece(raws, block, size, cost):
+        member, total_ref[:, at] = membership_of(block_ref[...], raw, scale)
+        if member_refs:
+            member_refs[i][...] = member
+
+
+def score_piece(raws, block, size, cost, keep):
     rows = sum(raw.shape[0] for raw in raws)
     count = block.shape[0]
     line = jax.ShapeDtypeStruct((1, rows), jnp.float32)
-    pieces = rows // size
-    return call(
-        functools.partial(piece_kernel, len(raws)),
+    pieces = rows // size if keep else 0
+    return call(
+        functools.partial(piece_kernel, len(raws), size),
         "score_piece",
         12,
         cost,
@@ -146,15 +147,18 @@
     return out[:pieces], out[pieces]
 
 
-def sum_kernel(pieces, depth, source_count, outs, core_ref, scale_ref, *rest):
+def sum_kernel(held, depth, source_count, outs, core_ref, scale_ref, block_ref, *rest):
+    pieces = len(held)
     total_refs, rest = rest[:depth], rest[depth:]
     *rest, members, taken, running, member_sem, row_sem = rest
     out_refs = rest[-outs:]
-    member_refs, sources = rest[:pieces], rest[pieces : pieces + source_count]
+    member_refs, sources = iter(rest[: sum(held)]), rest[sum(held) : sum(held) + source_count]
     half = running.shape[0] // 2
     size = members.shape[2]
     arriving = [
-        (rows, pltpu.make_async_copy(member_refs[i], members.at[i], member_sem.at[i]))
+        (rows, pltpu.make_async_copy(next(member_refs), members.at[i], member_sem.at[i]))
+        if held[i]
+        else (rows,)
         for i, rows in enumerate(fetches(sources, size, taken, row_sem))
     ]
     for pair in arriving:
@@ -168,7 +172,11 @@
         for k in range(1, depth):
             j = (i + pieces - k * (pieces // depth)) % pieces
             total = total + total_refs[k][:, j * size : (j + 1) * size]
-        weights = members[i].astype(jnp.float32) * (scale_ref[:, at] / total)
+        if held[i]:
+            member = members[i]
+        else:
+            member, _ = membership_of(block_ref[...], taken[at], scale_ref[:, at])
+        weights = member.astype(jnp.float32) * (scale_ref[:, at] / total)
         product = jnp.dot(
             weights.astype(jnp.bfloat16), taken[at], preferred_element_type=jnp.float32
         )
@@ -185,20 +193,21 @@
         out_refs[0][:, 1 - core_ref[0]] = other.reshape(chips, share, width)
 
 
-def weighted_sums(members, sources, scale, totals, core, chips, after):
+def weighted_sums(members, sources, scale, totals, block, core, chips, after):
     pieces = len(members)
     count, size = members[0].shape
     width = sources[0].shape[1]
+    held = tuple(member is not None for member in members)
     half = count // 2
     shapes = [(chips, 2, half // chips, width)] if chips else [(half, width)] * 2
     return call(
-        functools.partial(sum_kernel, pieces, len(totals), len(sources), len(shapes)),
+        functools.partial(sum_kernel, held, len(totals), len(sources), len(shapes)),
         "weighted_sums",
         FULL,
         2 * pieces * size * width * count,
         in_specs=[pl.BlockSpec(memory_space=pltpu.SMEM)]
-        + [whole()] * (1 + len(totals))
-        + [in_hbm()] * (pieces + len(sources))
+        + [whole()] * (2 + len(totals))
+        + [in_hbm()] * (sum(held) + len(sources))
         + [in_hbm()] * len(after),
         out_specs=[whole()] * len(shapes),
         out_shape=[jax.ShapeDtypeStruct(shape, jnp.bfloat16) for shape in shapes],
@@ -209,7 +218,15 @@
             pltpu.SemaphoreType.DMA((pieces,)),
             pltpu.SemaphoreType.DMA((pieces,)),
         ],
-    )(core.reshape(1).astype(jnp.int32), scale, *totals, *members, *sources, *after)
+    )(
+        core.reshape(1).astype(jnp.int32),
+        scale,
+        block,
+        *totals,
+        *[member for member in members if member is not None],
+        *sources,
+        *after,
+    )
 
 
 def combine_kernel(arrived_ref, *rest):
@@ -483,21 +500,21 @@
     other_half = lax.dynamic_slice_in_dim(initial, (1 - core) * half, half, 0)
     block = jnp.concatenate([own_half, other_half])
     scored = [
-        score_piece(raws, block, cut, cost)
-        for raws, cost in [
-            ([embeddings], OWN_COST),
-            ([above], NEAR_COST),
-            ([far_first, far_second], FAR_COST),
-            ([below], NEAR_COST),
+        score_piece(raws, block, cut, cost, keep)
+        for raws, cost, keep in [
+            ([embeddings], OWN_COST, True),
+            ([above], NEAR_COST, True),
+            ([far_first, far_second], FAR_COST, False),
+            ([below], NEAR_COST, True),
         ]
     ]
-    members = [member for *parts, _, _ in scored for member in parts]
+    members = [member for *parts, _, _ in scored for member in parts or [None, None]]
     partial_total = jnp.concatenate([total for *_, total, _ in scored], axis=1)
     scale = jnp.concatenate([scale for *_, scale in scored], axis=1)
 
     totals = [partial_total] + [send(partial_total, -k) for k in range(1, cent_count)]
     parted = [routed[:, k] for k in range(cent_count)]
-    own, for_sibling = weighted_sums(members, sources, scale, totals, core, 0, parted[1:])
+    own, for_sibling = weighted_sums(members, sources, scale, totals, block, core, 0, parted[1:])
     both = (own.astype(jnp.float32) + swap_cores(for_sibling).astype(jnp.float32)).astype(jnp.bfloat16)
     arrived = exchange_plane(both.reshape(planes, share, feature_width))
 
@@ -507,7 +524,7 @@
     own_half = exchange_plane(combine(arrived, planes, [])).reshape(half, feature_width)
     members, partial_total = score_rows(sources, scale, own_half, swap_cores(own_half), cut)
     totals = [partial_total] + [send(partial_total, -k) for k in range(1, cent_count)]
-    (sums,) = weighted_sums(members, sources, scale, totals, core, planes, [blocks[2]])
+    (sums,) = weighted_sums(members, sources, scale, totals, own_half, core, planes, [blocks[2]])
     arrived = exchange(sums.reshape(dp_count, share, feature_width))
     similarity, upper = similarity_of(blocks, depth, 0, 2, None)
     spread = combine(arrived, planes, [upper])

time: 185 us -> 185 us (level)
  waiting for transfers between devices: 47.8 us -> 50.6 us
  starting transfers between devices: 49.7 us -> 47.6 us
    unnamed x61 -> x59, local copies, waits for them, and re-layouts: 7.9 us -> 6.25 us
  transfers between devices with their start and end apart: 20 -> 20, of which waited for: 12 -> 13; matrix products, arithmetic and copies ran while one was open for 4% -> 4% of each run, Pallas kernels for 26% -> 27%
where the time goes in v6:
time: 185 us; the launch traced here: 184 us
  Pallas kernels  60.4 us (33%)
  waiting for transfers between devices  50.6 us (27%)
  starting transfers between devices  47.6 us (26%)
  blocking collectives  11.2 us (6%)
  local copies, waits for them, and re-layouts  10.9 us (6%)
  other arithmetic  2.37 us (1%)
    ppermute x13, waiting for transfers between devices, send(): lax.ppermute(value, 'cent', [(z, (z + step) % cent_count) for z in range(...  27.9 us
    pallas_call x2, Pallas kernels, weighted_sums(): call(functools.partial(sum_kernel, held, len(totals), len(sources), len(s...  18.6 us
    ppermute x13, starting transfers between devices, send(): lax.ppermute(value, 'cent', [(z, (z + step) % cent_count) for z in range(...  18.2 us
    pallas_call x2, Pallas kernels, similarity_of(): call(functools.partial(similarity_kernel, cent_count, part * steps), 'sim...  15.4 us
    all_to_all x2, starting transfers between devices, exchange(): return lax.all_to_all(value, 'dp', 0, 0, tiled=True)  13.8 us
    all_to_all x1, blocking collectives, exchange_plane(): lax.all_to_all(value, 'dp', 0, 0, axis_index_groups=same_core, tiled=True)  11.2 us
    all_to_all x2, starting transfers between devices, exchange_plane(): lax.all_to_all(value, 'dp', 0, 0, axis_index_groups=same_core, tiled=True)  9.77 us
    all_to_all x2, waiting for transfers between devices, exchange(): return lax.all_to_all(value, 'dp', 0, 0, tiled=True)  9.32 us
  transfers between devices with their start and end apart: 20, of which 13 were waited for; matrix products, arithmetic and copies ran while one was open for 4% of the time, Pallas kernels for 27%

profile of v6, /device:TPU:1, one launch (start us, length us, event | category | flops | bytes accessed | tf_op | source)
XLA Modules:
  0.0 184.1 jit_solution(16890137298086927974)
XLA Ops:
  0.6 2.5 %collective-permute-start.1 = (bf16[1024,768]{1,0:T(8,128)(2,1)}, bf16[1024,768]{1,0:T(8,128)(2,1)S(1)}, u32[]{:S(2)}, u32[]{:S(2)}) collective-permute-start(bf16[1024,768]{1,0:T(8,128)(2,1)} %rest_12_.1), channel_id=1, source_target_pairs={{0,1},{1,2},{2,3},{3,0},{4,5},{5,6},{6,7},{7,4},{8,9},{9,10},{10,1... | collective-permute-start | bytes 4718600 | tf_op jit(solution)/shard_map/ppermute | solution.py:473
  3.2 2.2 %collective-permute-start = (bf16[1024,768]{1,0:T(8,128)(2,1)}, bf16[1024,768]{1,0:T(8,128)(2,1)}, u32[]{:S(2)}, u32[]{:S(2)}) collective-permute-start(bf16[1024,768]{1,0:T(8,128)(2,1)} %rest_12_.1), channel_id=1, source_target_pairs={{0,3},{1,0},{2,1},{3,2},{4,7},{5,4},{6,5},{7,6},{8,11},{9,8},{10,9... | collective-permute-start | bytes 4718600 | tf_op jit(solution)/shard_map/ppermute | solution.py:473
  5.4 8.5 %pack.1 = bf16[2048,896]{1,0:T(8,128)(2,1)} custom-call(s32[1]{0:T(128)} %bitcast.1.depth_ref, bf16[1024,768]{1,0:T(8,128)(2,1)} %rest_12_.1, s32[1,1024]{1,0:T(1,128)} %bitcast.29, s32[16,128]{1,0:T(8,128)} %bitcast.28), custom_call_target="tpu_custom_call" | custom-call | flops 3221225472 | bytes 1048576 | tf_op jit(solution)/shard_map/pack/pallas_call | solution.py:331
  13.8 8.2 %all-to-all-start = ((bf16[32,64,896]{2,1,0:T(8,128)(2,1)}), bf16[32,64,896]{2,1,0:T(8,128)(2,1)}, u32[]{:S(2)}, u32[]{:S(2)}) async-start(bf16[32,64,896]{2,1,0:T(8,128)(2,1)} %bitcast.23), calls=%async_computation | async-start | bytes 7340032 | tf_op jit(solution)/shard_map/all_to_all | solution.py:478
  22.7 17.0 %collective-permute-done.1.rest_0_.rest_14_.rest_4_.rest_16_ = bf16[1024,768]{1,0:T(8,128)(2,1)S(1)} collective-permute-done((bf16[1024,768]{1,0:T(8,128)(2,1)}, bf16[1024,768]{1,0:T(8,128)(2,1)S(1)}, u32[]{:S(2)}, u32[]{:S(2)}) %collective-permute-start.1) | collective-permute-done | bytes 1572896 | tf_op jit(solution)/shard_map/ppermute | solution.py:473
  41.5 2.3 %collective-permute-start.3 = (bf16[512,768]{1,0:T(8,128)(2,1)S(1)}, bf16[512,768]{1,0:T(8,128)(2,1)S(1)}, u32[]{:S(2)}, u32[]{:S(2)}) collective-permute-start(bf16[512,768]{1,0:T(8,128)(2,1)S(1)} %slice.21), channel_id=1, source_target_pairs={{0,3},{1,0},{2,1},{3,2},{4,7},{5,4},{6,5},{7,6},{8,11},{9,8},{10,9... | collective-permute-start | bytes 2359304 | tf_op jit(solution)/shard_map/ppermute | solution.py:473
  48.0 3.0 %score_piece.5 = (bf16[512,512]{1,0:T(8,128)(2,1)S(1)}, bf16[512,512]{1,0:T(8,128)(2,1)S(1)}, f32[1,1024]{1,0:T(1,128)S(1)}, f32[1,1024]{1,0:T(1,128)S(1)}) custom-call(bf16[512,768]{1,0:T(8,128)(2,1)S(1)} %pad_maximum_fusion.block_ref, bf16[1024,768]{1,0:T(8,128)(2,1)} %collective-permute-done.rest_0_.rest_11_.rest_1_.rest_13_), custom_call_target="tpu_custom_call" | custom-call | flops 1000000 | bytes 1048576 | tf_op jit(solution)/shard_map/score_piece/pallas_call | solution.py:84
  51.8 7.3 %collective-permute-done.2.rest_0_.rest_12_.rest_2_.rest_14_ = bf16[512,768]{1,0:T(8,128)(2,1)S(1)} collective-permute-done((bf16[512,768]{1,0:T(8,128)(2,1)S(1)}, bf16[512,768]{1,0:T(8,128)(2,1)S(1)}, u32[]{:S(2)}, u32[]{:S(2)}) %collective-permute-start.2) | collective-permute-done | bytes 786464 | tf_op jit(solution)/shard_map/ppermute | solution.py:473
  61.0 4.2 %collective-permute-start.5 = (f32[1,4096]{1,0:T(1,128)S(1)}, f32[1,4096]{1,0:T(1,128)S(1)}, u32[]{:S(2)}, u32[]{:S(2)}) collective-permute-start(f32[1,4096]{1,0:T(1,128)S(1)} %constant_dynamic-update-slice_fusion.4.rest_0_), channel_id=1, source_target_pairs={{0,2},{1,3},{2,0},{3,1},{4,6},{5,7},{6,4},{7,5},{8,10},{9,11},{10,... | collective-permute-start | bytes 49160 | tf_op jit(solution)/shard_map/ppermute | solution.py:473
  65.2 2.8 %all-to-all-done = bf16[32,64,896]{2,1,0:T(8,128)(2,1)} async-done(((bf16[32,64,896]{2,1,0:T(8,128)(2,1)}), bf16[32,64,896]{2,1,0:T(8,128)(2,1)}, u32[]{:S(2)}, u32[]{:S(2)}) %all-to-all-start) | async-done | bytes 3670048 | tf_op jit(solution)/shard_map/all_to_all | solution.py:478
  68.1 2.9 %slice_bitcast_fusion = (bf16[32,16,896]{2,1,0:T(8,128)(2,1)S(1)}, bf16[32,16,896]{2,1,0:T(8,128)(2,1)}, bf16[32,16,896]{2,1,0:T(8,128)(2,1)S(1)}) fusion(bf16[32,4,16,896]{3,2,1,0:T(8,128)(2,1)} %bitcast.5.rest_0_), kind=kLoop, calls=%fused_computation.4 | loop fusion | bytes 5505024 | tf_op jit(solution)/shard_map/squeeze | solution.py:516
  73.4 9.8 %weighted_sums.2 = (bf16[256,768]{1,0:T(8,128)(2,1)}, bf16[256,768]{1,0:T(8,128)(2,1)}) custom-call(s32[1]{0:T(128)} %bitcast.core_ref, f32[1,4096]{1,0:T(1,128)} %copy-done.19, bf16[512,768]{1,0:T(8,128)(2,1)} %copy-done.2, f32[1,4096]{1,0:T(1,128)} %copy-done.20, f32[1,4096]{1,0:T(1,128)} %copy-done.23, f32[1,4096]{1,0:T(1,128)} %copy-done.22, ...), custom_call_target="tpu_custom_call" | custom-call | flops 3221225472 | bytes 1048576 | tf_op jit(solution)/shard_map/weighted_sums/pallas_call | solution.py:203
  87.9 6.2 %all-to-all-start.1 = ((bf16[16,16,768]{2,1,0:T(8,128)(2,1)}), bf16[16,16,768]{2,1,0:T(8,128)(2,1)S(1)}, u32[]{:S(2)}, u32[]{:S(2)}) async-start(bf16[16,16,768]{2,1,0:T(8,128)(2,1)} %bitcast.9), calls=%async_computation.1 | async-start | bytes 786432 | tf_op jit(solution)/shard_map/all_to_all | solution.py:484
  95.8 7.6 %all-to-all-done.1.arrived_ref = bf16[16,16,768]{2,1,0:T(8,128)(2,1)S(1)} async-done(((bf16[16,16,768]{2,1,0:T(8,128)(2,1)}), bf16[16,16,768]{2,1,0:T(8,128)(2,1)S(1)}, u32[]{:S(2)}, u32[]{:S(2)}) %all-to-all-start.1) | async-done | bytes 393248 | tf_op jit(solution)/shard_map/all_to_all | solution.py:484
  103.5 11.2 %all_to_all.25 = bf16[16,16,768]{2,1,0:T(8,128)(2,1)S(1)} all-to-all(bf16[16,16,768]{2,1,0:T(8,128)(2,1)S(1)} %combine.2), channel_id=1, replica_groups={{0,8,16,24,32,40,48,56,64,72,80,88,96,104,112,120},{4,12,20,28,36,44,52..., dimensions={0} | all-to-all | bytes 786432 | tf_op jit(solution)/shard_map/all_to_all | solution.py:484
  114.8 3.0 %collective-permute-start.8 = (bf16[256,768]{1,0:T(8,128)(2,1)S(1)}, bf16[256,768]{1,0:T(8,128)(2,1)S(1)}, u32[]{:S(2)}, u32[]{:S(2)}) collective-permute-start(bf16[256,768]{1,0:T(8,128)(2,1)S(1)} %bitcast.24), channel_id=1, source_target_pairs={{0,4},{4,0},{8,12},{12,8},{16,20},{20,16},{24,28},{28,24},{32,36},... | collective-permute-start | bytes 1179656 | tf_op jit(solution)/shard_map/ppermute | solution.py:487
  119.9 8.8 %score_rows.1 = (bf16[512,512]{1,0:T(8,128)(2,1)}, bf16[512,512]{1,0:T(8,128)(2,1)}, bf16[512,512]{1,0:T(8,128)(2,1)}, bf16[512,512]{1,0:T(8,128)(2,1)}, bf16[51...) custom-call(f32[1,4096]{1,0:T(1,128)} %copy-done.19, ...), custom_call_target="tpu_custom_call" | custom-call | flops 1000000 | bytes 1048576 | tf_op jit(solution)/shard_map/score_rows/pallas_call | solution.py:130
  130.2 1.9 %collective-permute-start.10 = (f32[1,4096]{1,0:T(1,128)}, f32[1,4096]{1,0:T(1,128)S(1)}, u32[]{:S(2)}, u32[]{:S(2)}) collective-permute-start(f32[1,4096]{1,0:T(1,128)} %get-tuple-element.47.rest_0_), channel_id=1, source_target_pairs={{0,2},{1,3},{2,0},{3,1},{4,6},{5,7},{6,4},{7,5},{8,10},{9,11},{10,... | collective-permute-start | bytes 49160 | tf_op jit(solution)/shard_map/ppermute | solution.py:473
  136.2 8.8 %weighted_sums.3 = bf16[16,2,16,768]{3,2,1,0:T(8,128)(2,1)} custom-call(s32[1]{0:T(128)} %bitcast.core_ref, f32[1,4096]{1,0:T(1,128)} %copy-done.19, bf16[256,768]{1,0:T(8,128)(2,1)} %bitcast.26, f32[1,4096]{1,0:T(1,128)} %get-tuple-element.47.rest_0_, f32[1,4096]{1,0:T(1,128)} %copy-done.26, f32[1,4096]{1,0:T(1,128)} %copy-done.25, f32[1,4096]{1,0:T(1,128)} %copy-done.24, ...), custom_call_target="tpu_custom_call" | custom-call | flops 3221225472 | bytes 1048576 | tf_op jit(solution)/shard_map/weighted_sums/pallas_call | solution.py:203
  145.0 5.6 %all-to-all-start.3 = ((bf16[32,16,768]{2,1,0:T(8,128)(2,1)}), bf16[32,16,768]{2,1,0:T(8,128)(2,1)S(1)}, u32[]{:S(2)}, u32[]{:S(2)}) async-start(bf16[32,16,768]{2,1,0:T(8,128)(2,1)} %bitcast.27), calls=%async_computation.3 | async-start | bytes 1572864 | tf_op jit(solution)/shard_map/all_to_all | solution.py:478
  150.5 7.7 %similarity.2 = (bf16[1,2048,2048]{2,1,0:T(8,128)(2,1)}, f32[8,128]{1,0:T(8,128)}) custom-call(s32[1]{0:T(128)} %bitcast.1.depth_ref, bf16[32,4,16,896]{3,2,1,0:T(8,128)(2,1)} %bitcast.5.rest_0_, bf16[32,16,896]{2,1,0:T(8,128)(2,1)} %collective-permute-done.12.refs_1_.rest_1_, bf16[32,16,896]{2,1,0:T(8,128)(2,1)} %copy-done.13, ...), custom_call_target="tpu_custom_call" | custom-call | flops 3758096384 | bytes 1048576 | tf_op jit(solution)/shard_map/similarity/pallas_call | solution.py:434
  158.3 6.5 %all-to-all-done.3.arrived_ref = bf16[32,16,768]{2,1,0:T(8,128)(2,1)S(1)} async-done(((bf16[32,16,768]{2,1,0:T(8,128)(2,1)}), bf16[32,16,768]{2,1,0:T(8,128)(2,1)S(1)}, u32[]{:S(2)}, u32[]{:S(2)}) %all-to-all-start.3) | async-done | bytes 786464 | tf_op jit(solution)/shard_map/all_to_all | solution.py:478
  166.4 3.6 %all-to-all-start.4 = ((bf16[16,16,768]{2,1,0:T(8,128)(2,1)}), bf16[16,16,768]{2,1,0:T(8,128)(2,1)S(1)}, u32[]{:S(2)}, u32[]{:S(2)}) async-start(bf16[16,16,768]{2,1,0:T(8,128)(2,1)} %combine.3), calls=%async_computation.4 | async-start | bytes 786432 | tf_op jit(solution)/shard_map/all_to_all | solution.py:484
  170.0 7.7 %similarity.3 = (bf16[1,2048,2048]{2,1,0:T(8,128)(2,1)}, f32[8,128]{1,0:T(8,128)}) custom-call(s32[1]{0:T(128)} %bitcast.1.depth_ref, bf16[32,4,16,896]{3,2,1,0:T(8,128)(2,1)} %bitcast.5.rest_0_, bf16[32,16,896]{2,1,0:T(8,128)(2,1)} %collective-permute-done.12.refs_1_.rest_1_, bf16[32,16,896]{2,1,0:T(8,128)(2,1)} %copy-done.13, ...), custom_call_target="tpu_custom_call", output_to_operand_aliasing={{0}: (5, {})} | custom-call | flops 3758096384 | bytes 1048576 | tf_op jit(solution)/shard_map/similarity/pallas_call | solution.py:434
  (102 shorter events, 33.8 us)
Async XLA Ops:
  0.6 39.1 %collective-permute-start.1 = (bf16[1024,768]{1,0:T(8,128)(2,1)}, bf16[1024,768]{1,0:T(8,128)(2,1)S(1)}, u32[]{:S(2)}, u32[]{:S(2)}) collective-permute-start(bf16[1024,768]{1,0:T(8,128)(2,1)} %rest_12_.1), channel_id=1, source_target_pairs={{0,1},{1,2},{2,3},{3,0},{4,5},{5,6},{6,7},{7,4},{8,9},{9,10},{10,1... | collective-permute-start | bytes 4718600 | tf_op jit(solution)/shard_map/ppermute | solution.py:473
  3.2 36.7 %collective-permute-start = (bf16[1024,768]{1,0:T(8,128)(2,1)}, bf16[1024,768]{1,0:T(8,128)(2,1)}, u32[]{:S(2)}, u32[]{:S(2)}) collective-permute-start(bf16[1024,768]{1,0:T(8,128)(2,1)} %rest_12_.1), channel_id=1, source_target_pairs={{0,3},{1,0},{2,1},{3,2},{4,7},{5,4},{6,5},{7,6},{8,11},{9,8},{10,9... | collective-permute-start | bytes 4718600 | tf_op jit(solution)/shard_map/ppermute | solution.py:473
  13.8 54.2 %all-to-all-start = ((bf16[32,64,896]{2,1,0:T(8,128)(2,1)}), bf16[32,64,896]{2,1,0:T(8,128)(2,1)}, u32[]{:S(2)}, u32[]{:S(2)}) async-start(bf16[32,64,896]{2,1,0:T(8,128)(2,1)} %bitcast.23), calls=%async_computation | async-start | bytes 7340032 | tf_op jit(solution)/shard_map/all_to_all | solution.py:478
  22.7 36.9 %copy-start.2 = (bf16[512,768]{1,0:T(8,128)(2,1)}, bf16[512,768]{1,0:T(8,128)(2,1)S(1)}, u32[]{:S(2)}) copy-start(bf16[512,768]{1,0:T(8,128)(2,1)S(1)} %pad_maximum_fusion.block_ref) | copy-start | bytes 2359300
  22.7 21.1 %copy-start.1 = (bf16[1024,768]{1,0:T(8,128)(2,1)S(1)}, bf16[1024,768]{1,0:T(8,128)(2,1)}, u32[]{:S(2)}) copy-start(bf16[1024,768]{1,0:T(8,128)(2,1)} %rest_12_.1) | copy-start | bytes 4718596
  39.8 19.3 %collective-permute-start.2 = (bf16[512,768]{1,0:T(8,128)(2,1)S(1)}, bf16[512,768]{1,0:T(8,128)(2,1)S(1)}, u32[]{:S(2)}, u32[]{:S(2)}) collective-permute-start(bf16[512,768]{1,0:T(8,128)(2,1)S(1)} %slice.20), channel_id=1, source_target_pairs={{0,1},{1,2},{2,3},{3,0},{4,5},{5,6},{6,7},{7,4},{8,9},{9,10},{10,1... | collective-permute-start | bytes 2359304 | tf_op jit(solution)/shard_map/ppermute | solution.py:473
  41.5 18.1 %collective-permute-start.3 = (bf16[512,768]{1,0:T(8,128)(2,1)S(1)}, bf16[512,768]{1,0:T(8,128)(2,1)S(1)}, u32[]{:S(2)}, u32[]{:S(2)}) collective-permute-start(bf16[512,768]{1,0:T(8,128)(2,1)S(1)} %slice.21), channel_id=1, source_target_pairs={{0,3},{1,0},{2,1},{3,2},{4,7},{5,4},{6,5},{7,6},{8,11},{9,8},{10,9... | collective-permute-start | bytes 2359304 | tf_op jit(solution)/shard_map/ppermute | solution.py:473
  47.9 12.9 %copy-start.7 = (bf16[512,512]{1,0:T(8,128)(2,1)}, bf16[512,512]{1,0:T(8,128)(2,1)S(1)}, u32[]{:S(2)}) copy-start(bf16[512,512]{1,0:T(8,128)(2,1)S(1)} %get-tuple-element.43.rest_8_) | copy-start | bytes 1572868
  48.0 12.9 %copy-start.8 = (bf16[512,512]{1,0:T(8,128)(2,1)}, bf16[512,512]{1,0:T(8,128)(2,1)S(1)}, u32[]{:S(2)}) copy-start(bf16[512,512]{1,0:T(8,128)(2,1)S(1)} %get-tuple-element.44.rest_9_) | copy-start | bytes 1572868
  60.9 11.8 %collective-permute-start.6 = (f32[1,4096]{1,0:T(1,128)S(1)}, f32[1,4096]{1,0:T(1,128)S(1)}, u32[]{:S(2)}, u32[]{:S(2)}) collective-permute-start(f32[1,4096]{1,0:T(1,128)S(1)} %constant_dynamic-update-slice_fusion.4.rest_0_), channel_id=1, source_target_pairs={{0,1},{1,2},{2,3},{3,0},{4,5},{5,6},{6,7},{7,4},{8,9},{9,10},{10,1... | collective-permute-start | bytes 49160 | tf_op jit(solution)/shard_map/ppermute | solution.py:473
  61.0 11.7 %collective-permute-start.5 = (f32[1,4096]{1,0:T(1,128)S(1)}, f32[1,4096]{1,0:T(1,128)S(1)}, u32[]{:S(2)}, u32[]{:S(2)}) collective-permute-start(f32[1,4096]{1,0:T(1,128)S(1)} %constant_dynamic-update-slice_fusion.4.rest_0_), channel_id=1, source_target_pairs={{0,2},{1,3},{2,0},{3,1},{4,6},{5,7},{6,4},{7,5},{8,10},{9,11},{10,... | collective-permute-start | bytes 49160 | tf_op jit(solution)/shard_map/ppermute | solution.py:473
  65.2 7.5 %collective-permute-start.4 = (f32[1,4096]{1,0:T(1,128)S(1)}, f32[1,4096]{1,0:T(1,128)S(1)}, u32[]{:S(2)}, u32[]{:S(2)}) collective-permute-start(f32[1,4096]{1,0:T(1,128)S(1)} %constant_dynamic-update-slice_fusion.4.rest_0_), channel_id=1, source_target_pairs={{0,3},{1,0},{2,1},{3,2},{4,7},{5,4},{6,5},{7,6},{8,11},{9,8},{10,9... | collective-permute-start | bytes 49160 | tf_op jit(solution)/shard_map/ppermute | solution.py:473
  71.0 23.2 %collective-permute-start.13 = (bf16[32,16,896]{2,1,0:T(8,128)(2,1)S(1)}, bf16[32,16,896]{2,1,0:T(8,128)(2,1)}, u32[]{:S(2)}, u32[]{:S(2)}) collective-permute-start(bf16[32,16,896]{2,1,0:T(8,128)(2,1)S(1)} %get-tuple-element.60.rest_17_), channel_id=1, source_target_pairs={{0,3},{1,0},{2,1},{3,2},{4,7},{5,4},{6,5},{7,6},{8,11},{9,8},{10,9... | collective-permute-start | bytes 2752520 | tf_op jit(solution)/shard_map/ppermute | solution.py:473
  72.7 22.0 %collective-permute-start.12 = (bf16[32,16,896]{2,1,0:T(8,128)(2,1)S(1)}, bf16[32,16,896]{2,1,0:T(8,128)(2,1)}, u32[]{:S(2)}, u32[]{:S(2)}) collective-permute-start(bf16[32,16,896]{2,1,0:T(8,128)(2,1)S(1)} %get-tuple-element.62.rest_15_), channel_id=1, source_target_pairs={{0,1},{1,2},{2,3},{3,0},{4,5},{5,6},{6,7},{7,4},{8,9},{9,10},{10,1... | collective-permute-start | bytes 2752520 | tf_op jit(solution)/shard_map/ppermute | solution.py:473
  83.2 2.9 %collective-permute-start.7 = (bf16[256,768]{1,0:T(8,128)(2,1)}, bf16[256,768]{1,0:T(8,128)(2,1)S(1)}, u32[]{:S(2)}, u32[]{:S(2)}) collective-permute-start(bf16[256,768]{1,0:T(8,128)(2,1)} %get-tuple-element.46), channel_id=1, source_target_pairs={{0,4},{4,0},{8,12},{12,8},{16,20},{20,16},{24,28},{28,24},{32,36},... | collective-permute-start | bytes 1179656 | tf_op jit(solution)/shard_map/ppermute | solution.py:487
  87.9 15.5 %all-to-all-start.1 = ((bf16[16,16,768]{2,1,0:T(8,128)(2,1)}), bf16[16,16,768]{2,1,0:T(8,128)(2,1)S(1)}, u32[]{:S(2)}, u32[]{:S(2)}) async-start(bf16[16,16,768]{2,1,0:T(8,128)(2,1)} %bitcast.9), calls=%async_computation.1 | async-start | bytes 786432 | tf_op jit(solution)/shard_map/all_to_all | solution.py:484
  94.7 40.5 %collective-permute-start.14 = (bf16[32,16,896]{2,1,0:T(8,128)(2,1)}, bf16[32,16,896]{2,1,0:T(8,128)(2,1)S(1)}, u32[]{:S(2)}, u32[]{:S(2)}) collective-permute-start(bf16[32,16,896]{2,1,0:T(8,128)(2,1)} %order.1), channel_id=1, source_target_pairs={{0,2},{1,3},{2,0},{3,1},{4,6},{5,7},{6,4},{7,5},{8,10},{9,11},{10,... | collective-permute-start | bytes 2752520 | tf_op jit(solution)/shard_map/ppermute | solution.py:473
  114.8 4.3 %collective-permute-start.8 = (bf16[256,768]{1,0:T(8,128)(2,1)S(1)}, bf16[256,768]{1,0:T(8,128)(2,1)S(1)}, u32[]{:S(2)}, u32[]{:S(2)}) collective-permute-start(bf16[256,768]{1,0:T(8,128)(2,1)S(1)} %bitcast.24), channel_id=1, source_target_pairs={{0,4},{4,0},{8,12},{12,8},{16,20},{20,16},{24,28},{28,24},{32,36},... | collective-permute-start | bytes 1179656 | tf_op jit(solution)/shard_map/ppermute | solution.py:487
  128.6 4.1 %collective-permute-start.11 = (f32[1,4096]{1,0:T(1,128)}, f32[1,4096]{1,0:T(1,128)S(1)}, u32[]{:S(2)}, u32[]{:S(2)}) collective-permute-start(f32[1,4096]{1,0:T(1,128)} %get-tuple-element.47.rest_0_), channel_id=1, source_target_pairs={{0,1},{1,2},{2,3},{3,0},{4,5},{5,6},{6,7},{7,4},{8,9},{9,10},{10,1... | collective-permute-start | bytes 49160 | tf_op jit(solution)/shard_map/ppermute | solution.py:473
  130.2 4.3 %collective-permute-start.10 = (f32[1,4096]{1,0:T(1,128)}, f32[1,4096]{1,0:T(1,128)S(1)}, u32[]{:S(2)}, u32[]{:S(2)}) collective-permute-start(f32[1,4096]{1,0:T(1,128)} %get-tuple-element.47.rest_0_), channel_id=1, source_target_pairs={{0,2},{1,3},{2,0},{3,1},{4,6},{5,7},{6,4},{7,5},{8,10},{9,11},{10,... | collective-permute-start | bytes 49160 | tf_op jit(solution)/shard_map/ppermute | solution.py:473
  132.1 3.1 %collective-permute-start.9 = (f32[1,4096]{1,0:T(1,128)}, f32[1,4096]{1,0:T(1,128)S(1)}, u32[]{:S(2)}, u32[]{:S(2)}) collective-permute-start(f32[1,4096]{1,0:T(1,128)} %get-tuple-element.47.rest_0_), channel_id=1, source_target_pairs={{0,3},{1,0},{2,1},{3,2},{4,7},{5,4},{6,5},{7,6},{8,11},{9,8},{10,9... | collective-permute-start | bytes 49160 | tf_op jit(solution)/shard_map/ppermute | solution.py:473
  145.0 19.8 %all-to-all-start.3 = ((bf16[32,16,768]{2,1,0:T(8,128)(2,1)}), bf16[32,16,768]{2,1,0:T(8,128)(2,1)S(1)}, u32[]{:S(2)}, u32[]{:S(2)}) async-start(bf16[32,16,768]{2,1,0:T(8,128)(2,1)} %bitcast.27), calls=%async_computation.3 | async-start | bytes 1572864 | tf_op jit(solution)/shard_map/all_to_all | solution.py:478
  166.4 12.8 %all-to-all-start.4 = ((bf16[16,16,768]{2,1,0:T(8,128)(2,1)}), bf16[16,16,768]{2,1,0:T(8,128)(2,1)S(1)}, u32[]{:S(2)}, u32[]{:S(2)}) async-start(bf16[16,16,768]{2,1,0:T(8,128)(2,1)} %combine.3), calls=%async_computation.4 | async-start | bytes 786432 | tf_op jit(solution)/shard_map/all_to_all | solution.py:484
  179.9 2.9 %collective-permute-start.15 = (bf16[256,768]{1,0:T(8,128)(2,1)S(1)}, bf16[256,768]{1,0:T(8,128)(2,1)S(1)}, u32[]{:S(2)}, u32[]{:S(2)}) collective-permute-start(bf16[256,768]{1,0:T(8,128)(2,1)S(1)} %hold.1.own_ref), channel_id=1, source_target_pairs={{0,4},{4,0},{8,12},{12,8},{16,20},{20,16},{24,28},{28,24},{32,36},... | collective-permute-start | bytes 1179656 | tf_op jit(solution)/shard_map/ppermute | solution.py:487
  (23 other events, 62.2 us)

commit v7 on v5

--- a/solution.py
+++ b/solution.py
@@ -210,6 +210,23 @@
             pltpu.SemaphoreType.DMA((pieces,)),
         ],
     )(core.reshape(1).astype(jnp.int32), scale, *totals, *members, *sources, *after)
+
+
+def add_kernel(left_ref, right_ref, out_ref):
+    total = left_ref[...].astype(jnp.float32) + right_ref[...].astype(jnp.float32)
+    out_ref[...] = total.astype(jnp.bfloat16)
+
+
+def add(left, right):
+    return call(
+        add_kernel,
+        "add",
+        8,
+        left.size,
+        in_specs=[whole()] * 2,
+        out_specs=whole(),
+        out_shape=jax.ShapeDtypeStruct(left.shape, left.dtype),
+    )(left, right)
 
 
 def combine_kernel(arrived_ref, *rest):
@@ -498,7 +515,7 @@
     totals = [partial_total] + [send(partial_total, -k) for k in range(1, cent_count)]
     parted = [routed[:, k] for k in range(cent_count)]
     own, for_sibling = weighted_sums(members, sources, scale, totals, core, 0, parted[1:])
-    both = (own.astype(jnp.float32) + swap_cores(for_sibling).astype(jnp.float32)).astype(jnp.bfloat16)
+    both = add(own, swap_cores(for_sibling))
     arrived = exchange_plane(both.reshape(planes, share, feature_width))
 
     blocks = [routed, send(parted[1], 1), None, send(parted[3], -1)]

time: 185 us -> 185 us (level)
  other arithmetic: 2.37 us -> 0.49 us
    convert_element_type x1 -> x0, other arithmetic: 1.88 us -> none  [shards(): (own.astype(jnp.float32) + swap_cores(for_sibling).astype(jnp.float32)).a...]
    unnamed x61 -> x63, local copies, waits for them, and re-layouts: 7.9 us -> 8.9 us
  transfers between devices with their start and end apart: 20 -> 20, of which waited for: 12 -> 12; matrix products, arithmetic and copies ran while one was open for 4% -> 3% of each run, Pallas kernels for 26% -> 27%
where the time goes in v7:
time: 185 us; the launch traced here: 184 us
  Pallas kernels  60 us (32%)
  starting transfers between devices  49.7 us (27%)
  waiting for transfers between devices  47.8 us (26%)
  local copies, waits for them, and re-layouts  13.5 us (7%)
  blocking collectives  11.2 us (6%)
    ppermute x13, waiting for transfers between devices, send(): lax.ppermute(value, 'cent', [(z, (z + step) % cent_count) for z in range(...  26.7 us
    ppermute x13, starting transfers between devices, send(): lax.ppermute(value, 'cent', [(z, (z + step) % cent_count) for z in range(...  18.7 us
    pallas_call x2, Pallas kernels, weighted_sums(): call(functools.partial(sum_kernel, pieces, len(totals), len(sources), len...  17.2 us
    pallas_call x2, Pallas kernels, similarity_of(): call(functools.partial(similarity_kernel, cent_count, part * steps), 'sim...  15.4 us
    all_to_all x2, starting transfers between devices, exchange(): return lax.all_to_all(value, 'dp', 0, 0, tiled=True)  13.8 us
    all_to_all x1, blocking collectives, exchange_plane(): lax.all_to_all(value, 'dp', 0, 0, axis_index_groups=same_core, tiled=True)  11.2 us
    all_to_all x2, starting transfers between devices, exchange_plane(): lax.all_to_all(value, 'dp', 0, 0, axis_index_groups=same_core, tiled=True)  10.3 us
    all_to_all x2, waiting for transfers between devices, exchange_plane(): lax.all_to_all(value, 'dp', 0, 0, axis_index_groups=same_core, tiled=True)  9.08 us
  transfers between devices with their start and end apart: 20, of which 12 were waited for; matrix products, arithmetic and copies ran while one was open for 3% of the time, Pallas kernels for 27%

profile of v7, /device:TPU:1, one launch (start us, length us, event | category | flops | bytes accessed | tf_op | source)
XLA Modules:
  0.0 183.7 jit_solution(230980416335128587)
XLA Ops:
  0.6 2.5 %collective-permute-start.1 = (bf16[1024,768]{1,0:T(8,128)(2,1)}, bf16[1024,768]{1,0:T(8,128)(2,1)S(1)}, u32[]{:S(2)}, u32[]{:S(2)}) collective-permute-start(bf16[1024,768]{1,0:T(8,128)(2,1)} %rest_12_.3), channel_id=1, source_target_pairs={{0,1},{1,2},{2,3},{3,0},{4,5},{5,6},{6,7},{7,4},{8,9},{9,10},{10,1... | collective-permute-start | bytes 4718600 | tf_op jit(solution)/shard_map/ppermute | solution.py:473
  3.2 2.2 %collective-permute-start = (bf16[1024,768]{1,0:T(8,128)(2,1)}, bf16[1024,768]{1,0:T(8,128)(2,1)}, u32[]{:S(2)}, u32[]{:S(2)}) collective-permute-start(bf16[1024,768]{1,0:T(8,128)(2,1)} %rest_12_.3), channel_id=1, source_target_pairs={{0,3},{1,0},{2,1},{3,2},{4,7},{5,4},{6,5},{7,6},{8,11},{9,8},{10,9... | collective-permute-start | bytes 4718600 | tf_op jit(solution)/shard_map/ppermute | solution.py:473
  5.4 8.5 %pack.1 = bf16[2048,896]{1,0:T(8,128)(2,1)} custom-call(s32[1]{0:T(128)} %bitcast.1.depth_ref, bf16[1024,768]{1,0:T(8,128)(2,1)} %rest_12_.3, s32[1,1024]{1,0:T(1,128)} %bitcast.28, s32[16,128]{1,0:T(8,128)} %bitcast.27), custom_call_target="tpu_custom_call" | custom-call | flops 3221225472 | bytes 1048576 | tf_op jit(solution)/shard_map/pack/pallas_call | solution.py:331
  13.8 8.2 %all-to-all-start = ((bf16[32,64,896]{2,1,0:T(8,128)(2,1)}), bf16[32,64,896]{2,1,0:T(8,128)(2,1)}, u32[]{:S(2)}, u32[]{:S(2)}) async-start(bf16[32,64,896]{2,1,0:T(8,128)(2,1)} %bitcast.23), calls=%async_computation | async-start | bytes 7340032 | tf_op jit(solution)/shard_map/all_to_all | solution.py:478
  22.7 17.0 %collective-permute-done.1.rest_0_.rest_16_.rest_4_ = bf16[1024,768]{1,0:T(8,128)(2,1)S(1)} collective-permute-done((bf16[1024,768]{1,0:T(8,128)(2,1)}, bf16[1024,768]{1,0:T(8,128)(2,1)S(1)}, u32[]{:S(2)}, u32[]{:S(2)}) %collective-permute-start.1) | collective-permute-done | bytes 1572896 | tf_op jit(solution)/shard_map/ppermute | solution.py:473
  41.5 2.3 %collective-permute-start.3 = (bf16[512,768]{1,0:T(8,128)(2,1)S(1)}, bf16[512,768]{1,0:T(8,128)(2,1)S(1)}, u32[]{:S(2)}, u32[]{:S(2)}) collective-permute-start(bf16[512,768]{1,0:T(8,128)(2,1)S(1)} %slice.21), channel_id=1, source_target_pairs={{0,3},{1,0},{2,1},{3,2},{4,7},{5,4},{6,5},{7,6},{8,11},{9,8},{10,9... | collective-permute-start | bytes 2359304 | tf_op jit(solution)/shard_map/ppermute | solution.py:473
  47.1 3.0 %score_piece.5 = (bf16[512,512]{1,0:T(8,128)(2,1)S(1)}, bf16[512,512]{1,0:T(8,128)(2,1)S(1)}, f32[1,1024]{1,0:T(1,128)S(1)}, f32[1,1024]{1,0:T(1,128)S(1)}) custom-call(bf16[512,768]{1,0:T(8,128)(2,1)S(1)} %pad_maximum_fusion.block_ref, bf16[1024,768]{1,0:T(8,128)(2,1)} %collective-permute-done.rest_0_.rest_13_.rest_1_), custom_call_target="tpu_custom_call" | custom-call | flops 1000000 | bytes 1048576 | tf_op jit(solution)/shard_map/score_piece/pallas_call | solution.py:83
  51.9 7.2 %collective-permute-done.2.rest_0_.rest_14_.rest_2_ = bf16[512,768]{1,0:T(8,128)(2,1)S(1)} collective-permute-done((bf16[512,768]{1,0:T(8,128)(2,1)S(1)}, bf16[512,768]{1,0:T(8,128)(2,1)S(1)}, u32[]{:S(2)}, u32[]{:S(2)}) %collective-permute-start.2) | collective-permute-done | bytes 786464 | tf_op jit(solution)/shard_map/ppermute | solution.py:473
  62.6 4.2 %collective-permute-start.5 = (f32[1,4096]{1,0:T(1,128)S(1)}, f32[1,4096]{1,0:T(1,128)S(1)}, u32[]{:S(2)}, u32[]{:S(2)}) collective-permute-start(f32[1,4096]{1,0:T(1,128)S(1)} %constant_dynamic-update-slice_fusion.4.rest_0_), channel_id=1, source_target_pairs={{0,2},{1,3},{2,0},{3,1},{4,6},{5,7},{6,4},{7,5},{8,10},{9,11},{10,... | collective-permute-start | bytes 49160 | tf_op jit(solution)/shard_map/ppermute | solution.py:473
  68.1 2.9 %slice_bitcast_fusion = (bf16[32,16,896]{2,1,0:T(8,128)(2,1)S(1)}, bf16[32,16,896]{2,1,0:T(8,128)(2,1)}, bf16[32,16,896]{2,1,0:T(8,128)(2,1)S(1)}) fusion(bf16[32,4,16,896]{3,2,1,0:T(8,128)(2,1)} %bitcast.5.rest_0_), kind=kLoop, calls=%fused_computation.4 | loop fusion | bytes 5505024 | tf_op jit(solution)/shard_map/squeeze | solution.py:516
  73.4 8.7 %weighted_sums.2 = (bf16[256,768]{1,0:T(8,128)(2,1)}, bf16[256,768]{1,0:T(8,128)(2,1)}) custom-call(s32[1]{0:T(128)} %bitcast.core_ref, f32[1,4096]{1,0:T(1,128)} %copy-done.21, f32[1,4096]{1,0:T(1,128)} %copy-done.22, f32[1,4096]{1,0:T(1,128)} %copy-done.25, f32[1,4096]{1,0:T(1,128)} %copy-done.24, f32[1,4096]{1,0:T(1,128)} %copy-done.23, ...), custom_call_target="tpu_custom_call" | custom-call | flops 3221225472 | bytes 1048576 | tf_op jit(solution)/shard_map/weighted_sums/pallas_call | solution.py:194
  82.1 2.3 %collective-permute-start.7 = (bf16[256,768]{1,0:T(8,128)(2,1)}, bf16[256,768]{1,0:T(8,128)(2,1)S(1)}, u32[]{:S(2)}, u32[]{:S(2)}) collective-permute-start(bf16[256,768]{1,0:T(8,128)(2,1)} %get-tuple-element.50), channel_id=1, source_target_pairs={{0,4},{4,0},{8,12},{12,8},{16,20},{20,16},{24,28},{28,24},{32,36},... | collective-permute-start | bytes 1179656 | tf_op jit(solution)/shard_map/ppermute | solution.py:487
  87.8 6.7 %all-to-all-start.1 = ((bf16[16,16,768]{2,1,0:T(8,128)(2,1)}), bf16[16,16,768]{2,1,0:T(8,128)(2,1)S(1)}, u32[]{:S(2)}, u32[]{:S(2)}) async-start(bf16[16,16,768]{2,1,0:T(8,128)(2,1)} %bitcast.9), calls=%async_computation.1 | async-start | bytes 786432 | tf_op jit(solution)/shard_map/all_to_all | solution.py:484
  96.2 7.6 %all-to-all-done.1.arrived_ref = bf16[16,16,768]{2,1,0:T(8,128)(2,1)S(1)} async-done(((bf16[16,16,768]{2,1,0:T(8,128)(2,1)}), bf16[16,16,768]{2,1,0:T(8,128)(2,1)S(1)}, u32[]{:S(2)}, u32[]{:S(2)}) %all-to-all-start.1) | async-done | bytes 393248 | tf_op jit(solution)/shard_map/all_to_all | solution.py:484
  104.0 11.2 %all_to_all.25 = bf16[16,16,768]{2,1,0:T(8,128)(2,1)S(1)} all-to-all(bf16[16,16,768]{2,1,0:T(8,128)(2,1)S(1)} %combine.2), channel_id=1, replica_groups={{0,8,16,24,32,40,48,56,64,72,80,88,96,104,112,120},{4,12,20,28,36,44,52..., dimensions={0} | all-to-all | bytes 786432 | tf_op jit(solution)/shard_map/all_to_all | solution.py:484
  115.2 3.0 %collective-permute-start.8 = (bf16[256,768]{1,0:T(8,128)(2,1)S(1)}, bf16[256,768]{1,0:T(8,128)(2,1)S(1)}, u32[]{:S(2)}, u32[]{:S(2)}) collective-permute-start(bf16[256,768]{1,0:T(8,128)(2,1)S(1)} %bitcast.25), channel_id=1, source_target_pairs={{0,4},{4,0},{8,12},{12,8},{16,20},{20,16},{24,28},{28,24},{32,36},... | collective-permute-start | bytes 1179656 | tf_op jit(solution)/shard_map/ppermute | solution.py:487
  120.3 8.8 %score_rows.1 = (bf16[512,512]{1,0:T(8,128)(2,1)}, bf16[512,512]{1,0:T(8,128)(2,1)}, bf16[512,512]{1,0:T(8,128)(2,1)}, bf16[512,512]{1,0:T(8,128)(2,1)}, bf16[51...) custom-call(f32[1,4096]{1,0:T(1,128)} %copy-done.21, ...), custom_call_target="tpu_custom_call" | custom-call | flops 1000000 | bytes 1048576 | tf_op jit(solution)/shard_map/score_rows/pallas_call | solution.py:129
  133.2 1.8 collective-permute-done.10.rest_2_
  136.0 8.6 %weighted_sums.3 = bf16[16,2,16,768]{3,2,1,0:T(8,128)(2,1)} custom-call(s32[1]{0:T(128)} %bitcast.core_ref, f32[1,4096]{1,0:T(1,128)} %copy-done.21, f32[1,4096]{1,0:T(1,128)} %get-tuple-element.51.rest_0_, f32[1,4096]{1,0:T(1,128)} %copy-done.28, f32[1,4096]{1,0:T(1,128)} %copy-done.27, f32[1,4096]{1,0:T(1,128)} %copy-done.26, ...), custom_call_target="tpu_custom_call" | custom-call | flops 3221225472 | bytes 1048576 | tf_op jit(solution)/shard_map/weighted_sums/pallas_call | solution.py:194
  144.6 5.6 %all-to-all-start.3 = ((bf16[32,16,768]{2,1,0:T(8,128)(2,1)}), bf16[32,16,768]{2,1,0:T(8,128)(2,1)S(1)}, u32[]{:S(2)}, u32[]{:S(2)}) async-start(bf16[32,16,768]{2,1,0:T(8,128)(2,1)} %bitcast.24), calls=%async_computation.3 | async-start | bytes 1572864 | tf_op jit(solution)/shard_map/all_to_all | solution.py:478
  150.2 7.7 %similarity.2 = (bf16[1,2048,2048]{2,1,0:T(8,128)(2,1)}, f32[8,128]{1,0:T(8,128)}) custom-call(s32[1]{0:T(128)} %bitcast.1.depth_ref, bf16[32,4,16,896]{3,2,1,0:T(8,128)(2,1)} %bitcast.5.rest_0_, bf16[32,16,896]{2,1,0:T(8,128)(2,1)} %collective-permute-done.12.refs_1_.rest_1_, bf16[32,16,896]{2,1,0:T(8,128)(2,1)} %copy-done.15, ...), custom_call_target="tpu_custom_call" | custom-call | flops 3758096384 | bytes 1048576 | tf_op jit(solution)/shard_map/similarity/pallas_call | solution.py:434
  157.9 6.5 %all-to-all-done.3.arrived_ref = bf16[32,16,768]{2,1,0:T(8,128)(2,1)S(1)} async-done(((bf16[32,16,768]{2,1,0:T(8,128)(2,1)}), bf16[32,16,768]{2,1,0:T(8,128)(2,1)S(1)}, u32[]{:S(2)}, u32[]{:S(2)}) %all-to-all-start.3) | async-done | bytes 786464 | tf_op jit(solution)/shard_map/all_to_all | solution.py:478
  166.0 3.6 %all-to-all-start.4 = ((bf16[16,16,768]{2,1,0:T(8,128)(2,1)}), bf16[16,16,768]{2,1,0:T(8,128)(2,1)S(1)}, u32[]{:S(2)}, u32[]{:S(2)}) async-start(bf16[16,16,768]{2,1,0:T(8,128)(2,1)} %combine.3), calls=%async_computation.4 | async-start | bytes 786432 | tf_op jit(solution)/shard_map/all_to_all | solution.py:484
  169.6 7.7 %similarity.3 = (bf16[1,2048,2048]{2,1,0:T(8,128)(2,1)}, f32[8,128]{1,0:T(8,128)}) custom-call(s32[1]{0:T(128)} %bitcast.1.depth_ref, bf16[32,4,16,896]{3,2,1,0:T(8,128)(2,1)} %bitcast.5.rest_0_, bf16[32,16,896]{2,1,0:T(8,128)(2,1)} %collective-permute-done.12.refs_1_.rest_1_, bf16[32,16,896]{2,1,0:T(8,128)(2,1)} %copy-done.15, ...), custom_call_target="tpu_custom_call", output_to_operand_aliasing={{0}: (5, {})} | custom-call | flops 3758096384 | bytes 1048576 | tf_op jit(solution)/shard_map/similarity/pallas_call | solution.py:434
  (106 shorter events, 34.8 us)
Async XLA Ops:
  0.6 39.1 %collective-permute-start.1 = (bf16[1024,768]{1,0:T(8,128)(2,1)}, bf16[1024,768]{1,0:T(8,128)(2,1)S(1)}, u32[]{:S(2)}, u32[]{:S(2)}) collective-permute-start(bf16[1024,768]{1,0:T(8,128)(2,1)} %rest_12_.3), channel_id=1, source_target_pairs={{0,1},{1,2},{2,3},{3,0},{4,5},{5,6},{6,7},{7,4},{8,9},{9,10},{10,1... | collective-permute-start | bytes 4718600 | tf_op jit(solution)/shard_map/ppermute | solution.py:473
  3.2 36.7 %collective-permute-start = (bf16[1024,768]{1,0:T(8,128)(2,1)}, bf16[1024,768]{1,0:T(8,128)(2,1)}, u32[]{:S(2)}, u32[]{:S(2)}) collective-permute-start(bf16[1024,768]{1,0:T(8,128)(2,1)} %rest_12_.3), channel_id=1, source_target_pairs={{0,3},{1,0},{2,1},{3,2},{4,7},{5,4},{6,5},{7,6},{8,11},{9,8},{10,9... | collective-permute-start | bytes 4718600 | tf_op jit(solution)/shard_map/ppermute | solution.py:473
  13.8 54.2 %all-to-all-start = ((bf16[32,64,896]{2,1,0:T(8,128)(2,1)}), bf16[32,64,896]{2,1,0:T(8,128)(2,1)}, u32[]{:S(2)}, u32[]{:S(2)}) async-start(bf16[32,64,896]{2,1,0:T(8,128)(2,1)} %bitcast.23), calls=%async_computation | async-start | bytes 7340032 | tf_op jit(solution)/shard_map/all_to_all | solution.py:478
  22.7 21.1 %copy-start.1 = (bf16[1024,768]{1,0:T(8,128)(2,1)S(1)}, bf16[1024,768]{1,0:T(8,128)(2,1)}, u32[]{:S(2)}) copy-start(bf16[1024,768]{1,0:T(8,128)(2,1)} %rest_12_.3) | copy-start | bytes 4718596
  39.8 19.3 %collective-permute-start.2 = (bf16[512,768]{1,0:T(8,128)(2,1)S(1)}, bf16[512,768]{1,0:T(8,128)(2,1)S(1)}, u32[]{:S(2)}, u32[]{:S(2)}) collective-permute-start(bf16[512,768]{1,0:T(8,128)(2,1)S(1)} %slice.20), channel_id=1, source_target_pairs={{0,1},{1,2},{2,3},{3,0},{4,5},{5,6},{6,7},{7,4},{8,9},{9,10},{10,1... | collective-permute-start | bytes 2359304 | tf_op jit(solution)/shard_map/ppermute | solution.py:473
  41.5 18.1 %collective-permute-start.3 = (bf16[512,768]{1,0:T(8,128)(2,1)S(1)}, bf16[512,768]{1,0:T(8,128)(2,1)S(1)}, u32[]{:S(2)}, u32[]{:S(2)}) collective-permute-start(bf16[512,768]{1,0:T(8,128)(2,1)S(1)} %slice.21), channel_id=1, source_target_pairs={{0,3},{1,0},{2,1},{3,2},{4,7},{5,4},{6,5},{7,6},{8,11},{9,8},{10,9... | collective-permute-start | bytes 2359304 | tf_op jit(solution)/shard_map/ppermute | solution.py:473
  47.1 13.7 %copy-start.6 = (bf16[512,512]{1,0:T(8,128)(2,1)}, bf16[512,512]{1,0:T(8,128)(2,1)S(1)}, u32[]{:S(2)}) copy-start(bf16[512,512]{1,0:T(8,128)(2,1)S(1)} %get-tuple-element.47.rest_10_) | copy-start | bytes 1572868
  47.1 13.7 %copy-start.7 = (bf16[512,512]{1,0:T(8,128)(2,1)}, bf16[512,512]{1,0:T(8,128)(2,1)S(1)}, u32[]{:S(2)}) copy-start(bf16[512,512]{1,0:T(8,128)(2,1)S(1)} %get-tuple-element.48.rest_11_) | copy-start | bytes 1572868
  62.5 8.4 %copy-start.22 = (f32[1,4096]{1,0:T(1,128)}, f32[1,4096]{1,0:T(1,128)S(1)}, u32[]{:S(2)}) copy-start(f32[1,4096]{1,0:T(1,128)S(1)} %constant_dynamic-update-slice_fusion.4.rest_0_) | copy-start | bytes 49156
  62.5 10.2 %collective-permute-start.6 = (f32[1,4096]{1,0:T(1,128)S(1)}, f32[1,4096]{1,0:T(1,128)S(1)}, u32[]{:S(2)}, u32[]{:S(2)}) collective-permute-start(f32[1,4096]{1,0:T(1,128)S(1)} %constant_dynamic-update-slice_fusion.4.rest_0_), channel_id=1, source_target_pairs={{0,1},{1,2},{2,3},{3,0},{4,5},{5,6},{6,7},{7,4},{8,9},{9,10},{10,1... | collective-permute-start | bytes 49160 | tf_op jit(solution)/shard_map/ppermute | solution.py:473
  62.6 10.1 %collective-permute-start.5 = (f32[1,4096]{1,0:T(1,128)S(1)}, f32[1,4096]{1,0:T(1,128)S(1)}, u32[]{:S(2)}, u32[]{:S(2)}) collective-permute-start(f32[1,4096]{1,0:T(1,128)S(1)} %constant_dynamic-update-slice_fusion.4.rest_0_), channel_id=1, source_target_pairs={{0,2},{1,3},{2,0},{3,1},{4,6},{5,7},{6,4},{7,5},{8,10},{9,11},{10,... | collective-permute-start | bytes 49160 | tf_op jit(solution)/shard_map/ppermute | solution.py:473
  66.8 5.9 %collective-permute-start.4 = (f32[1,4096]{1,0:T(1,128)S(1)}, f32[1,4096]{1,0:T(1,128)S(1)}, u32[]{:S(2)}, u32[]{:S(2)}) collective-permute-start(f32[1,4096]{1,0:T(1,128)S(1)} %constant_dynamic-update-slice_fusion.4.rest_0_), channel_id=1, source_target_pairs={{0,3},{1,0},{2,1},{3,2},{4,7},{5,4},{6,5},{7,6},{8,11},{9,8},{10,9... | collective-permute-start | bytes 49160 | tf_op jit(solution)/shard_map/ppermute | solution.py:473
  71.0 23.6 %collective-permute-start.13 = (bf16[32,16,896]{2,1,0:T(8,128)(2,1)S(1)}, bf16[32,16,896]{2,1,0:T(8,128)(2,1)}, u32[]{:S(2)}, u32[]{:S(2)}) collective-permute-start(bf16[32,16,896]{2,1,0:T(8,128)(2,1)S(1)} %get-tuple-element.64.rest_19_), channel_id=1, source_target_pairs={{0,3},{1,0},{2,1},{3,2},{4,7},{5,4},{6,5},{7,6},{8,11},{9,8},{10,9... | collective-permute-start | bytes 2752520 | tf_op jit(solution)/shard_map/ppermute | solution.py:473
  72.7 22.0 %collective-permute-start.12 = (bf16[32,16,896]{2,1,0:T(8,128)(2,1)S(1)}, bf16[32,16,896]{2,1,0:T(8,128)(2,1)}, u32[]{:S(2)}, u32[]{:S(2)}) collective-permute-start(bf16[32,16,896]{2,1,0:T(8,128)(2,1)S(1)} %get-tuple-element.66.rest_17_), channel_id=1, source_target_pairs={{0,1},{1,2},{2,3},{3,0},{4,5},{5,6},{6,7},{7,4},{8,9},{9,10},{10,1... | collective-permute-start | bytes 2752520 | tf_op jit(solution)/shard_map/ppermute | solution.py:473
  82.1 3.9 %collective-permute-start.7 = (bf16[256,768]{1,0:T(8,128)(2,1)}, bf16[256,768]{1,0:T(8,128)(2,1)S(1)}, u32[]{:S(2)}, u32[]{:S(2)}) collective-permute-start(bf16[256,768]{1,0:T(8,128)(2,1)} %get-tuple-element.50), channel_id=1, source_target_pairs={{0,4},{4,0},{8,12},{12,8},{16,20},{20,16},{24,28},{28,24},{32,36},... | collective-permute-start | bytes 1179656 | tf_op jit(solution)/shard_map/ppermute | solution.py:487
  87.8 16.0 %all-to-all-start.1 = ((bf16[16,16,768]{2,1,0:T(8,128)(2,1)}), bf16[16,16,768]{2,1,0:T(8,128)(2,1)S(1)}, u32[]{:S(2)}, u32[]{:S(2)}) async-start(bf16[16,16,768]{2,1,0:T(8,128)(2,1)} %bitcast.9), calls=%async_computation.1 | async-start | bytes 786432 | tf_op jit(solution)/shard_map/all_to_all | solution.py:484
  94.7 40.3 %collective-permute-start.14 = (bf16[32,16,896]{2,1,0:T(8,128)(2,1)}, bf16[32,16,896]{2,1,0:T(8,128)(2,1)S(1)}, u32[]{:S(2)}, u32[]{:S(2)}) collective-permute-start(bf16[32,16,896]{2,1,0:T(8,128)(2,1)} %order.1), channel_id=1, source_target_pairs={{0,2},{1,3},{2,0},{3,1},{4,6},{5,7},{6,4},{7,5},{8,10},{9,11},{10,... | collective-permute-start | bytes 2752520 | tf_op jit(solution)/shard_map/ppermute | solution.py:473
  115.2 4.3 %collective-permute-start.8 = (bf16[256,768]{1,0:T(8,128)(2,1)S(1)}, bf16[256,768]{1,0:T(8,128)(2,1)S(1)}, u32[]{:S(2)}, u32[]{:S(2)}) collective-permute-start(bf16[256,768]{1,0:T(8,128)(2,1)S(1)} %bitcast.25), channel_id=1, source_target_pairs={{0,4},{4,0},{8,12},{12,8},{16,20},{20,16},{24,28},{28,24},{32,36},... | collective-permute-start | bytes 1179656 | tf_op jit(solution)/shard_map/ppermute | solution.py:487
  129.1 4.1 %collective-permute-start.11 = (f32[1,4096]{1,0:T(1,128)}, f32[1,4096]{1,0:T(1,128)S(1)}, u32[]{:S(2)}, u32[]{:S(2)}) collective-permute-start(f32[1,4096]{1,0:T(1,128)} %get-tuple-element.51.rest_0_), channel_id=1, source_target_pairs={{0,1},{1,2},{2,3},{3,0},{4,5},{5,6},{6,7},{7,4},{8,9},{9,10},{10,1... | collective-permute-start | bytes 49160 | tf_op jit(solution)/shard_map/ppermute | solution.py:473
  130.7 4.3 %collective-permute-start.10 = (f32[1,4096]{1,0:T(1,128)}, f32[1,4096]{1,0:T(1,128)S(1)}, u32[]{:S(2)}, u32[]{:S(2)}) collective-permute-start(f32[1,4096]{1,0:T(1,128)} %get-tuple-element.51.rest_0_), channel_id=1, source_target_pairs={{0,2},{1,3},{2,0},{3,1},{4,6},{5,7},{6,4},{7,5},{8,10},{9,11},{10,... | collective-permute-start | bytes 49160 | tf_op jit(solution)/shard_map/ppermute | solution.py:473
  131.6 3.4 %collective-permute-start.9 = (f32[1,4096]{1,0:T(1,128)}, f32[1,4096]{1,0:T(1,128)S(1)}, u32[]{:S(2)}, u32[]{:S(2)}) collective-permute-start(f32[1,4096]{1,0:T(1,128)} %get-tuple-element.51.rest_0_), channel_id=1, source_target_pairs={{0,3},{1,0},{2,1},{3,2},{4,7},{5,4},{6,5},{7,6},{8,11},{9,8},{10,9... | collective-permute-start | bytes 49160 | tf_op jit(solution)/shard_map/ppermute | solution.py:473
  144.6 19.8 %all-to-all-start.3 = ((bf16[32,16,768]{2,1,0:T(8,128)(2,1)}), bf16[32,16,768]{2,1,0:T(8,128)(2,1)S(1)}, u32[]{:S(2)}, u32[]{:S(2)}) async-start(bf16[32,16,768]{2,1,0:T(8,128)(2,1)} %bitcast.24), calls=%async_computation.3 | async-start | bytes 1572864 | tf_op jit(solution)/shard_map/all_to_all | solution.py:478
  166.0 12.8 %all-to-all-start.4 = ((bf16[16,16,768]{2,1,0:T(8,128)(2,1)}), bf16[16,16,768]{2,1,0:T(8,128)(2,1)S(1)}, u32[]{:S(2)}, u32[]{:S(2)}) async-start(bf16[16,16,768]{2,1,0:T(8,128)(2,1)} %combine.3), calls=%async_computation.4 | async-start | bytes 786432 | tf_op jit(solution)/shard_map/all_to_all | solution.py:484
  179.5 2.9 %collective-permute-start.15 = (bf16[256,768]{1,0:T(8,128)(2,1)S(1)}, bf16[256,768]{1,0:T(8,128)(2,1)S(1)}, u32[]{:S(2)}, u32[]{:S(2)}) collective-permute-start(bf16[256,768]{1,0:T(8,128)(2,1)S(1)} %hold.1.own_ref), channel_id=1, source_target_pairs={{0,4},{4,0},{8,12},{12,8},{16,20},{20,16},{24,28},{28,24},{32,36},... | collective-permute-start | bytes 1179656 | tf_op jit(solution)/shard_map/ppermute | solution.py:487
  (25 other events, 46.9 us)
